TPU v7x, 32 devices: a whole 2x2x4 slice. The times are simulated.
32 devices in a mesh: parts: 2 (over x), tile: 16 (over z, y, core).
Axes of the slice: x: 2, y: 2, z: 4, core: 2. Of those that a mesh axis runs over, the one named last changes fastest.
Arguments:
- sections: bfloat16 [4096, 2048], P(('parts', 'tile')), parts along dimension 0, may hold values from -10 to 10
- valid_mask: int32 [32, 16], P(('parts', 'tile')), parts along dimension 0, may hold values 0 or 1
- coarse_offsets: int32 [8, 2], P('parts'), parts along dimension 0, may hold values from -3 to 3
Outputs:
- aligned: bfloat16 [4096, 2048], P(('parts', 'tile')), parts along dimension 0
- node_shift: float32 [2, 32, 16], P(None, ('parts', 'tile')), parts along dimension 1
There are 2 independent parts, one for each index of `parts`. A program takes and returns all parts, laid end to end along the dimension named above; each array names one. Nothing has to cross between parts.
All inputs are finite; a program needn't handle non-finite values. No bound on the sum of `valid_mask` on one device may be relied on, other than what follows from the above.
Results may differ from a plain program's by a relative error of at most 0.002.
Values may be sent and summed in bfloat16 or wider, within the bound.
No kernel may reach another device: no remote copies, remote signals or barrier semaphores. Data moves between devices by JAX's collectives and lax.ppermute only.
A program may use at most 64 MiB of HBM per device.

v0:
```python
import functools
import math

import jax
import jax.numpy as jnp
from jax import lax
from jax.experimental import pallas as pl
from jax.experimental.pallas import tpu as pltpu
from jax.sharding import PartitionSpec as P

SECTIONS = 4
PATCH = 128
HALF = 4
SWEEPS = 3
LANES = 128
WIDTH = 2 * HALF + 1
MASK_LANE = 64
GROUP = 2

sharpness = 12.0
anchor_weight = 2.0
f32 = jnp.float32
bf16 = jnp.bfloat16


def iota(shape, axis):
    return lax.broadcasted_iota(jnp.int32, shape, axis)


def split(value):
    high = value.astype(bf16)
    return high, (value - high.astype(f32)).astype(bf16)


def dot(lhs, rhs):
    return jnp.dot(lhs, rhs, preferred_element_type=f32)


def dot_t(lhs, rhs):
    return lax.dot_general(lhs, rhs, (((1,), (1,)), ((), ())), preferred_element_type=f32)


def sine(x):
    y = x * x
    acc = jnp.full_like(x, 1.0 / math.factorial(13))
    for order in (11, 9, 7, 5, 3, 1):
        acc = (-1.0 if order % 4 == 3 else 1.0) / math.factorial(order) + y * acc
    return x * acc


def cosine(x):
    y = x * x
    acc = jnp.full_like(x, 1.0 / math.factorial(12))
    for order in (10, 8, 6, 4, 2, 0):
        acc = (-1.0 if order % 4 == 2 else 1.0) / math.factorial(order) + y * acc
    return acc


def total(value):
    return jnp.sum(jnp.sum(value, axis=0, keepdims=True), axis=1, keepdims=True)


def tile_sum(value):
    parts = [value[r : r + 8] for r in range(0, value.shape[0], 8)]
    while len(parts) > 1:
        parts = [x + y for x, y in zip(parts[::2], parts[1::2])]
    return parts[0]


def sign_tile(shape):
    return (1 - 2 * ((iota(shape, 0) + iota(shape, 1)) % 2)).astype(f32)


def section_grid(gathered, step, rows):
    count = gathered.shape[0]
    padded = rows + 8 - rows % 8
    out = None
    for group in (step - 1, step):
        start = (group * rows + rows // 2) % count
        part = jnp.concatenate([gathered[start:], gathered[:start]], axis=0) if start else gathered
        part = part[:padded]
        out = part if out is None else out + part
    return out


def relax(grid, rows, nodes):
    shape = grid.shape
    row, lane = iota(shape, 0), iota(shape, 1)
    col = lane % nodes
    valid = (row < rows) & (lane < 2 * nodes)
    mask = pltpu.roll(grid, LANES - MASK_LANE, 1)
    one = lambda cond: jnp.where(cond, 1.0, 0.0)
    count = one(row > 0) + one(row < rows - 1) + one(col > 0) + one(col < nodes - 1)
    weight = anchor_weight * mask
    inverse = 1.0 / jnp.where(valid, weight + count, 1.0)
    pulled = weight * grid
    shift = jnp.where(valid, grid * mask, 0.0)
    for _ in range(SWEEPS):
        near = pltpu.roll(shift, 1, 0) + pltpu.roll(shift, shape[0] - 1, 0)
        near += jnp.where(col > 0, pltpu.roll(shift, 1, 1), 0.0)
        near += jnp.where(col < nodes - 1, pltpu.roll(shift, LANES - 1, 1), 0.0)
        shift = jnp.where(valid, (pulled + near) * inverse, 0.0)
    return shift


def own_row(shift, index):
    return jnp.sum(jnp.where(iota(shift.shape, 0) == index, shift, 0.0), axis=0, keepdims=True)


def kernels_of(row_shift, first, cols, nodes):
    shape = (2 * cols, LANES)
    sub, lane = iota(shape, 0), iota(shape, 1)
    is_row = sub < cols
    target = first + jnp.where(is_row, sub, sub - cols + nodes)
    shift = jnp.sum(jnp.where(lane == target, row_shift, 0.0), axis=1, keepdims=True)
    shift = jnp.broadcast_to(shift, shape)
    whole = jnp.floor(shift + 0.5)
    part = shift - whole
    steps = jnp.where(is_row, -lane, lane).astype(f32) + whole
    steps = steps - LANES * jnp.floor((steps + LANES // 2) * (1.0 / LANES))
    sign = lambda n: 1.0 - 2.0 * (n - 2.0 * jnp.floor(n * 0.5))
    swing = sine(part * math.pi)
    angle = (steps + part) * (math.pi / LANES)
    centre = (steps == 0.0) & (jnp.abs(part) < 1e-20)
    below = jnp.where(centre, 1.0, sine(angle))
    base = swing * sign(steps) * (1.0 / LANES) * cosine(angle) / below
    return jnp.where(centre, 1.0, base), swing * sign(whole)


def circulant(row):
    return pltpu.roll(jnp.broadcast_to(row, (PATCH, LANES)), 0, 1, stride=1, stride_axis=0)


def warp(patch, row_base, col_base, row_swing, col_swing, nyquist):
    row_high, row_low = split(circulant(row_base))
    col_high, col_low = split(circulant(col_base))
    inner = dot(
        jnp.concatenate([patch, patch], axis=1), jnp.concatenate([col_high, col_low], axis=0)
    )
    in_high, in_low = split(inner)
    out = dot(
        jnp.concatenate([row_high, row_low], axis=1), jnp.concatenate([in_high, in_high], axis=0)
    ) + dot(row_high, in_low)
    factor = row_swing * col_swing * nyquist * (1.0 / (PATCH * PATCH))
    return out - factor * sign_tile((PATCH, LANES))


def correlate(own, prev, base, column_offset):
    half, edge, third = PATCH // 2, 16, 3
    own32, prev32 = own.astype(f32), prev.astype(f32)
    left = []
    for i in range(third):
        amount = (PATCH + HALF - i - column_offset) % PATCH
        turned = pltpu.roll(own32, amount, 1).astype(bf16)
        left.append(jnp.concatenate([turned[:half], turned[half:]], axis=1))
    right = []
    for j in range(third):
        turned = (pltpu.roll(prev32, third * j, 1) if j else prev32).astype(bf16)
        low = jnp.concatenate([turned[PATCH - edge :], turned[: PATCH - edge]], axis=0)
        high = jnp.concatenate([turned[half - edge :], turned[: half - edge]], axis=0)
        right.append(jnp.concatenate([low, high], axis=1))
    product = dot_t(jnp.concatenate(left, axis=0), jnp.concatenate(right, axis=0))
    lane = iota((8, LANES), 1)
    sub = iota((16, LANES), 0)
    out = jnp.zeros((16, LANES), f32)
    for j in range(third):
        for i in range(third):
            block = product[i * half : (i + 1) * half, j * LANES : (j + 1) * LANES]
            band = None
            for k in range(4):
                later = (lane >= 8 * k + 32) & (lane < 8 * k + 64)
                kept = jnp.where(later, block[8 * k + 32 : 8 * k + 40], block[8 * k : 8 * k + 8])
                kept = pltpu.roll(kept, LANES - 8 * k, 1) if k else kept
                band = kept if band is None else band + kept
            band = band - base
            for step in (4, 2, 1):
                band = band + pltpu.roll(pltpu.roll(band, 8 - step, 0), LANES - step, 1)
            line = band[0:1]
            line = line + pltpu.roll(line, LANES - 32, 1)
            out = jnp.where(sub == i + third * j, line, out)
    return out


def stats(tile):
    return total(tile) * (1.0 / (PATCH * PATCH))


def chain_kernel(
    step, rows, nodes, offsets_ref, own_ref, below_ref, above_ref, mask_ref, *refs
):
    gathered_ref = refs[0] if step > 1 else None
    out_ref, score_ref, base_ref, swing_ref = refs[-4:]
    cols = nodes // 2
    count = lax.axis_size("tile")
    rotated = (lax.axis_index("tile") + count - rows // 2) % count
    group, row_index = rotated // rows, rotated % rows
    is_upper = group == step
    first = jnp.where(is_upper, cols, 0)
    if step > 1:
        shift = relax(section_grid(gathered_ref[...], step - 1, rows), rows, nodes)
        base, swing = kernels_of(own_row(shift, row_index), first, cols, nodes)
        base_ref[...] = base
        swing_ref[...] = swing
    row_offset, col_offset = offsets_ref[step, 0], offsets_ref[step, 1]
    area = float(PATCH * PATCH)

    def one(index):
        here = pl.ds(pl.multiple_of(index * PATCH, PATCH), PATCH)
        beyond = pl.ds(pl.multiple_of((index + cols) * PATCH, PATCH), PATCH)
        own = jnp.where(is_upper, own_ref[:, beyond], above_ref[:, here])
        prev = jnp.where(is_upper, below_ref[:, here], own_ref[:, here])
        own32, prev32 = own.astype(f32), prev.astype(f32)
        own_mean = stats(tile_sum(own32))
        own_var = stats(tile_sum((own32 - own_mean) * (own32 - own_mean)))
        prev_tile = tile_sum(prev32)
        prev_mean = stats(prev_tile)
        if step > 1:
            nyquist = total(prev_tile * sign_tile((8, LANES)))
            prev = warp(
                prev,
                base_ref[pl.ds(index, 1), :],
                base_ref[pl.ds(index + cols, 1), :],
                swing_ref[pl.ds(index, 1), :],
                swing_ref[pl.ds(index + cols, 1), :],
                nyquist,
            ).astype(bf16)
            prev32 = prev.astype(f32)
        centre = prev32 - prev_mean
        drift = stats(tile_sum(centre))
        prev_var = stats(tile_sum(centre * centre)) - drift * drift
        spread = jnp.sqrt((own_var + 1e-5) * (prev_var + 1e-5))
        lags = correlate(own, prev, (own_mean * (prev_mean + drift)) * (8.0 * LANES), col_offset)
        score_ref[pl.ds(index, 1)] = (lags * (sharpness / area / spread))[None]

    def body(turn, carry):
        for k in range(GROUP):
            one(turn * GROUP + k)
        return carry

    lax.fori_loop(0, cols // GROUP, body, 0)
    shape = (cols, 16, LANES)
    line, lane = iota(shape, 1), iota(shape, 2)
    row_step = 16 - lane - row_offset
    inside = (line < WIDTH) & (row_step >= -HALF) & (row_step <= HALF)
    weights = jnp.where(inside, jnp.exp(jnp.where(inside, score_ref[...], 0.0)), 0.0)
    reduce = lambda value: jnp.sum(jnp.sum(value, axis=1), axis=1, keepdims=True)
    inverse = 1.0 / reduce(weights)
    flow_row = reduce(weights * (row_step + row_offset).astype(f32)) * inverse
    flow_col = reduce(weights * (line - HALF + col_offset).astype(f32)) * inverse
    shape = (cols, LANES)
    node, lane = iota(shape, 0) + first, iota(shape, 1)
    sent = jnp.where(lane == node, flow_row, jnp.where(lane == node + nodes, flow_col, 0.0))
    sent = jnp.sum(sent, axis=0, keepdims=True)
    masks = mask_ref[...].astype(f32)
    masks = jnp.concatenate(
        [jnp.zeros((1, MASK_LANE), f32), masks, masks, jnp.zeros((1, LANES - MASK_LANE - 2 * nodes), f32)],
        axis=1,
    )
    sent = sent + jnp.where(is_upper, masks, 0.0)
    out_ref[...] = jnp.broadcast_to(sent, out_ref.shape)


def home_kernel(rows, nodes, own_ref, *refs):
    gathered_refs = refs[: SECTIONS - 1]
    out_ref, shift_ref, base_ref, swing_ref = refs[SECTIONS - 1 :]
    count = lax.axis_size("tile")
    rotated = (lax.axis_index("tile") + count - rows // 2) % count
    group, row_index = rotated // rows, rotated % rows
    grid = None
    for step in range(1, SECTIONS):
        part = section_grid(gathered_refs[step - 1][...], step, rows)
        grid = part if grid is None else jnp.where(group == step, part, grid)
    row_shift = own_row(relax(grid, rows, nodes), row_index)
    row_shift = jnp.where(group == 0, 0.0, row_shift)
    shift_ref[0, :, :] = row_shift[:, :nodes]
    shift_ref[1, :, :] = pltpu.roll(row_shift, LANES - nodes, 1)[:, :nodes]
    base, swing = kernels_of(row_shift, 0, nodes, nodes)
    base_ref[...] = base
    swing_ref[...] = swing

    def one(index):
        here = pl.ds(pl.multiple_of(index * PATCH, PATCH), PATCH)
        own = own_ref[:, here]
        nyquist = total(tile_sum(own.astype(f32)) * sign_tile((8, LANES)))
        out_ref[:, here] = warp(
            own,
            base_ref[pl.ds(index, 1), :],
            base_ref[pl.ds(index + nodes, 1), :],
            swing_ref[pl.ds(index, 1), :],
            swing_ref[pl.ds(index + nodes, 1), :],
            nyquist,
        ).astype(bf16)

    def body(turn, carry):
        for k in range(GROUP):
            one(turn * GROUP + k)
        return carry

    lax.fori_loop(0, nodes // GROUP, body, 0)


def shards(sections, valid_mask, coarse_offsets):
    count = lax.axis_size("tile")
    rows = count // SECTIONS
    nodes = valid_mask.shape[1]
    cols = nodes // 2
    width = cols * PATCH
    place = lambda group, row: (group * rows + row + rows // 2) % count

    def moved(value, pairs):
        return lax.ppermute(
            value, "tile", [(place(s, i), place(d, i)) for s, d in pairs for i in range(rows)]
        )

    left, right = sections[:, :width], sections[:, width:]
    below = moved(right, [(s, s + 1) for s in range(SECTIONS - 1)])
    above = moved(left, [(s + 1, s) for s in range(SECTIONS - 1)])

    vmem = pl.BlockSpec(memory_space=pltpu.VMEM)
    smem = pl.BlockSpec(memory_space=pltpu.SMEM)
    params = pltpu.CompilerParams(vmem_limit_bytes=16 * 2**20)
    gathered = []
    for step in range(1, SECTIONS):
        extra = gathered[-1:]
        sent = pl.pallas_call(
            functools.partial(chain_kernel, step, rows, nodes),
            out_shape=jax.ShapeDtypeStruct((count, LANES), f32),
            in_specs=[smem] + [vmem] * (4 + len(extra)),
            out_specs=vmem,
            scratch_shapes=[
                pltpu.VMEM((cols, 16, LANES), f32),
                pltpu.VMEM((2 * cols, LANES), f32),
                pltpu.VMEM((2 * cols, LANES), f32),
            ],
            compiler_params=params,
            name=f"chain{step}",
        )(coarse_offsets, sections, below, above, valid_mask, *extra)
        gathered.append(lax.all_to_all(sent, "tile", 0, 0, tiled=True))
    return pl.pallas_call(
        functools.partial(home_kernel, rows, nodes),
        out_shape=(
            jax.ShapeDtypeStruct(sections.shape, bf16),
            jax.ShapeDtypeStruct((2, 1, nodes), f32),
        ),
        in_specs=[vmem] * SECTIONS,
        out_specs=(vmem, vmem),
        scratch_shapes=[pltpu.VMEM((2 * nodes, LANES), f32)] * 2,
        compiler_params=params,
        name="home",
    )(sections, *gathered)


def solution(mesh):
    placed = (P(("parts", "tile"), None), P(("parts", "tile"), None), P("parts", None))
    return jax.shard_map(
        shards,
        mesh=mesh,
        in_specs=placed,
        out_specs=(P(("parts", "tile"), None), P(None, ("parts", "tile"), None)),
        check_vma=False,
    )
```

profile of v0, /device:TPU:0, one launch (start us, length us, event | category | flops | bytes accessed | tf_op | source)
XLA Modules:
  0.0 71.2 jit_solution(3035000075060120451)
XLA Ops:
  0.6 0.0 copy-start
  0.6 1.1 %fusion = (bf16[128,1024]{1,0:T(8,128)(2,1)S(1)}, bf16[128,1024]{1,0:T(8,128)(2,1)S(1)}) fusion(bf16[128,2048]{1,0:T(8,128)(2,1)} %own_ref.7), kind=kLoop, calls=%fused_computation | loop fusion | bytes 1048576 | tf_op jit(solution)/shard_map/slice | solution.py:315
  1.8 0.0 copy-start.2
  1.8 1.3 %collective-permute-start = (bf16[128,1024]{1,0:T(8,128)(2,1)S(1)}, bf16[128,1024]{1,0:T(8,128)(2,1)S(1)}, u32[]{:S(2)}, u32[]{:S(2)}) collective-permute-start(bf16[128,1024]{1,0:T(8,128)(2,1)S(1)} %get-tuple-element.3), channel_id=1, source_target_pairs={{2,6},{3,7},{4,8},{5,9},{6,10},{7,11},{8,12},{9,13},{10,14},{11,15... | collective-permute-start | bytes 786440 | tf_op jit(solution)/shard_map/ppermute | solution.py:311
  3.1 0.0 copy-start.1
  3.1 7.6 %collective-permute-start.1 = (bf16[128,1024]{1,0:T(8,128)(2,1)S(1)}, bf16[128,1024]{1,0:T(8,128)(2,1)S(1)}, u32[]{:S(2)}, u32[]{:S(2)}) collective-permute-start(bf16[128,1024]{1,0:T(8,128)(2,1)S(1)} %get-tuple-element.2), channel_id=1, source_target_pairs={{6,2},{7,3},{8,4},{9,5},{10,6},{11,7},{12,8},{13,9},{14,10},{15,11... | collective-permute-start | bytes 786440 | tf_op jit(solution)/shard_map/ppermute | solution.py:311
  10.7 0.0 copy-done.2
  10.7 0.1 copy.8.offsets_ref
  10.8 5.1 %collective-permute-done.below_ref = bf16[128,1024]{1,0:T(8,128)(2,1)S(1)} collective-permute-done((bf16[128,1024]{1,0:T(8,128)(2,1)S(1)}, bf16[128,1024]{1,0:T(8,128)(2,1)S(1)}, u32[]{:S(2)}, u32[]{:S(2)}) %collective-permute-start) | collective-permute-done | bytes 262176 | tf_op jit(solution)/shard_map/ppermute | solution.py:311
  15.9 0.4 collective-permute-done.1.above_ref
  16.3 0.0 copy-done
  16.3 0.0 copy-done.1
  16.3 3.8 %chain1.1 = f32[16,128]{1,0:T(8,128)S(1)} custom-call(s32[4,2]{1,0:T(4,128)S(1)} %copy.8.offsets_ref, bf16[128,2048]{1,0:T(8,128)(2,1)S(1)} %copy-done, bf16[128,1024]{1,0:T(8,128)(2,1)S(1)} %collective-permute-done.below_ref, bf16[128,1024]{1,0:T(8,128)(2,1)S(1)} %collective-permute-done.1.above_ref, s32[1,16]{1,0:T(1,128)S(1)} %copy-done.1), custom_call_target="tpu_custom_call" | custom-call | tf_op jit(solution)/shard_map/chain1/pallas_call | solution.py:325
  20.0 13.7 %all_to_all.33 = f32[16,1,128]{2,1,0:T(1,128)S(1)} all-to-all(f32[16,1,128]{2,1,0:T(1,128)S(1)} %bitcast.18), channel_id=1, replica_groups=mesh['parts'=2,'tile'=16] {'tile'}, dimensions={0} | all-to-all | bytes 16384 | tf_op jit(solution)/shard_map/all_to_all | solution.py:338
  33.8 7.3 %chain2.1 = f32[16,128]{1,0:T(8,128)S(1)} custom-call(s32[4,2]{1,0:T(4,128)S(1)} %copy.8.offsets_ref, bf16[128,2048]{1,0:T(8,128)(2,1)S(1)} %copy-done, bf16[128,1024]{1,0:T(8,128)(2,1)S(1)} %collective-permute-done.below_ref, bf16[128,1024]{1,0:T(8,128)(2,1)S(1)} %collective-permute-done.1.above_ref, s32[1,16]{1,0:T(1,128)S(1)} %copy-done.1, ...), custom_call_target="tpu_custom_call" | custom-call | tf_op jit(solution)/shard_map/chain2/pallas_call | solution.py:325
  41.1 9.0 %all_to_all.34 = f32[16,1,128]{2,1,0:T(1,128)S(1)} all-to-all(f32[16,1,128]{2,1,0:T(1,128)S(1)} %bitcast.19), channel_id=1, replica_groups=mesh['parts'=2,'tile'=16] {'tile'}, dimensions={0} | all-to-all | bytes 16384 | tf_op jit(solution)/shard_map/all_to_all | solution.py:338
  50.1 7.3 %chain3.1 = f32[16,128]{1,0:T(8,128)S(1)} custom-call(s32[4,2]{1,0:T(4,128)S(1)} %copy.8.offsets_ref, bf16[128,2048]{1,0:T(8,128)(2,1)S(1)} %copy-done, bf16[128,1024]{1,0:T(8,128)(2,1)S(1)} %collective-permute-done.below_ref, bf16[128,1024]{1,0:T(8,128)(2,1)S(1)} %collective-permute-done.1.above_ref, s32[1,16]{1,0:T(1,128)S(1)} %copy-done.1, ...), custom_call_target="tpu_custom_call" | custom-call | tf_op jit(solution)/shard_map/chain3/pallas_call | solution.py:325
  57.4 9.0 %all_to_all.35 = f32[16,1,128]{2,1,0:T(1,128)S(1)} all-to-all(f32[16,1,128]{2,1,0:T(1,128)S(1)} %bitcast.17), channel_id=1, replica_groups=mesh['parts'=2,'tile'=16] {'tile'}, dimensions={0} | all-to-all | bytes 16384 | tf_op jit(solution)/shard_map/all_to_all | solution.py:338
  66.4 4.8 %home.1 = (bf16[128,2048]{1,0:T(8,128)(2,1)}, f32[2,1,16]{2,1,0:T(1,128)}) custom-call(bf16[128,2048]{1,0:T(8,128)(2,1)S(1)} %copy-done, f32[16,128]{1,0:T(8,128)S(1)} %bitcast.13, f32[16,128]{1,0:T(8,128)S(1)} %bitcast.15, f32[16,128]{1,0:T(8,128)S(1)} %bitcast.16), custom_call_target="tpu_custom_call" | custom-call | tf_op jit(solution)/shard_map/home/pallas_call | solution.py:339
Async XLA Ops:
  0.6 15.6 %copy-start = (bf16[128,2048]{1,0:T(8,128)(2,1)S(1)}, bf16[128,2048]{1,0:T(8,128)(2,1)}, u32[]{:S(2)}) copy-start(bf16[128,2048]{1,0:T(8,128)(2,1)} %own_ref.7) | copy-start | bytes 1572868
  1.8 8.9 %copy-start.2 = (s32[4,2]{0,1:T(2,128)S(1)}, s32[4,2]{0,1:T(2,128)}, u32[]{:S(2)}) copy-start(s32[4,2]{0,1:T(2,128)} %param.5) | copy-start | bytes 100
  1.8 14.1 %collective-permute-start = (bf16[128,1024]{1,0:T(8,128)(2,1)S(1)}, bf16[128,1024]{1,0:T(8,128)(2,1)S(1)}, u32[]{:S(2)}, u32[]{:S(2)}) collective-permute-start(bf16[128,1024]{1,0:T(8,128)(2,1)S(1)} %get-tuple-element.3), channel_id=1, source_target_pairs={{2,6},{3,7},{4,8},{5,9},{6,10},{7,11},{8,12},{9,13},{10,14},{11,15... | collective-permute-start | bytes 786440 | tf_op jit(solution)/shard_map/ppermute | solution.py:311
  3.1 13.2 %copy-start.1 = (s32[1,16]{1,0:T(1,128)S(1)}, s32[1,16]{1,0:T(1,128)}, u32[]{:S(2)}) copy-start(s32[1,16]{1,0:T(1,128)} %mask_ref.5) | copy-start | bytes 196
  3.1 13.2 %collective-permute-start.1 = (bf16[128,1024]{1,0:T(8,128)(2,1)S(1)}, bf16[128,1024]{1,0:T(8,128)(2,1)S(1)}, u32[]{:S(2)}, u32[]{:S(2)}) collective-permute-start(bf16[128,1024]{1,0:T(8,128)(2,1)S(1)} %get-tuple-element.2), channel_id=1, source_target_pairs={{6,2},{7,3},{8,4},{9,5},{10,6},{11,7},{12,8},{13,9},{14,10},{15,11... | collective-permute-start | bytes 786440 | tf_op jit(solution)/shard_map/ppermute | solution.py:311
where the time goes:
time: 71.4 us; the launch traced here: 71.2 us
  blocking collectives  31.7 us (44%)
  Pallas kernels  23.2 us (32%)
  starting transfers between devices  8.89 us (12%)
  waiting for transfers between devices  5.47 us (8%)
  local copies, waits for them, and re-layouts  1.23 us (2%)
    all_to_all x3, blocking collectives, shards(): gathered.append(lax.all_to_all(sent, 'tile', 0, 0, tiled=True))  31.7 us
    pallas_call x3, Pallas kernels, shards(): pl.pallas_call(functools.partial(chain_kernel, step, rows, nodes), out_sh...  18.4 us
    ppermute x2, starting transfers between devices, moved(): lax.ppermute(value, 'tile', [(place(s, i), place(d, i)) for s, d in pairs...  8.89 us
    ppermute x2, waiting for transfers between devices, moved(): lax.ppermute(value, 'tile', [(place(s, i), place(d, i)) for s, d in pairs...  5.47 us
    pallas_call x1, Pallas kernels, shards(): pl.pallas_call(functools.partial(home_kernel, rows, nodes), out_shape=(ja...  4.75 us
  transfers between devices with their start and end apart: 2, of which 2 were waited for; matrix products, arithmetic and copies ran while one was open for 0% of the time, Pallas kernels for 0%

commit v1 on v0

--- a/solution.py
+++ b/solution.py
@@ -15,7 +15,7 @@
 LANES = 128
 WIDTH = 2 * HALF + 1
 MASK_LANE = 64
-GROUP = 2
+GROUP = 4
 
 sharpness = 12.0
 anchor_weight = 2.0
@@ -72,15 +72,8 @@
 
 
 def section_grid(gathered, step, rows):
-    count = gathered.shape[0]
-    padded = rows + 8 - rows % 8
-    out = None
-    for group in (step - 1, step):
-        start = (group * rows + rows // 2) % count
-        part = jnp.concatenate([gathered[start:], gathered[:start]], axis=0) if start else gathered
-        part = part[:padded]
-        out = part if out is None else out + part
-    return out
+    out = gathered[(step - 1) * rows : step * rows] + gathered[step * rows : (step + 1) * rows]
+    return jnp.concatenate([out, jnp.zeros((8 - rows % 8, LANES), f32)], axis=0)
 
 
 def relax(grid, rows, nodes):
@@ -186,7 +179,7 @@
 
 
 def chain_kernel(
-    step, rows, nodes, offsets_ref, own_ref, below_ref, above_ref, mask_ref, *refs
+    step, rows, nodes, offsets_ref, own_ref, other_ref, mask_ref, *refs
 ):
     gathered_ref = refs[0] if step > 1 else None
     out_ref, score_ref, base_ref, swing_ref = refs[-4:]
@@ -207,8 +200,9 @@
     def one(index):
         here = pl.ds(pl.multiple_of(index * PATCH, PATCH), PATCH)
         beyond = pl.ds(pl.multiple_of((index + cols) * PATCH, PATCH), PATCH)
-        own = jnp.where(is_upper, own_ref[:, beyond], above_ref[:, here])
-        prev = jnp.where(is_upper, below_ref[:, here], own_ref[:, here])
+        other = other_ref[:, here]
+        own = jnp.where(is_upper, own_ref[:, beyond], other)
+        prev = jnp.where(is_upper, other, own_ref[:, here])
         own32, prev32 = own.astype(f32), prev.astype(f32)
         own_mean = stats(tile_sum(own32))
         own_var = stats(tile_sum((own32 - own_mean) * (own32 - own_mean)))
@@ -306,15 +300,26 @@
     cols = nodes // 2
     width = cols * PATCH
     place = lambda group, row: (group * rows + row + rows // 2) % count
-
-    def moved(value, pairs):
-        return lax.ppermute(
-            value, "tile", [(place(s, i), place(d, i)) for s, d in pairs for i in range(rows)]
-        )
-
-    left, right = sections[:, :width], sections[:, width:]
-    below = moved(right, [(s, s + 1) for s in range(SECTIONS - 1)])
-    above = moved(left, [(s + 1, s) for s in range(SECTIONS - 1)])
+    group = (lax.axis_index("tile") + count - rows // 2) % count // rows
+    row_groups = [[place(s, i) for i in range(rows)] for s in range(SECTIONS)]
+    section_groups = [[place(s, i) for s in range(SECTIONS)] for i in range(rows)]
+
+    def swapped(lower, after=None):
+        half = lax.dynamic_slice_in_dim(sections, jnp.where(group == lower, width, 0), width, 1)
+        if after is not None:
+            half, after = lax.optimization_barrier((half, after))
+        ends = [(place(lower, i), place(lower + 1, i)) for i in range(rows)]
+        return lax.ppermute(half, "tile", ends + [(d, s) for s, d in ends])
+
+    def exchanged(sent):
+        near = lax.all_to_all(sent, "tile", 0, 0, axis_index_groups=row_groups, tiled=True)
+        near = jnp.broadcast_to(near[None], (SECTIONS,) + near.shape)
+        return lax.all_to_all(
+            near, "tile", 0, 0, axis_index_groups=section_groups, tiled=True
+        ).reshape(count, LANES)
+
+    others = [swapped(0), swapped(1)]
+    others += [swapped(s, others[0]) for s in range(2, SECTIONS - 1)]
 
     vmem = pl.BlockSpec(memory_space=pltpu.VMEM)
     smem = pl.BlockSpec(memory_space=pltpu.SMEM)
@@ -324,8 +329,8 @@
         extra = gathered[-1:]
         sent = pl.pallas_call(
             functools.partial(chain_kernel, step, rows, nodes),
-            out_shape=jax.ShapeDtypeStruct((count, LANES), f32),
-            in_specs=[smem] + [vmem] * (4 + len(extra)),
+            out_shape=jax.ShapeDtypeStruct((rows, LANES), f32),
+            in_specs=[smem] + [vmem] * (3 + len(extra)),
             out_specs=vmem,
             scratch_shapes=[
                 pltpu.VMEM((cols, 16, LANES), f32),
@@ -334,8 +339,8 @@
             ],
             compiler_params=params,
             name=f"chain{step}",
-        )(coarse_offsets, sections, below, above, valid_mask, *extra)
-        gathered.append(lax.all_to_all(sent, "tile", 0, 0, tiled=True))
+        )(coarse_offsets, sections, others[step - 1], valid_mask, *extra)
+        gathered.append(exchanged(sent))
     return pl.pallas_call(
         functools.partial(home_kernel, rows, nodes),
         out_shape=(

time: 71.4 us -> 97.2 us (1.36); the launches traced: 71.2 us -> 95.7 us
  Pallas kernels: 23.2 us -> 33.7 us
  blocking collectives: 31.7 us -> 40.1 us
  starting transfers between devices: 8.89 us -> 15.1 us
  waiting for transfers between devices: 5.47 us -> 4.13 us
    pallas_call x3, Pallas kernels: 18.4 us -> 29.2 us  [shards(): pl.pallas_call(functools.partial(chain_kernel, step, rows, nodes), out_sh...]
    all_to_all x3 -> x5, blocking collectives: 31.7 us -> 40.1 us  [the longest x3 24.3 us: exchanged(): lax.all_to_all(sent, 'tile', 0, 0, axis_index_groups=row_groups, tiled=True)]
    ppermute x2 -> x3, waiting for transfers between devices: 5.47 us -> 0.01 us  [swapped(): return lax.ppermute(half, 'tile', ends + [(d, s) for s, d in ends])]
    all_to_all x0 -> x1, waiting for transfers between devices: none -> 4.12 us  [exchanged(): lax.all_to_all(near, 'tile', 0, 0, axis_index_groups=section_groups, tile...]
    all_to_all x0 -> x1, starting transfers between devices: none -> 3.46 us  [exchanged(): lax.all_to_all(near, 'tile', 0, 0, axis_index_groups=section_groups, tile...]
    ppermute x2 -> x3, starting transfers between devices: 8.89 us -> 11.7 us  [swapped(): return lax.ppermute(half, 'tile', ends + [(d, s) for s, d in ends])]
    dynamic_slice x0 -> x1, local copies, waits for them, and re-layouts: none -> 1.22 us  [swapped(): lax.dynamic_slice_in_dim(sections, jnp.where(group == lower, width, 0), w...]
    slice x1 -> x0, local copies, waits for them, and re-layouts: 1.12 us -> none  [shards(): left, right = (sections[:, :width], sections[:, width:])]
  transfers between devices with their start and end apart: 2 -> 4, of which waited for: 2 -> 1; matrix products, arithmetic and copies ran while one was open for 0% -> 1% of each run, Pallas kernels for 0% -> 17%
where the time goes in v1:
time: 97.2 us; the launch traced here: 95.7 us
  blocking collectives  40.1 us (41%)
  Pallas kernels  33.7 us (35%)
  starting transfers between devices  15.1 us (16%)
  waiting for transfers between devices  4.13 us (4%)
  local copies, waits for them, and re-layouts  1.94 us (2%)
    pallas_call x3, Pallas kernels, shards(): pl.pallas_call(functools.partial(chain_kernel, step, rows, nodes), out_sh...  29.2 us
    all_to_all x3, blocking collectives, exchanged(): lax.all_to_all(sent, 'tile', 0, 0, axis_index_groups=row_groups, tiled=True)  24.3 us
    all_to_all x2, blocking collectives, exchanged(): lax.all_to_all(near, 'tile', 0, 0, axis_index_groups=section_groups, tile...  15.8 us
    ppermute x3, starting transfers between devices, swapped(): return lax.ppermute(half, 'tile', ends + [(d, s) for s, d in ends])  11.7 us
    pallas_call x1, Pallas kernels, shards(): pl.pallas_call(functools.partial(home_kernel, rows, nodes), out_shape=(ja...  4.5 us
    all_to_all x1, waiting for transfers between devices, exchanged(): lax.all_to_all(near, 'tile', 0, 0, axis_index_groups=section_groups, tile...  4.12 us
    all_to_all x1, starting transfers between devices, exchanged(): lax.all_to_all(near, 'tile', 0, 0, axis_index_groups=section_groups, tile...  3.46 us
  transfers between devices with their start and end apart: 4, of which 1 were waited for; matrix products, arithmetic and copies ran while one was open for 1% of the time, Pallas kernels for 17%

profile of v1, /device:TPU:0, one launch (start us, length us, event | category | flops | bytes accessed | tf_op | source)
XLA Modules:
  0.0 95.7 jit_solution(15656628656845188820)
XLA Ops:
  0.7 0.0 copy-start
  0.7 1.2 %constant_dynamic-slice_fusion = (bf16[128,1024]{1,0:T(8,128)(2,1)S(1)}, bf16[128,1024]{1,0:T(8,128)(2,1)S(1)}, bf16[128,1024]{1,0:T(8,128)(2,1)S(1)}) fusion(bf16[128,2048]{1,0:T(8,128)(2,1)} %own_ref.7, s32[]{:T(128)S(6)} %select_n.28, s32[]{:T(128)S(6)} %select_n.27, s32[]{:T(128)S(6)} %select_n.26), kind=kLoop, calls=%fused_computation | loop fusion | bytes 1572876 | tf_op jit(solution)/shard_map/dynamic_slice | solution.py:308
  1.9 0.7 collective-permute-start
  2.6 0.0 copy-start.2
  2.6 0.7 collective-permute-start.1
  3.3 0.0 collective-permute-done.other_ref
  3.3 0.0 copy-start.1
  3.3 10.3 %collective-permute-start.2 = (bf16[128,1024]{1,0:T(8,128)(2,1)S(1)}, bf16[128,1024]{1,0:T(8,128)(2,1)S(1)}, u32[]{:S(2)}, u32[]{:S(2)}) collective-permute-start(bf16[128,1024]{1,0:T(8,128)(2,1)S(1)} %get-tuple-element.3), channel_id=1, source_target_pairs={{10,14},{11,15},{12,0},{13,1},{14,10},{15,11},{0,12},{1,13},{26,30... | collective-permute-start | bytes 786440 | tf_op jit(solution)/shard_map/ppermute | solution.py:312
  13.6 0.0 copy-done.2
  13.7 0.1 copy.8.offsets_ref
  13.7 0.0 copy-done
  13.7 0.0 copy-done.1
  13.7 2.7 %chain1.1 = f32[4,128]{1,0:T(4,128)S(1)} custom-call(s32[4,2]{1,0:T(4,128)S(1)} %copy.8.offsets_ref, bf16[128,2048]{1,0:T(8,128)(2,1)S(1)} %copy-done, bf16[128,1024]{1,0:T(8,128)(2,1)S(1)} %collective-permute-done.other_ref, s32[1,16]{1,0:T(1,128)S(1)} %copy-done.1), custom_call_target="tpu_custom_call" | custom-call | tf_op jit(solution)/shard_map/chain1/pallas_call | solution.py:330
  16.5 7.5 %all_to_all.42 = f32[4,1,128]{2,1,0:T(1,128)S(1)} all-to-all(f32[4,1,128]{2,1,0:T(1,128)S(1)} %bitcast.21), channel_id=1, replica_groups={{2,3,4,5},{6,7,8,9},{10,11,12,13},{14,15,0,1},{18,19,20,21},{22,23,24,2..., dimensions={0} | all-to-all | bytes 4096 | tf_op jit(solution)/shard_map/all_to_all | solution.py:315
  24.0 0.6 broadcast_in_dim.25
  24.6 3.5 %all-to-all-start.1 = ((f32[4,4,128]{2,1,0:T(4,128)}), f32[4,4,128]{2,1,0:T(4,128)S(1)}, u32[]{:S(2)}, u32[]{:S(2)}) async-start(f32[4,4,128]{2,1,0:T(4,128)} %broadcast_in_dim.25), calls=%async_computation.1 | async-start | bytes 16384 | tf_op jit(solution)/shard_map/all_to_all | solution.py:317
  28.0 0.0 collective-permute-done.1.other_ref
  28.0 4.1 %all-to-all-done.1 = f32[4,4,128]{2,1,0:T(4,128)S(1)} async-done(((f32[4,4,128]{2,1,0:T(4,128)}), f32[4,4,128]{2,1,0:T(4,128)S(1)}, u32[]{:S(2)}, u32[]{:S(2)}) %all-to-all-start.1) | async-done | bytes 8224 | tf_op jit(solution)/shard_map/all_to_all | solution.py:317
  32.2 13.2 %chain2.1 = f32[4,128]{1,0:T(4,128)S(1)} custom-call(s32[4,2]{1,0:T(4,128)S(1)} %copy.8.offsets_ref, bf16[128,2048]{1,0:T(8,128)(2,1)S(1)} %copy-done, bf16[128,1024]{1,0:T(8,128)(2,1)S(1)} %collective-permute-done.1.other_ref, s32[1,16]{1,0:T(1,128)S(1)} %copy-done.1, f32[16,128]{1,0:T(8,128)S(1)} %bitcast.15), custom_call_target="tpu_custom_call" | custom-call | tf_op jit(solution)/shard_map/chain2/pallas_call | solution.py:330
  45.4 8.7 %all_to_all.43 = f32[4,1,128]{2,1,0:T(1,128)S(1)} all-to-all(f32[4,1,128]{2,1,0:T(1,128)S(1)} %bitcast.22), channel_id=1, replica_groups={{2,3,4,5},{6,7,8,9},{10,11,12,13},{14,15,0,1},{18,19,20,21},{22,23,24,2..., dimensions={0} | all-to-all | bytes 4096 | tf_op jit(solution)/shard_map/all_to_all | solution.py:315
  54.1 7.9 %all_to_all.44 = f32[4,4,128]{2,1,0:T(4,128)S(1)} all-to-all(f32[4,4,128]{2,1,0:T(4,128)S(1)} %broadcast_in_dim.27), channel_id=1, replica_groups={{2,6,10,14},{3,7,11,15},{4,8,12,0},{5,9,13,1},{18,22,26,30},{19,23,27,3..., dimensions={0} | all-to-all | bytes 16384 | tf_op jit(solution)/shard_map/all_to_all | solution.py:317
  62.0 0.0 collective-permute-done.2.other_ref
  62.0 13.2 %chain3.1 = f32[4,128]{1,0:T(4,128)S(1)} custom-call(s32[4,2]{1,0:T(4,128)S(1)} %copy.8.offsets_ref, bf16[128,2048]{1,0:T(8,128)(2,1)S(1)} %copy-done, bf16[128,1024]{1,0:T(8,128)(2,1)S(1)} %collective-permute-done.2.other_ref, s32[1,16]{1,0:T(1,128)S(1)} %copy-done.1, f32[16,128]{1,0:T(8,128)S(1)} %bitcast.17), custom_call_target="tpu_custom_call" | custom-call | tf_op jit(solution)/shard_map/chain3/pallas_call | solution.py:330
  75.2 8.1 %all_to_all.45 = f32[4,1,128]{2,1,0:T(1,128)S(1)} all-to-all(f32[4,1,128]{2,1,0:T(1,128)S(1)} %bitcast.20), channel_id=1, replica_groups={{2,3,4,5},{6,7,8,9},{10,11,12,13},{14,15,0,1},{18,19,20,21},{22,23,24,2..., dimensions={0} | all-to-all | bytes 4096 | tf_op jit(solution)/shard_map/all_to_all | solution.py:315
  83.4 7.9 %all_to_all.46 = f32[4,4,128]{2,1,0:T(4,128)S(1)} all-to-all(f32[4,4,128]{2,1,0:T(4,128)S(1)} %broadcast_in_dim.29), channel_id=1, replica_groups={{2,6,10,14},{3,7,11,15},{4,8,12,0},{5,9,13,1},{18,22,26,30},{19,23,27,3..., dimensions={0} | all-to-all | bytes 16384 | tf_op jit(solution)/shard_map/all_to_all | solution.py:317
  91.3 4.5 %home.1 = (bf16[128,2048]{1,0:T(8,128)(2,1)}, f32[2,1,16]{2,1,0:T(1,128)}) custom-call(bf16[128,2048]{1,0:T(8,128)(2,1)S(1)} %copy-done, f32[16,128]{1,0:T(8,128)S(1)} %bitcast.16, f32[16,128]{1,0:T(8,128)S(1)} %bitcast.18, f32[16,128]{1,0:T(8,128)S(1)} %bitcast.19), custom_call_target="tpu_custom_call" | custom-call | tf_op jit(solution)/shard_map/home/pallas_call | solution.py:344
  (2 shorter events, 0.0 us)
Async XLA Ops:
  0.7 13.1 %copy-start = (bf16[128,2048]{1,0:T(8,128)(2,1)S(1)}, bf16[128,2048]{1,0:T(8,128)(2,1)}, u32[]{:S(2)}) copy-start(bf16[128,2048]{1,0:T(8,128)(2,1)} %own_ref.7) | copy-start | bytes 1572868
  1.9 1.4 %collective-permute-start = (bf16[128,1024]{1,0:T(8,128)(2,1)S(1)}, bf16[128,1024]{1,0:T(8,128)(2,1)S(1)}, u32[]{:S(2)}, u32[]{:S(2)}) collective-permute-start(bf16[128,1024]{1,0:T(8,128)(2,1)S(1)} %get-tuple-element.6), channel_id=1, source_target_pairs={{2,6},{3,7},{4,8},{5,9},{6,2},{7,3},{8,4},{9,5},{18,22},{19,23},{2... | collective-permute-start | bytes 786440 | tf_op jit(solution)/shard_map/ppermute | solution.py:312
  2.6 11.0 %copy-start.2 = (s32[4,2]{0,1:T(2,128)S(1)}, s32[4,2]{0,1:T(2,128)}, u32[]{:S(2)}) copy-start(s32[4,2]{0,1:T(2,128)} %param.5) | copy-start | bytes 100
  2.6 25.4 %collective-permute-start.1 = (bf16[128,1024]{1,0:T(8,128)(2,1)S(1)}, bf16[128,1024]{1,0:T(8,128)(2,1)S(1)}, u32[]{:S(2)}, u32[]{:S(2)}) collective-permute-start(bf16[128,1024]{1,0:T(8,128)(2,1)S(1)} %get-tuple-element.5), channel_id=1, source_target_pairs={{6,10},{7,11},{8,12},{9,13},{10,6},{11,7},{12,8},{13,9},{22,26},{2... | collective-permute-start | bytes 786440 | tf_op jit(solution)/shard_map/ppermute | solution.py:312
  3.3 10.4 %copy-start.1 = (s32[1,16]{1,0:T(1,128)S(1)}, s32[1,16]{1,0:T(1,128)}, u32[]{:S(2)}) copy-start(s32[1,16]{1,0:T(1,128)} %mask_ref.5) | copy-start | bytes 196
  3.3 58.7 %collective-permute-start.2 = (bf16[128,1024]{1,0:T(8,128)(2,1)S(1)}, bf16[128,1024]{1,0:T(8,128)(2,1)S(1)}, u32[]{:S(2)}, u32[]{:S(2)}) collective-permute-start(bf16[128,1024]{1,0:T(8,128)(2,1)S(1)} %get-tuple-element.3), channel_id=1, source_target_pairs={{10,14},{11,15},{12,0},{13,1},{14,10},{15,11},{0,12},{1,13},{26,30... | collective-permute-start | bytes 786440 | tf_op jit(solution)/shard_map/ppermute | solution.py:312
  24.6 7.6 %all-to-all-start.1 = ((f32[4,4,128]{2,1,0:T(4,128)}), f32[4,4,128]{2,1,0:T(4,128)S(1)}, u32[]{:S(2)}, u32[]{:S(2)}) async-start(f32[4,4,128]{2,1,0:T(4,128)} %broadcast_in_dim.25), calls=%async_computation.1 | async-start | bytes 16384 | tf_op jit(solution)/shard_map/all_to_all | solution.py:317

commit v2 on v1

--- a/solution.py
+++ b/solution.py
@@ -71,12 +71,12 @@
     return (1 - 2 * ((iota(shape, 0) + iota(shape, 1)) % 2)).astype(f32)
 
 
-def section_grid(gathered, step, rows):
-    out = gathered[(step - 1) * rows : step * rows] + gathered[step * rows : (step + 1) * rows]
-    return jnp.concatenate([out, jnp.zeros((8 - rows % 8, LANES), f32)], axis=0)
+def padded_rows(grid):
+    return jnp.concatenate([grid, jnp.zeros((8 - grid.shape[0] % 8, LANES), f32)], axis=0)
 
 
 def relax(grid, rows, nodes):
+    grid = padded_rows(grid)
     shape = grid.shape
     row, lane = iota(shape, 0), iota(shape, 1)
     col = lane % nodes
@@ -178,60 +178,67 @@
     return total(tile) * (1.0 / (PATCH * PATCH))
 
 
-def chain_kernel(
-    step, rows, nodes, offsets_ref, own_ref, other_ref, mask_ref, *refs
-):
-    gathered_ref = refs[0] if step > 1 else None
-    out_ref, score_ref, base_ref, swing_ref = refs[-4:]
+def looped(count, one):
+    def body(turn, carry):
+        for k in range(GROUP):
+            one(turn * GROUP + k)
+        return carry
+
+    lax.fori_loop(0, count // GROUP, body, 0)
+
+
+def columns(index):
+    return pl.ds(pl.multiple_of(index * PATCH, PATCH), PATCH)
+
+
+def warp_indexed(patch, base_ref, swing_ref, index, cols):
+    nyquist = total(tile_sum(patch.astype(f32)) * sign_tile((8, LANES)))
+    return warp(
+        patch,
+        base_ref[pl.ds(index, 1), :],
+        base_ref[pl.ds(index + cols, 1), :],
+        swing_ref[pl.ds(index, 1), :],
+        swing_ref[pl.ds(index + cols, 1), :],
+        nyquist,
+    ).astype(bf16)
+
+
+def chain_kernel(step, rows, nodes, offsets_ref, own_ref, other_ref, mask_ref, *refs):
+    out_ref, score_ref, prev_ref, base_ref, swing_ref = refs[-5:]
     cols = nodes // 2
     count = lax.axis_size("tile")
     rotated = (lax.axis_index("tile") + count - rows // 2) % count
     group, row_index = rotated // rows, rotated % rows
     is_upper = group == step
     first = jnp.where(is_upper, cols, 0)
-    if step > 1:
-        shift = relax(section_grid(gathered_ref[...], step - 1, rows), rows, nodes)
-        base, swing = kernels_of(own_row(shift, row_index), first, cols, nodes)
-        base_ref[...] = base
-        swing_ref[...] = swing
     row_offset, col_offset = offsets_ref[step, 0], offsets_ref[step, 1]
     area = float(PATCH * PATCH)
 
+    if step > 1:
+        near_ref, next_ref, beyond_ref = refs[:3]
+        grid = next_ref[...] + jnp.where(is_upper, beyond_ref[...], near_ref[...])
+        row_shift = own_row(relax(grid, rows, nodes), row_index)
+        base_ref[...], swing_ref[...] = kernels_of(row_shift, first, cols, nodes)
+
+        def warp_one(index):
+            patch = jnp.where(is_upper, other_ref[:, columns(index)], own_ref[:, columns(index)])
+            prev_ref[index] = warp_indexed(patch, base_ref, swing_ref, index, cols)
+
+        looped(cols, warp_one)
+
     def one(index):
-        here = pl.ds(pl.multiple_of(index * PATCH, PATCH), PATCH)
-        beyond = pl.ds(pl.multiple_of((index + cols) * PATCH, PATCH), PATCH)
-        other = other_ref[:, here]
-        own = jnp.where(is_upper, own_ref[:, beyond], other)
-        prev = jnp.where(is_upper, other, own_ref[:, here])
+        other = other_ref[:, columns(index)]
+        own = jnp.where(is_upper, own_ref[:, columns(index + cols)], other)
+        prev = prev_ref[index] if step > 1 else jnp.where(is_upper, other, own_ref[:, columns(index)])
         own32, prev32 = own.astype(f32), prev.astype(f32)
-        own_mean = stats(tile_sum(own32))
+        own_mean, prev_mean = stats(tile_sum(own32)), stats(tile_sum(prev32))
         own_var = stats(tile_sum((own32 - own_mean) * (own32 - own_mean)))
-        prev_tile = tile_sum(prev32)
-        prev_mean = stats(prev_tile)
-        if step > 1:
-            nyquist = total(prev_tile * sign_tile((8, LANES)))
-            prev = warp(
-                prev,
-                base_ref[pl.ds(index, 1), :],
-                base_ref[pl.ds(index + cols, 1), :],
-                swing_ref[pl.ds(index, 1), :],
-                swing_ref[pl.ds(index + cols, 1), :],
-                nyquist,
-            ).astype(bf16)
-            prev32 = prev.astype(f32)
-        centre = prev32 - prev_mean
-        drift = stats(tile_sum(centre))
-        prev_var = stats(tile_sum(centre * centre)) - drift * drift
+        prev_var = stats(tile_sum((prev32 - prev_mean) * (prev32 - prev_mean)))
         spread = jnp.sqrt((own_var + 1e-5) * (prev_var + 1e-5))
-        lags = correlate(own, prev, (own_mean * (prev_mean + drift)) * (8.0 * LANES), col_offset)
+        lags = correlate(own, prev, (own_mean * prev_mean) * (8.0 * LANES), col_offset)
         score_ref[pl.ds(index, 1)] = (lags * (sharpness / area / spread))[None]
 
-    def body(turn, carry):
-        for k in range(GROUP):
-            one(turn * GROUP + k)
-        return carry
-
-    lax.fori_loop(0, cols // GROUP, body, 0)
+    looped(cols, one)
     shape = (cols, 16, LANES)
     line, lane = iota(shape, 1), iota(shape, 2)
     row_step = 16 - lane - row_offset
@@ -251,46 +258,30 @@
         axis=1,
     )
     sent = sent + jnp.where(is_upper, masks, 0.0)
-    out_ref[...] = jnp.broadcast_to(sent, out_ref.shape)
+    out_ref[...] = jnp.where(iota(out_ref.shape, 0) == row_index, sent, 0.0)
 
 
 def home_kernel(rows, nodes, own_ref, *refs):
-    gathered_refs = refs[: SECTIONS - 1]
-    out_ref, shift_ref, base_ref, swing_ref = refs[SECTIONS - 1 :]
+    out_ref, shift_ref, base_ref, swing_ref = refs[-4:]
     count = lax.axis_size("tile")
     rotated = (lax.axis_index("tile") + count - rows // 2) % count
     group, row_index = rotated // rows, rotated % rows
     grid = None
     for step in range(1, SECTIONS):
-        part = section_grid(gathered_refs[step - 1][...], step, rows)
+        near_ref, next_ref = refs[2 * step - 2 : 2 * step]
+        part = near_ref[...] + next_ref[...]
         grid = part if grid is None else jnp.where(group == step, part, grid)
     row_shift = own_row(relax(grid, rows, nodes), row_index)
     row_shift = jnp.where(group == 0, 0.0, row_shift)
     shift_ref[0, :, :] = row_shift[:, :nodes]
     shift_ref[1, :, :] = pltpu.roll(row_shift, LANES - nodes, 1)[:, :nodes]
-    base, swing = kernels_of(row_shift, 0, nodes, nodes)
-    base_ref[...] = base
-    swing_ref[...] = swing
+    base_ref[...], swing_ref[...] = kernels_of(row_shift, 0, nodes, nodes)
 
     def one(index):
-        here = pl.ds(pl.multiple_of(index * PATCH, PATCH), PATCH)
-        own = own_ref[:, here]
-        nyquist = total(tile_sum(own.astype(f32)) * sign_tile((8, LANES)))
-        out_ref[:, here] = warp(
-            own,
-            base_ref[pl.ds(index, 1), :],
-            base_ref[pl.ds(index + nodes, 1), :],
-            swing_ref[pl.ds(index, 1), :],
-            swing_ref[pl.ds(index + nodes, 1), :],
-            nyquist,
-        ).astype(bf16)
-
-    def body(turn, carry):
-        for k in range(GROUP):
-            one(turn * GROUP + k)
-        return carry
-
-    lax.fori_loop(0, nodes // GROUP, body, 0)
+        here = columns(index)
+        out_ref[:, here] = warp_indexed(own_ref[:, here], base_ref, swing_ref, index, nodes)
+
+    looped(nodes, one)
 
 
 def shards(sections, valid_mask, coarse_offsets):
@@ -301,32 +292,46 @@
     width = cols * PATCH
     place = lambda group, row: (group * rows + row + rows // 2) % count
     group = (lax.axis_index("tile") + count - rows // 2) % count // rows
-    row_groups = [[place(s, i) for i in range(rows)] for s in range(SECTIONS)]
-    section_groups = [[place(s, i) for s in range(SECTIONS)] for i in range(rows)]
+    moved = lambda value, pairs: lax.ppermute(value, "tile", pairs)
 
     def swapped(lower, after=None):
         half = lax.dynamic_slice_in_dim(sections, jnp.where(group == lower, width, 0), width, 1)
         if after is not None:
             half, after = lax.optimization_barrier((half, after))
         ends = [(place(lower, i), place(lower + 1, i)) for i in range(rows)]
-        return lax.ppermute(half, "tile", ends + [(d, s) for s, d in ends])
-
-    def exchanged(sent):
-        near = lax.all_to_all(sent, "tile", 0, 0, axis_index_groups=row_groups, tiled=True)
-        near = jnp.broadcast_to(near[None], (SECTIONS,) + near.shape)
-        return lax.all_to_all(
-            near, "tile", 0, 0, axis_index_groups=section_groups, tiled=True
-        ).reshape(count, LANES)
+        return moved(half, ends + [(d, s) for s, d in ends])
+
+    def exchanged(sent, step):
+        around = [
+            moved(
+                sent,
+                [
+                    (place(s, i), place(s, (i + k) % rows))
+                    for s in range(SECTIONS)
+                    for i in range(rows)
+                ],
+            )
+            for k in range(1, rows)
+        ]
+        near = functools.reduce(jnp.add, around, sent)
+        onward = lambda source, ahead: [
+            (place(source, i), place(source + ahead, i))
+            for i in range(rows)
+            if source + ahead < SECTIONS
+        ]
+        ahead = moved(near, onward(step - 1, 1) + onward(step, 1))
+        if step + 1 == SECTIONS:
+            return near, ahead
+        return near, ahead, moved(near, onward(step - 1, 2))
 
     others = [swapped(0), swapped(1)]
-    others += [swapped(s, others[0]) for s in range(2, SECTIONS - 1)]
 
     vmem = pl.BlockSpec(memory_space=pltpu.VMEM)
     smem = pl.BlockSpec(memory_space=pltpu.SMEM)
     params = pltpu.CompilerParams(vmem_limit_bytes=16 * 2**20)
     gathered = []
     for step in range(1, SECTIONS):
-        extra = gathered[-1:]
+        extra = gathered[-1] if gathered else ()
         sent = pl.pallas_call(
             functools.partial(chain_kernel, step, rows, nodes),
             out_shape=jax.ShapeDtypeStruct((rows, LANES), f32),
@@ -334,25 +339,28 @@
             out_specs=vmem,
             scratch_shapes=[
                 pltpu.VMEM((cols, 16, LANES), f32),
+                pltpu.VMEM((cols, PATCH, PATCH), bf16),
                 pltpu.VMEM((2 * cols, LANES), f32),
                 pltpu.VMEM((2 * cols, LANES), f32),
             ],
             compiler_params=params,
             name=f"chain{step}",
         )(coarse_offsets, sections, others[step - 1], valid_mask, *extra)
-        gathered.append(exchanged(sent))
+        gathered.append(exchanged(sent, step))
+        if step + 1 < SECTIONS - 1:
+            others.append(swapped(step + 1, gathered[-1][0]))
     return pl.pallas_call(
         functools.partial(home_kernel, rows, nodes),
         out_shape=(
             jax.ShapeDtypeStruct(sections.shape, bf16),
             jax.ShapeDtypeStruct((2, 1, nodes), f32),
         ),
-        in_specs=[vmem] * SECTIONS,
+        in_specs=[vmem] * (2 * SECTIONS - 1),
         out_specs=(vmem, vmem),
         scratch_shapes=[pltpu.VMEM((2 * nodes, LANES), f32)] * 2,
         compiler_params=params,
         name="home",
-    )(sections, *gathered)
+    )(sections, *[rows_of for parts in gathered for rows_of in parts[:2]])
 
 
 def solution(mesh):

time: 97.2 us -> 72.7 us (0.75)
  blocking collectives: 40.1 us -> 0 us
  starting transfers between devices: 15.1 us -> 33.1 us
  Pallas kernels: 33.7 us -> 16.5 us
  waiting for transfers between devices: 4.13 us -> 20 us
    all_to_all x5 -> x0, blocking collectives: 40.1 us -> none  [the longest x3 24.3 us: exchanged(): lax.all_to_all(sent, 'tile', 0, 0, axis_index_groups=row_groups, tiled=True)]
    ppermute x3 -> x17, starting transfers between devices: 11.7 us -> 33.1 us  [shards(): moved = lambda value, pairs: lax.ppermute(value, 'tile', pairs)]
    ppermute x3 -> x17, waiting for transfers between devices: 0.01 us -> 20 us  [shards(): moved = lambda value, pairs: lax.ppermute(value, 'tile', pairs)]
    pallas_call x3, Pallas kernels: 29.2 us -> 12 us  [shards(): pl.pallas_call(functools.partial(chain_kernel, step, rows, nodes), out_sh...]
    all_to_all x1 -> x0, waiting for transfers between devices: 4.12 us -> none  [exchanged(): lax.all_to_all(near, 'tile', 0, 0, axis_index_groups=section_groups, tile...]
    all_to_all x1 -> x0, starting transfers between devices: 3.46 us -> none  [exchanged(): lax.all_to_all(near, 'tile', 0, 0, axis_index_groups=section_groups, tile...]
  transfers between devices with their start and end apart: 4 -> 17, of which waited for: 1 -> 7; matrix products, arithmetic and copies ran while one was open for 1% -> 0% of each run, Pallas kernels for 17% -> 10%
where the time goes in v2:
time: 72.7 us; the launch traced here: 71.7 us
  starting transfers between devices  33.1 us (46%)
  waiting for transfers between devices  20 us (28%)
  Pallas kernels  16.5 us (23%)
  local copies, waits for them, and re-layouts  1.33 us (2%)
  between operations  0.83 us (1%)
    ppermute x17, starting transfers between devices, shards(): moved = lambda value, pairs: lax.ppermute(value, 'tile', pairs)  33.1 us
    ppermute x17, waiting for transfers between devices, shards(): moved = lambda value, pairs: lax.ppermute(value, 'tile', pairs)  20 us
    pallas_call x3, Pallas kernels, shards(): pl.pallas_call(functools.partial(chain_kernel, step, rows, nodes), out_sh...  12 us
    pallas_call x1, Pallas kernels, shards(): pl.pallas_call(functools.partial(home_kernel, rows, nodes), out_shape=(ja...  4.5 us
  transfers between devices with their start and end apart: 17, of which 7 were waited for; matrix products, arithmetic and copies ran while one was open for 0% of the time, Pallas kernels for 10%

profile of v2, /device:TPU:0, one launch (start us, length us, event | category | flops | bytes accessed | tf_op | source)
XLA Modules:
  0.0 71.7 jit_solution(14649245679839572086)
XLA Ops:
  0.7 0.0 copy-start
  0.7 1.2 %constant_dynamic-slice_fusion = (bf16[128,1024]{1,0:T(8,128)(2,1)S(1)}, bf16[128,1024]{1,0:T(8,128)(2,1)S(1)}, bf16[128,1024]{1,0:T(8,128)(2,1)S(1)}) fusion(bf16[128,2048]{1,0:T(8,128)(2,1)} %own_ref.7, s32[]{:T(128)S(6)} %select_n.28, s32[]{:T(128)S(6)} %select_n.27, s32[]{:T(128)S(6)} %select_n.26), kind=kLoop, calls=%fused_computation.3 | loop fusion | bytes 1572876 | tf_op jit(solution)/shard_map/dynamic_slice | solution.py:298
  1.9 0.0 copy-start.2
  1.9 0.7 collective-permute-start
  2.6 0.0 copy-start.1
  2.6 0.7 collective-permute-start.5
  3.3 0.0 copy-done.2
  3.3 0.1 copy.5.offsets_ref
  3.4 0.0 collective-permute-done.other_ref
  3.4 0.0 copy-done
  3.4 0.0 copy-done.1
  3.4 2.6 %chain1.1 = f32[4,128]{1,0:T(4,128)S(1)} custom-call(s32[4,2]{1,0:T(4,128)S(1)} %copy.5.offsets_ref, bf16[128,2048]{1,0:T(8,128)(2,1)S(1)} %copy-done, bf16[128,1024]{1,0:T(8,128)(2,1)S(1)} %collective-permute-done.other_ref, s32[1,16]{1,0:T(1,128)S(1)} %copy-done.1), custom_call_target="tpu_custom_call" | custom-call | tf_op jit(solution)/shard_map/chain1/pallas_call | solution.py:335
  6.1 0.5 collective-permute-start.1
  6.6 5.6 %collective-permute-start.2 = (f32[4,128]{1,0:T(4,128)S(1)}, f32[4,128]{1,0:T(4,128)S(1)}, u32[]{:S(2)}, u32[]{:S(2)}) collective-permute-start(f32[4,128]{1,0:T(4,128)S(1)} %chain1.1), channel_id=1, source_target_pairs={{2,4},{3,5},{4,2},{5,3},{6,8},{7,9},{8,6},{9,7},{10,12},{11,13},{1... | collective-permute-start | bytes 6152 | tf_op jit(solution)/shard_map/ppermute | solution.py:295
  12.2 4.1 %collective-permute-start.3 = (f32[4,128]{1,0:T(4,128)S(1)}, f32[4,128]{1,0:T(4,128)S(1)}, u32[]{:S(2)}, u32[]{:S(2)}) collective-permute-start(f32[4,128]{1,0:T(4,128)S(1)} %chain1.1), channel_id=1, source_target_pairs={{2,5},{3,2},{4,3},{5,4},{6,9},{7,6},{8,7},{9,8},{10,13},{11,10},{1... | collective-permute-start | bytes 6152 | tf_op jit(solution)/shard_map/ppermute | solution.py:295
  16.3 0.0 collective-permute-done.1
  16.3 0.0 collective-permute-done.2
  16.3 1.3 %collective-permute-done.3 = f32[4,128]{1,0:T(4,128)S(1)} collective-permute-done((f32[4,128]{1,0:T(4,128)S(1)}, f32[4,128]{1,0:T(4,128)S(1)}, u32[]{:S(2)}, u32[]{:S(2)}) %collective-permute-start.3) | collective-permute-done | bytes 2080 | tf_op jit(solution)/shard_map/ppermute | solution.py:295
  17.6 3.9 %collective-permute-start.11 = (bf16[128,1024]{1,0:T(8,128)(2,1)S(1)}, bf16[128,1024]{1,0:T(8,128)(2,1)S(1)}, u32[]{:S(2)}, u32[]{:S(2)}) collective-permute-start(bf16[128,1024]{1,0:T(8,128)(2,1)S(1)} %get-tuple-element.3), channel_id=1, source_target_pairs={{10,14},{11,15},{12,0},{13,1},{14,10},{15,11},{0,12},{1,13},{26,30... | collective-permute-start | bytes 786440 | tf_op jit(solution)/shard_map/ppermute | solution.py:295
  21.5 0.7 collective-permute-start.4
  22.2 0.7 collective-permute-start.6
  22.8 0.0 collective-permute-done.5.other_ref
  22.9 0.0 collective-permute-done.4.refs_1_
  22.9 0.0 collective-permute-done.6.refs_2_
  22.9 4.7 %chain2.1 = f32[4,128]{1,0:T(4,128)S(1)} custom-call(s32[4,2]{1,0:T(4,128)S(1)} %copy.5.offsets_ref, bf16[128,2048]{1,0:T(8,128)(2,1)S(1)} %copy-done, bf16[128,1024]{1,0:T(8,128)(2,1)S(1)} %collective-permute-done.5.other_ref, s32[1,16]{1,0:T(1,128)S(1)} %copy-done.1, f32[4,128]{1,0:T(4,128)S(1)} %add_add_fusion.2.refs_0_, ...), custom_call_target="tpu_custom_call" | custom-call | tf_op jit(solution)/shard_map/chain2/pallas_call | solution.py:335
  27.6 1.4 %collective-permute-start.7 = (f32[4,128]{1,0:T(4,128)S(1)}, f32[4,128]{1,0:T(4,128)S(1)}, u32[]{:S(2)}, u32[]{:S(2)}) collective-permute-start(f32[4,128]{1,0:T(4,128)S(1)} %chain2.1), channel_id=1, source_target_pairs={{2,3},{3,4},{4,5},{5,2},{6,7},{7,8},{8,9},{9,6},{10,11},{11,12},{1... | collective-permute-start | bytes 6152 | tf_op jit(solution)/shard_map/ppermute | solution.py:295
  28.9 1.5 %collective-permute-start.8 = (f32[4,128]{1,0:T(4,128)S(1)}, f32[4,128]{1,0:T(4,128)S(1)}, u32[]{:S(2)}, u32[]{:S(2)}) collective-permute-start(f32[4,128]{1,0:T(4,128)S(1)} %chain2.1), channel_id=1, source_target_pairs={{2,4},{3,5},{4,2},{5,3},{6,8},{7,9},{8,6},{9,7},{10,12},{11,13},{1... | collective-permute-start | bytes 6152 | tf_op jit(solution)/shard_map/ppermute | solution.py:295
  30.4 2.9 %collective-permute-start.9 = (f32[4,128]{1,0:T(4,128)S(1)}, f32[4,128]{1,0:T(4,128)S(1)}, u32[]{:S(2)}, u32[]{:S(2)}) collective-permute-start(f32[4,128]{1,0:T(4,128)S(1)} %chain2.1), channel_id=1, source_target_pairs={{2,5},{3,2},{4,3},{5,4},{6,9},{7,6},{8,7},{9,8},{10,13},{11,10},{1... | collective-permute-start | bytes 6152 | tf_op jit(solution)/shard_map/ppermute | solution.py:295
  33.3 0.0 collective-permute-done.7
  33.3 1.9 %collective-permute-done.8 = f32[4,128]{1,0:T(4,128)S(1)} collective-permute-done((f32[4,128]{1,0:T(4,128)S(1)}, f32[4,128]{1,0:T(4,128)S(1)}, u32[]{:S(2)}, u32[]{:S(2)}) %collective-permute-start.8) | collective-permute-done | bytes 2080 | tf_op jit(solution)/shard_map/ppermute | solution.py:295
  35.2 0.0 collective-permute-done.9
  35.2 1.3 %collective-permute-start.10 = (f32[4,128]{1,0:T(4,128)S(1)}, f32[4,128]{1,0:T(4,128)S(1)}, u32[]{:S(2)}, u32[]{:S(2)}) collective-permute-start(f32[4,128]{1,0:T(4,128)S(1)} %add_add_fusion.1.refs_0_.refs_2_), channel_id=1, source_target_pairs={{6,10},{7,11},{8,12},{9,13},{10,14},{11,15},{12,0},{13,1},{22,26},... | collective-permute-start | bytes 6152 | tf_op jit(solution)/shard_map/ppermute | solution.py:295
  36.5 1.3 %collective-permute-start.12 = (f32[4,128]{1,0:T(4,128)S(1)}, f32[4,128]{1,0:T(4,128)S(1)}, u32[]{:S(2)}, u32[]{:S(2)}) collective-permute-start(f32[4,128]{1,0:T(4,128)S(1)} %add_add_fusion.1.refs_0_.refs_2_), channel_id=1, source_target_pairs={{6,14},{7,15},{8,0},{9,1},{22,30},{23,31},{24,16},{25,17}} | collective-permute-start | bytes 6152 | tf_op jit(solution)/shard_map/ppermute | solution.py:295
  37.8 7.6 %collective-permute-done.10.refs_1_.refs_3_ = f32[4,128]{1,0:T(4,128)S(1)} collective-permute-done((f32[4,128]{1,0:T(4,128)S(1)}, f32[4,128]{1,0:T(4,128)S(1)}, u32[]{:S(2)}, u32[]{:S(2)}) %collective-permute-start.10) | collective-permute-done | bytes 2080 | tf_op jit(solution)/shard_map/ppermute | solution.py:295
  45.4 1.8 %collective-permute-done.12.refs_2_ = f32[4,128]{1,0:T(4,128)S(1)} collective-permute-done((f32[4,128]{1,0:T(4,128)S(1)}, f32[4,128]{1,0:T(4,128)S(1)}, u32[]{:S(2)}, u32[]{:S(2)}) %collective-permute-start.12) | collective-permute-done | bytes 2080 | tf_op jit(solution)/shard_map/ppermute | solution.py:295
  47.3 0.0 collective-permute-done.11.other_ref
  47.3 4.7 %chain3.1 = f32[4,128]{1,0:T(4,128)S(1)} custom-call(s32[4,2]{1,0:T(4,128)S(1)} %copy.5.offsets_ref, bf16[128,2048]{1,0:T(8,128)(2,1)S(1)} %copy-done, bf16[128,1024]{1,0:T(8,128)(2,1)S(1)} %collective-permute-done.11.other_ref, s32[1,16]{1,0:T(1,128)S(1)} %copy-done.1, f32[4,128]{1,0:T(4,128)S(1)} %add_add_fusion.1.refs_0_.refs_2_, ...), custom_call_target="tpu_custom_call" | custom-call | tf_op jit(solution)/shard_map/chain3/pallas_call | solution.py:335
  52.0 0.5 collective-permute-start.13
  52.5 2.3 %collective-permute-start.14 = (f32[4,128]{1,0:T(4,128)S(1)}, f32[4,128]{1,0:T(4,128)S(1)}, u32[]{:S(2)}, u32[]{:S(2)}) collective-permute-start(f32[4,128]{1,0:T(4,128)S(1)} %chain3.1), channel_id=1, source_target_pairs={{2,4},{3,5},{4,2},{5,3},{6,8},{7,9},{8,6},{9,7},{10,12},{11,13},{1... | collective-permute-start | bytes 6152 | tf_op jit(solution)/shard_map/ppermute | solution.py:295
  54.8 3.9 %collective-permute-start.15 = (f32[4,128]{1,0:T(4,128)S(1)}, f32[4,128]{1,0:T(4,128)S(1)}, u32[]{:S(2)}, u32[]{:S(2)}) collective-permute-start(f32[4,128]{1,0:T(4,128)S(1)} %chain3.1), channel_id=1, source_target_pairs={{2,5},{3,2},{4,3},{5,4},{6,9},{7,6},{8,7},{9,8},{10,13},{11,10},{1... | collective-permute-start | bytes 6152 | tf_op jit(solution)/shard_map/ppermute | solution.py:295
  58.7 0.0 collective-permute-done.13
  58.7 0.1 collective-permute-done.14
  58.8 1.2 %collective-permute-done.15 = f32[4,128]{1,0:T(4,128)S(1)} collective-permute-done((f32[4,128]{1,0:T(4,128)S(1)}, f32[4,128]{1,0:T(4,128)S(1)}, u32[]{:S(2)}, u32[]{:S(2)}) %collective-permute-start.15) | collective-permute-done | bytes 2080 | tf_op jit(solution)/shard_map/ppermute | solution.py:295
  60.0 1.3 %collective-permute-start.16 = (f32[4,128]{1,0:T(4,128)S(1)}, f32[4,128]{1,0:T(4,128)S(1)}, u32[]{:S(2)}, u32[]{:S(2)}) collective-permute-start(f32[4,128]{1,0:T(4,128)S(1)} %add_add_fusion.refs_4_), channel_id=1, source_target_pairs={{10,14},{11,15},{12,0},{13,1},{26,30},{27,31},{28,16},{29,17}} | collective-permute-start | bytes 6152 | tf_op jit(solution)/shard_map/ppermute | solution.py:295
  61.3 6.0 %collective-permute-done.16.refs_5_ = f32[4,128]{1,0:T(4,128)S(1)} collective-permute-done((f32[4,128]{1,0:T(4,128)S(1)}, f32[4,128]{1,0:T(4,128)S(1)}, u32[]{:S(2)}, u32[]{:S(2)}) %collective-permute-start.16) | collective-permute-done | bytes 2080 | tf_op jit(solution)/shard_map/ppermute | solution.py:295
  67.2 4.5 %home.1 = (bf16[128,2048]{1,0:T(8,128)(2,1)}, f32[2,1,16]{2,1,0:T(1,128)}) custom-call(bf16[128,2048]{1,0:T(8,128)(2,1)S(1)} %copy-done, f32[4,128]{1,0:T(4,128)S(1)} %add_add_fusion.2.refs_0_, f32[4,128]{1,0:T(4,128)S(1)} %collective-permute-done.4.refs_1_, f32[4,128]{1,0:T(4,128)S(1)} %add_add_fusion.1.refs_0_.refs_2_, ...), custom_call_target="tpu_custom_call" | custom-call | tf_op jit(solution)/shard_map/home/pallas_call | solution.py:352
  (3 shorter events, 0.0 us)
Async XLA Ops:
  0.7 2.7 %copy-start = (bf16[128,2048]{1,0:T(8,128)(2,1)S(1)}, bf16[128,2048]{1,0:T(8,128)(2,1)}, u32[]{:S(2)}) copy-start(bf16[128,2048]{1,0:T(8,128)(2,1)} %own_ref.7) | copy-start | bytes 1572868
  1.9 1.4 %copy-start.2 = (s32[4,2]{0,1:T(2,128)S(1)}, s32[4,2]{0,1:T(2,128)}, u32[]{:S(2)}) copy-start(s32[4,2]{0,1:T(2,128)} %param.5) | copy-start | bytes 100
  1.9 1.5 %collective-permute-start = (bf16[128,1024]{1,0:T(8,128)(2,1)S(1)}, bf16[128,1024]{1,0:T(8,128)(2,1)S(1)}, u32[]{:S(2)}, u32[]{:S(2)}) collective-permute-start(bf16[128,1024]{1,0:T(8,128)(2,1)S(1)} %get-tuple-element.6), channel_id=1, source_target_pairs={{2,6},{3,7},{4,8},{5,9},{6,2},{7,3},{8,4},{9,5},{18,22},{19,23},{2... | collective-permute-start | bytes 786440 | tf_op jit(solution)/shard_map/ppermute | solution.py:295
  2.6 0.8 %copy-start.1 = (s32[1,16]{1,0:T(1,128)S(1)}, s32[1,16]{1,0:T(1,128)}, u32[]{:S(2)}) copy-start(s32[1,16]{1,0:T(1,128)} %mask_ref.5) | copy-start | bytes 196
  2.6 20.2 %collective-permute-start.5 = (bf16[128,1024]{1,0:T(8,128)(2,1)S(1)}, bf16[128,1024]{1,0:T(8,128)(2,1)S(1)}, u32[]{:S(2)}, u32[]{:S(2)}) collective-permute-start(bf16[128,1024]{1,0:T(8,128)(2,1)S(1)} %get-tuple-element.5), channel_id=1, source_target_pairs={{6,10},{7,11},{8,12},{9,13},{10,6},{11,7},{12,8},{13,9},{22,26},{2... | collective-permute-start | bytes 786440 | tf_op jit(solution)/shard_map/ppermute | solution.py:295
  6.1 10.2 %collective-permute-start.1 = (f32[4,128]{1,0:T(4,128)S(1)}, f32[4,128]{1,0:T(4,128)S(1)}, u32[]{:S(2)}, u32[]{:S(2)}) collective-permute-start(f32[4,128]{1,0:T(4,128)S(1)} %chain1.1), channel_id=1, source_target_pairs={{2,3},{3,4},{4,5},{5,2},{6,7},{7,8},{8,9},{9,6},{10,11},{11,12},{1... | collective-permute-start | bytes 6152 | tf_op jit(solution)/shard_map/ppermute | solution.py:295
  6.6 9.7 %collective-permute-start.2 = (f32[4,128]{1,0:T(4,128)S(1)}, f32[4,128]{1,0:T(4,128)S(1)}, u32[]{:S(2)}, u32[]{:S(2)}) collective-permute-start(f32[4,128]{1,0:T(4,128)S(1)} %chain1.1), channel_id=1, source_target_pairs={{2,4},{3,5},{4,2},{5,3},{6,8},{7,9},{8,6},{9,7},{10,12},{11,13},{1... | collective-permute-start | bytes 6152 | tf_op jit(solution)/shard_map/ppermute | solution.py:295
  12.2 5.4 %collective-permute-start.3 = (f32[4,128]{1,0:T(4,128)S(1)}, f32[4,128]{1,0:T(4,128)S(1)}, u32[]{:S(2)}, u32[]{:S(2)}) collective-permute-start(f32[4,128]{1,0:T(4,128)S(1)} %chain1.1), channel_id=1, source_target_pairs={{2,5},{3,2},{4,3},{5,4},{6,9},{7,6},{8,7},{9,8},{10,13},{11,10},{1... | collective-permute-start | bytes 6152 | tf_op jit(solution)/shard_map/ppermute | solution.py:295
  17.6 29.7 %collective-permute-start.11 = (bf16[128,1024]{1,0:T(8,128)(2,1)S(1)}, bf16[128,1024]{1,0:T(8,128)(2,1)S(1)}, u32[]{:S(2)}, u32[]{:S(2)}) collective-permute-start(bf16[128,1024]{1,0:T(8,128)(2,1)S(1)} %get-tuple-element.3), channel_id=1, source_target_pairs={{10,14},{11,15},{12,0},{13,1},{14,10},{15,11},{0,12},{1,13},{26,30... | collective-permute-start | bytes 786440 | tf_op jit(solution)/shard_map/ppermute | solution.py:295
  21.5 1.4 %collective-permute-start.4 = (f32[4,128]{1,0:T(4,128)S(1)}, f32[4,128]{1,0:T(4,128)S(1)}, u32[]{:S(2)}, u32[]{:S(2)}) collective-permute-start(f32[4,128]{1,0:T(4,128)S(1)} %add_add_fusion.2.refs_0_), channel_id=1, source_target_pairs={{2,6},{3,7},{4,8},{5,9},{6,10},{7,11},{8,12},{9,13},{18,22},{19,23... | collective-permute-start | bytes 6152 | tf_op jit(solution)/shard_map/ppermute | solution.py:295
  22.2 0.7 collective-permute-start.6
  27.6 5.8 %collective-permute-start.7 = (f32[4,128]{1,0:T(4,128)S(1)}, f32[4,128]{1,0:T(4,128)S(1)}, u32[]{:S(2)}, u32[]{:S(2)}) collective-permute-start(f32[4,128]{1,0:T(4,128)S(1)} %chain2.1), channel_id=1, source_target_pairs={{2,3},{3,4},{4,5},{5,2},{6,7},{7,8},{8,9},{9,6},{10,11},{11,12},{1... | collective-permute-start | bytes 6152 | tf_op jit(solution)/shard_map/ppermute | solution.py:295
  28.9 6.3 %collective-permute-start.8 = (f32[4,128]{1,0:T(4,128)S(1)}, f32[4,128]{1,0:T(4,128)S(1)}, u32[]{:S(2)}, u32[]{:S(2)}) collective-permute-start(f32[4,128]{1,0:T(4,128)S(1)} %chain2.1), channel_id=1, source_target_pairs={{2,4},{3,5},{4,2},{5,3},{6,8},{7,9},{8,6},{9,7},{10,12},{11,13},{1... | collective-permute-start | bytes 6152 | tf_op jit(solution)/shard_map/ppermute | solution.py:295
  30.4 4.8 %collective-permute-start.9 = (f32[4,128]{1,0:T(4,128)S(1)}, f32[4,128]{1,0:T(4,128)S(1)}, u32[]{:S(2)}, u32[]{:S(2)}) collective-permute-start(f32[4,128]{1,0:T(4,128)S(1)} %chain2.1), channel_id=1, source_target_pairs={{2,5},{3,2},{4,3},{5,4},{6,9},{7,6},{8,7},{9,8},{10,13},{11,10},{1... | collective-permute-start | bytes 6152 | tf_op jit(solution)/shard_map/ppermute | solution.py:295
  35.2 10.2 %collective-permute-start.10 = (f32[4,128]{1,0:T(4,128)S(1)}, f32[4,128]{1,0:T(4,128)S(1)}, u32[]{:S(2)}, u32[]{:S(2)}) collective-permute-start(f32[4,128]{1,0:T(4,128)S(1)} %add_add_fusion.1.refs_0_.refs_2_), channel_id=1, source_target_pairs={{6,10},{7,11},{8,12},{9,13},{10,14},{11,15},{12,0},{13,1},{22,26},... | collective-permute-start | bytes 6152 | tf_op jit(solution)/shard_map/ppermute | solution.py:295
  36.5 10.7 %collective-permute-start.12 = (f32[4,128]{1,0:T(4,128)S(1)}, f32[4,128]{1,0:T(4,128)S(1)}, u32[]{:S(2)}, u32[]{:S(2)}) collective-permute-start(f32[4,128]{1,0:T(4,128)S(1)} %add_add_fusion.1.refs_0_.refs_2_), channel_id=1, source_target_pairs={{6,14},{7,15},{8,0},{9,1},{22,30},{23,31},{24,16},{25,17}} | collective-permute-start | bytes 6152 | tf_op jit(solution)/shard_map/ppermute | solution.py:295
  52.0 6.7 %collective-permute-start.13 = (f32[4,128]{1,0:T(4,128)S(1)}, f32[4,128]{1,0:T(4,128)S(1)}, u32[]{:S(2)}, u32[]{:S(2)}) collective-permute-start(f32[4,128]{1,0:T(4,128)S(1)} %chain3.1), channel_id=1, source_target_pairs={{2,3},{3,4},{4,5},{5,2},{6,7},{7,8},{8,9},{9,6},{10,11},{11,12},{1... | collective-permute-start | bytes 6152 | tf_op jit(solution)/shard_map/ppermute | solution.py:295
  52.5 6.3 %collective-permute-start.14 = (f32[4,128]{1,0:T(4,128)S(1)}, f32[4,128]{1,0:T(4,128)S(1)}, u32[]{:S(2)}, u32[]{:S(2)}) collective-permute-start(f32[4,128]{1,0:T(4,128)S(1)} %chain3.1), channel_id=1, source_target_pairs={{2,4},{3,5},{4,2},{5,3},{6,8},{7,9},{8,6},{9,7},{10,12},{11,13},{1... | collective-permute-start | bytes 6152 | tf_op jit(solution)/shard_map/ppermute | solution.py:295
  54.8 5.2 %collective-permute-start.15 = (f32[4,128]{1,0:T(4,128)S(1)}, f32[4,128]{1,0:T(4,128)S(1)}, u32[]{:S(2)}, u32[]{:S(2)}) collective-permute-start(f32[4,128]{1,0:T(4,128)S(1)} %chain3.1), channel_id=1, source_target_pairs={{2,5},{3,2},{4,3},{5,4},{6,9},{7,6},{8,7},{9,8},{10,13},{11,10},{1... | collective-permute-start | bytes 6152 | tf_op jit(solution)/shard_map/ppermute | solution.py:295
  60.0 7.3 %collective-permute-start.16 = (f32[4,128]{1,0:T(4,128)S(1)}, f32[4,128]{1,0:T(4,128)S(1)}, u32[]{:S(2)}, u32[]{:S(2)}) collective-permute-start(f32[4,128]{1,0:T(4,128)S(1)} %add_add_fusion.refs_4_), channel_id=1, source_target_pairs={{10,14},{11,15},{12,0},{13,1},{26,30},{27,31},{28,16},{29,17}} | collective-permute-start | bytes 6152 | tf_op jit(solution)/shard_map/ppermute | solution.py:295

commit v3 on v2

--- a/solution.py
+++ b/solution.py
@@ -121,7 +121,9 @@
 
 
 def circulant(row):
-    return pltpu.roll(jnp.broadcast_to(row, (PATCH, LANES)), 0, 1, stride=1, stride_axis=0)
+    first = pltpu.roll(jnp.broadcast_to(row, (8, LANES)), 0, 1, stride=1, stride_axis=0)
+    later = [pltpu.roll(first, r, 1) for r in range(8, PATCH, 8)]
+    return jnp.concatenate([first] + later, axis=0)
 
 
 def warp(patch, row_base, col_base, row_swing, col_swing, nyquist):
@@ -138,7 +140,7 @@
     return out - factor * sign_tile((PATCH, LANES))
 
 
-def correlate(own, prev, base, column_offset):
+def correlate(own, prev, base, column_offset, band_ref):
     half, edge, third = PATCH // 2, 16, 3
     own32, prev32 = own.astype(f32), prev.astype(f32)
     left = []
@@ -148,14 +150,12 @@
         left.append(jnp.concatenate([turned[:half], turned[half:]], axis=1))
     right = []
     for j in range(third):
-        turned = (pltpu.roll(prev32, third * j, 1) if j else prev32).astype(bf16)
+        turned = pltpu.roll(prev32, third * j, 1).astype(bf16) if j else prev
         low = jnp.concatenate([turned[PATCH - edge :], turned[: PATCH - edge]], axis=0)
         high = jnp.concatenate([turned[half - edge :], turned[: half - edge]], axis=0)
         right.append(jnp.concatenate([low, high], axis=1))
     product = dot_t(jnp.concatenate(left, axis=0), jnp.concatenate(right, axis=0))
     lane = iota((8, LANES), 1)
-    sub = iota((16, LANES), 0)
-    out = jnp.zeros((16, LANES), f32)
     for j in range(third):
         for i in range(third):
             block = product[i * half : (i + 1) * half, j * LANES : (j + 1) * LANES]
@@ -165,17 +165,18 @@
                 kept = jnp.where(later, block[8 * k + 32 : 8 * k + 40], block[8 * k : 8 * k + 8])
                 kept = pltpu.roll(kept, LANES - 8 * k, 1) if k else kept
                 band = kept if band is None else band + kept
-            band = band - base
-            for step in (4, 2, 1):
-                band = band + pltpu.roll(pltpu.roll(band, 8 - step, 0), LANES - step, 1)
-            line = band[0:1]
-            line = line + pltpu.roll(line, LANES - 32, 1)
-            out = jnp.where(sub == i + third * j, line, out)
-    return out
-
-
-def stats(tile):
-    return total(tile) * (1.0 / (PATCH * PATCH))
+            band_ref[8 * (i + third * j) : 8 * (i + third * j) + 8, :] = band - base
+    out = None
+    for row in range(8):
+        part = band_ref[pl.ds(row, WIDTH, stride=8), :]
+        part = pltpu.roll(part, LANES - row, 1) if row else part
+        out = part if out is None else out + part
+    return out + pltpu.roll(out, LANES - 32, 1)
+
+
+def moments(values, corner):
+    values = values.astype(f32) - corner
+    return tile_sum(values), tile_sum(values * values)
 
 
 def looped(count, one):
@@ -204,7 +205,7 @@
 
 
 def chain_kernel(step, rows, nodes, offsets_ref, own_ref, other_ref, mask_ref, *refs):
-    out_ref, score_ref, prev_ref, base_ref, swing_ref = refs[-5:]
+    out_ref, score_ref, band_ref, sums_ref, corner_ref, prev_ref, base_ref, swing_ref = refs[-8:]
     cols = nodes // 2
     count = lax.axis_size("tile")
     rotated = (lax.axis_index("tile") + count - rows // 2) % count
@@ -215,9 +216,7 @@
     area = float(PATCH * PATCH)
 
     if step > 1:
-        near_ref, next_ref, beyond_ref = refs[:3]
-        grid = next_ref[...] + jnp.where(is_upper, beyond_ref[...], near_ref[...])
-        row_shift = own_row(relax(grid, rows, nodes), row_index)
+        row_shift = own_row(relax(refs[0][...], rows, nodes), row_index)
         base_ref[...], swing_ref[...] = kernels_of(row_shift, first, cols, nodes)
 
         def warp_one(index):
@@ -230,21 +229,30 @@
         other = other_ref[:, columns(index)]
         own = jnp.where(is_upper, own_ref[:, columns(index + cols)], other)
         prev = prev_ref[index] if step > 1 else jnp.where(is_upper, other, own_ref[:, columns(index)])
-        own32, prev32 = own.astype(f32), prev.astype(f32)
-        own_mean, prev_mean = stats(tile_sum(own32)), stats(tile_sum(prev32))
-        own_var = stats(tile_sum((own32 - own_mean) * (own32 - own_mean)))
-        prev_var = stats(tile_sum((prev32 - prev_mean) * (prev32 - prev_mean)))
-        spread = jnp.sqrt((own_var + 1e-5) * (prev_var + 1e-5))
-        lags = correlate(own, prev, (own_mean * prev_mean) * (8.0 * LANES), col_offset)
-        score_ref[pl.ds(index, 1)] = (lags * (sharpness / area / spread))[None]
+        own_corner, prev_corner = (x[0:1, 0:1].astype(f32) for x in (own, prev))
+        corner_ref[0, pl.ds(index, 1), :] = jnp.broadcast_to(own_corner, (1, LANES))
+        corner_ref[1, pl.ds(index, 1), :] = jnp.broadcast_to(prev_corner, (1, LANES))
+        sums = moments(own, own_corner) + moments(prev, prev_corner)
+        for k, value in enumerate(sums):
+            sums_ref[k, pl.ds(index, 1)] = value[None]
+        base = own_corner * prev_corner * (8.0 * LANES)
+        score_ref[pl.ds(index, 1)] = correlate(own, prev, base, col_offset, band_ref.at[index])[None]
 
     looped(cols, one)
-    shape = (cols, 16, LANES)
+    reduce = lambda value: jnp.sum(jnp.sum(value, axis=1), axis=1, keepdims=True)
+    own_sum, own_square, prev_sum, prev_square = (reduce(sums_ref[k]) * (1.0 / area) for k in range(4))
+    spread = jnp.sqrt(
+        (jnp.maximum(own_square - own_sum * own_sum, 0.0) + 1e-5)
+        * (jnp.maximum(prev_square - prev_sum * prev_sum, 0.0) + 1e-5)
+    )
+    scale = sharpness / area / spread
+    level = corner_ref[0] * prev_sum + corner_ref[1] * own_sum + own_sum * prev_sum
+    shape = (cols, WIDTH, LANES)
     line, lane = iota(shape, 1), iota(shape, 2)
     row_step = 16 - lane - row_offset
-    inside = (line < WIDTH) & (row_step >= -HALF) & (row_step <= HALF)
-    weights = jnp.where(inside, jnp.exp(jnp.where(inside, score_ref[...], 0.0)), 0.0)
-    reduce = lambda value: jnp.sum(jnp.sum(value, axis=1), axis=1, keepdims=True)
+    inside = (row_step >= -HALF) & (row_step <= HALF)
+    score = (score_ref[...] - (level * area)[:, None, :]) * jnp.broadcast_to(scale, (cols, LANES))[:, None, :]
+    weights = jnp.where(inside, jnp.exp(jnp.where(inside, score, 0.0)), 0.0)
     inverse = 1.0 / reduce(weights)
     flow_row = reduce(weights * (row_step + row_offset).astype(f32)) * inverse
     flow_col = reduce(weights * (line - HALF + col_offset).astype(f32)) * inverse
@@ -258,7 +266,8 @@
         axis=1,
     )
     sent = sent + jnp.where(is_upper, masks, 0.0)
-    out_ref[...] = jnp.where(iota(out_ref.shape, 0) == row_index, sent, 0.0)
+    sends = (iota(out_ref.shape, 0) == row_index) & (is_upper | (group == step - 1))
+    out_ref[...] = jnp.where(sends, sent, 0.0)
 
 
 def home_kernel(rows, nodes, own_ref, *refs):
@@ -268,8 +277,7 @@
     group, row_index = rotated // rows, rotated % rows
     grid = None
     for step in range(1, SECTIONS):
-        near_ref, next_ref = refs[2 * step - 2 : 2 * step]
-        part = near_ref[...] + next_ref[...]
+        part = refs[step - 1][...]
         grid = part if grid is None else jnp.where(group == step, part, grid)
     row_shift = own_row(relax(grid, rows, nodes), row_index)
     row_shift = jnp.where(group == 0, 0.0, row_shift)
@@ -301,29 +309,6 @@
         ends = [(place(lower, i), place(lower + 1, i)) for i in range(rows)]
         return moved(half, ends + [(d, s) for s, d in ends])
 
-    def exchanged(sent, step):
-        around = [
-            moved(
-                sent,
-                [
-                    (place(s, i), place(s, (i + k) % rows))
-                    for s in range(SECTIONS)
-                    for i in range(rows)
-                ],
-            )
-            for k in range(1, rows)
-        ]
-        near = functools.reduce(jnp.add, around, sent)
-        onward = lambda source, ahead: [
-            (place(source, i), place(source + ahead, i))
-            for i in range(rows)
-            if source + ahead < SECTIONS
-        ]
-        ahead = moved(near, onward(step - 1, 1) + onward(step, 1))
-        if step + 1 == SECTIONS:
-            return near, ahead
-        return near, ahead, moved(near, onward(step - 1, 2))
-
     others = [swapped(0), swapped(1)]
 
     vmem = pl.BlockSpec(memory_space=pltpu.VMEM)
@@ -331,14 +316,17 @@
     params = pltpu.CompilerParams(vmem_limit_bytes=16 * 2**20)
     gathered = []
     for step in range(1, SECTIONS):
-        extra = gathered[-1] if gathered else ()
+        extra = gathered[-1:]
         sent = pl.pallas_call(
             functools.partial(chain_kernel, step, rows, nodes),
             out_shape=jax.ShapeDtypeStruct((rows, LANES), f32),
             in_specs=[smem] + [vmem] * (3 + len(extra)),
             out_specs=vmem,
             scratch_shapes=[
-                pltpu.VMEM((cols, 16, LANES), f32),
+                pltpu.VMEM((cols, WIDTH, LANES), f32),
+                pltpu.VMEM((cols, 8 * WIDTH, LANES), f32),
+                pltpu.VMEM((4, cols, 8, LANES), f32),
+                pltpu.VMEM((2, cols, LANES), f32),
                 pltpu.VMEM((cols, PATCH, PATCH), bf16),
                 pltpu.VMEM((2 * cols, LANES), f32),
                 pltpu.VMEM((2 * cols, LANES), f32),
@@ -346,21 +334,21 @@
             compiler_params=params,
             name=f"chain{step}",
         )(coarse_offsets, sections, others[step - 1], valid_mask, *extra)
-        gathered.append(exchanged(sent, step))
+        gathered.append(lax.psum(sent, "tile"))
         if step + 1 < SECTIONS - 1:
-            others.append(swapped(step + 1, gathered[-1][0]))
+            others.append(swapped(step + 1, sent))
     return pl.pallas_call(
         functools.partial(home_kernel, rows, nodes),
         out_shape=(
             jax.ShapeDtypeStruct(sections.shape, bf16),
             jax.ShapeDtypeStruct((2, 1, nodes), f32),
         ),
-        in_specs=[vmem] * (2 * SECTIONS - 1),
+        in_specs=[vmem] * SECTIONS,
         out_specs=(vmem, vmem),
         scratch_shapes=[pltpu.VMEM((2 * nodes, LANES), f32)] * 2,
         compiler_params=params,
         name="home",
-    )(sections, *[rows_of for parts in gathered for rows_of in parts[:2]])
+    )(sections, *gathered)
 
 
 def solution(mesh):

time: 72.7 us -> 122 us (1.68)
  blocking collectives: 0 us -> 91.1 us
  starting transfers between devices: 33.1 us -> 11.7 us
  waiting for transfers between devices: 20 us -> 0.01 us
    psum x0 -> x3, blocking collectives: none -> 91.1 us  [shards(): gathered.append(lax.psum(sent, 'tile'))]
    ppermute x17 -> x3, starting transfers between devices: 33.1 us -> 11.7 us  [shards(): moved = lambda value, pairs: lax.ppermute(value, 'tile', pairs)]
    ppermute x17 -> x3, waiting for transfers between devices: 20 us -> 0.01 us  [shards(): moved = lambda value, pairs: lax.ppermute(value, 'tile', pairs)]
  transfers between devices with their start and end apart: 17 -> 3, of which waited for: 7 -> 0; matrix products, arithmetic and copies ran while one was open for 0% -> 0% of each run, Pallas kernels for 10% -> 6%
where the time goes in v3:
time: 122 us; the launch traced here: 121 us
  blocking collectives  91.1 us (75%)
  Pallas kernels  16.5 us (14%)
  starting transfers between devices  11.7 us (10%)
  local copies, waits for them, and re-layouts  1.33 us (1%)
    psum x3, blocking collectives, shards(): gathered.append(lax.psum(sent, 'tile'))  91.1 us
    ppermute x3, starting transfers between devices, shards(): moved = lambda value, pairs: lax.ppermute(value, 'tile', pairs)  11.7 us
    pallas_call x3, Pallas kernels, shards(): pl.pallas_call(functools.partial(chain_kernel, step, rows, nodes), out_sh...  11.6 us
    pallas_call x1, Pallas kernels, shards(): pl.pallas_call(functools.partial(home_kernel, rows, nodes), out_shape=(ja...  4.91 us
  transfers between devices with their start and end apart: 3, of which 0 were waited for; matrix products, arithmetic and copies ran while one was open for 0% of the time, Pallas kernels for 6%

profile of v3, /device:TPU:0, one launch (start us, length us, event | category | flops | bytes accessed | tf_op | source)
XLA Modules:
  0.0 121.3 jit_solution(6679238224261723016)
XLA Ops:
  0.7 0.0 copy-start
  0.7 1.2 %constant_dynamic-slice_fusion = (bf16[128,1024]{1,0:T(8,128)(2,1)S(1)}, bf16[128,1024]{1,0:T(8,128)(2,1)S(1)}, bf16[128,1024]{1,0:T(8,128)(2,1)S(1)}) fusion(bf16[128,2048]{1,0:T(8,128)(2,1)} %own_ref.7, s32[]{:T(128)S(6)} %select_n.28, s32[]{:T(128)S(6)} %select_n.27, s32[]{:T(128)S(6)} %select_n.26), kind=kLoop, calls=%fused_computation | loop fusion | bytes 1572876 | tf_op jit(solution)/shard_map/dynamic_slice | solution.py:306
  1.9 0.0 copy-start.2
  1.9 0.7 collective-permute-start
  2.6 0.0 copy-start.1
  2.6 0.7 collective-permute-start.1
  3.3 0.0 copy-done.2
  3.3 0.1 copy.5.offsets_ref
  3.4 0.0 collective-permute-done.other_ref
  3.4 0.0 copy-done
  3.4 0.0 copy-done.1
  3.4 2.4 %chain1.1 = f32[4,128]{1,0:T(4,128)S(1)} custom-call(s32[4,2]{1,0:T(4,128)S(1)} %copy.5.offsets_ref, bf16[128,2048]{1,0:T(8,128)(2,1)S(1)} %copy-done, bf16[128,1024]{1,0:T(8,128)(2,1)S(1)} %collective-permute-done.other_ref, s32[1,16]{1,0:T(1,128)S(1)} %copy-done.1), custom_call_target="tpu_custom_call" | custom-call | tf_op jit(solution)/shard_map/chain1/pallas_call | solution.py:320
  5.8 10.3 %collective-permute-start.2 = (bf16[128,1024]{1,0:T(8,128)(2,1)S(1)}, bf16[128,1024]{1,0:T(8,128)(2,1)S(1)}, u32[]{:S(2)}, u32[]{:S(2)}) collective-permute-start(bf16[128,1024]{1,0:T(8,128)(2,1)S(1)} %get-tuple-element.3), channel_id=1, source_target_pairs={{10,14},{11,15},{12,0},{13,1},{14,10},{15,11},{0,12},{1,13},{26,30... | collective-permute-start | bytes 786440 | tf_op jit(solution)/shard_map/ppermute | solution.py:303
  16.1 32.1 %psum.21.refs_0_ = f32[4,128]{1,0:T(4,128)S(1)} all-reduce(f32[4,128]{1,0:T(4,128)S(1)} %chain1.1), channel_id=1, replica_groups=mesh['parts'=2,'tile'=16] {'tile'}, use_global_device_ids=true, to_apply=%region_0.1 | all-reduce | flops 512 | bytes 4096 | tf_op jit(solution)/shard_map/psum | solution.py:337
  48.2 0.0 collective-permute-done.1.other_ref
  48.2 4.6 %chain2.1 = f32[4,128]{1,0:T(4,128)S(1)} custom-call(s32[4,2]{1,0:T(4,128)S(1)} %copy.5.offsets_ref, bf16[128,2048]{1,0:T(8,128)(2,1)S(1)} %copy-done, bf16[128,1024]{1,0:T(8,128)(2,1)S(1)} %collective-permute-done.1.other_ref, s32[1,16]{1,0:T(1,128)S(1)} %copy-done.1, f32[4,128]{1,0:T(4,128)S(1)} %psum.21.refs_0_), custom_call_target="tpu_custom_call" | custom-call | tf_op jit(solution)/shard_map/chain2/pallas_call | solution.py:320
  52.8 29.5 %psum.22.refs_0_.refs_1_ = f32[4,128]{1,0:T(4,128)S(1)} all-reduce(f32[4,128]{1,0:T(4,128)S(1)} %chain2.1), channel_id=1, replica_groups=mesh['parts'=2,'tile'=16] {'tile'}, use_global_device_ids=true, to_apply=%region_1.2 | all-reduce | flops 512 | bytes 4096 | tf_op jit(solution)/shard_map/psum | solution.py:337
  82.3 0.0 collective-permute-done.2.other_ref
  82.3 4.6 %chain3.1 = f32[4,128]{1,0:T(4,128)S(1)} custom-call(s32[4,2]{1,0:T(4,128)S(1)} %copy.5.offsets_ref, bf16[128,2048]{1,0:T(8,128)(2,1)S(1)} %copy-done, bf16[128,1024]{1,0:T(8,128)(2,1)S(1)} %collective-permute-done.2.other_ref, s32[1,16]{1,0:T(1,128)S(1)} %copy-done.1, f32[4,128]{1,0:T(4,128)S(1)} %psum.22.refs_0_.refs_1_), custom_call_target="tpu_custom_call" | custom-call | tf_op jit(solution)/shard_map/chain3/pallas_call | solution.py:320
  86.9 29.5 %psum.23.refs_2_ = f32[4,128]{1,0:T(4,128)S(1)} all-reduce(f32[4,128]{1,0:T(4,128)S(1)} %chain3.1), channel_id=1, replica_groups=mesh['parts'=2,'tile'=16] {'tile'}, use_global_device_ids=true, to_apply=%region_2.3 | all-reduce | flops 512 | bytes 4096 | tf_op jit(solution)/shard_map/psum | solution.py:337
  116.4 4.9 %home.1 = (bf16[128,2048]{1,0:T(8,128)(2,1)}, f32[2,1,16]{2,1,0:T(1,128)}) custom-call(bf16[128,2048]{1,0:T(8,128)(2,1)S(1)} %copy-done, f32[4,128]{1,0:T(4,128)S(1)} %psum.21.refs_0_, f32[4,128]{1,0:T(4,128)S(1)} %psum.22.refs_0_.refs_1_, f32[4,128]{1,0:T(4,128)S(1)} %psum.23.refs_2_), custom_call_target="tpu_custom_call" | custom-call | tf_op jit(solution)/shard_map/home/pallas_call | solution.py:340
Async XLA Ops:
  0.7 2.7 %copy-start = (bf16[128,2048]{1,0:T(8,128)(2,1)S(1)}, bf16[128,2048]{1,0:T(8,128)(2,1)}, u32[]{:S(2)}) copy-start(bf16[128,2048]{1,0:T(8,128)(2,1)} %own_ref.7) | copy-start | bytes 1572868
  1.9 1.4 %copy-start.2 = (s32[4,2]{0,1:T(2,128)S(1)}, s32[4,2]{0,1:T(2,128)}, u32[]{:S(2)}) copy-start(s32[4,2]{0,1:T(2,128)} %param.5) | copy-start | bytes 100
  1.9 1.5 %collective-permute-start = (bf16[128,1024]{1,0:T(8,128)(2,1)S(1)}, bf16[128,1024]{1,0:T(8,128)(2,1)S(1)}, u32[]{:S(2)}, u32[]{:S(2)}) collective-permute-start(bf16[128,1024]{1,0:T(8,128)(2,1)S(1)} %get-tuple-element.6), channel_id=1, source_target_pairs={{2,6},{3,7},{4,8},{5,9},{6,2},{7,3},{8,4},{9,5},{18,22},{19,23},{2... | collective-permute-start | bytes 786440 | tf_op jit(solution)/shard_map/ppermute | solution.py:303
  2.6 0.8 copy-start.1
  2.6 45.6 %collective-permute-start.1 = (bf16[128,1024]{1,0:T(8,128)(2,1)S(1)}, bf16[128,1024]{1,0:T(8,128)(2,1)S(1)}, u32[]{:S(2)}, u32[]{:S(2)}) collective-permute-start(bf16[128,1024]{1,0:T(8,128)(2,1)S(1)} %get-tuple-element.5), channel_id=1, source_target_pairs={{6,10},{7,11},{8,12},{9,13},{10,6},{11,7},{12,8},{13,9},{22,26},{2... | collective-permute-start | bytes 786440 | tf_op jit(solution)/shard_map/ppermute | solution.py:303
  5.8 76.5 %collective-permute-start.2 = (bf16[128,1024]{1,0:T(8,128)(2,1)S(1)}, bf16[128,1024]{1,0:T(8,128)(2,1)S(1)}, u32[]{:S(2)}, u32[]{:S(2)}) collective-permute-start(bf16[128,1024]{1,0:T(8,128)(2,1)S(1)} %get-tuple-element.3), channel_id=1, source_target_pairs={{10,14},{11,15},{12,0},{13,1},{14,10},{15,11},{0,12},{1,13},{26,30... | collective-permute-start | bytes 786440 | tf_op jit(solution)/shard_map/ppermute | solution.py:303

commit v4 on v3

--- a/solution.py
+++ b/solution.py
@@ -16,6 +16,8 @@
 WIDTH = 2 * HALF + 1
 MASK_LANE = 64
 GROUP = 4
+THIRD = WIDTH // 3
+SPAN = PATCH // 2 + 16
 
 sharpness = 12.0
 anchor_weight = 2.0
@@ -71,12 +73,17 @@
     return (1 - 2 * ((iota(shape, 0) + iota(shape, 1)) % 2)).astype(f32)
 
 
-def padded_rows(grid):
-    return jnp.concatenate([grid, jnp.zeros((8 - grid.shape[0] % 8, LANES), f32)], axis=0)
+def section_grid(gathered, step, rows):
+    count = gathered.shape[0]
+    out = None
+    for group in (step - 1, step):
+        start = (group * rows + rows // 2) % count
+        part = jnp.concatenate([gathered[start:], gathered[:start]], axis=0)[:rows]
+        out = part if out is None else out + part
+    return jnp.concatenate([out, jnp.zeros((8 - rows % 8, LANES), f32)], axis=0)
 
 
 def relax(grid, rows, nodes):
-    grid = padded_rows(grid)
     shape = grid.shape
     row, lane = iota(shape, 0), iota(shape, 1)
     col = lane % nodes
@@ -121,9 +128,7 @@
 
 
 def circulant(row):
-    first = pltpu.roll(jnp.broadcast_to(row, (8, LANES)), 0, 1, stride=1, stride_axis=0)
-    later = [pltpu.roll(first, r, 1) for r in range(8, PATCH, 8)]
-    return jnp.concatenate([first] + later, axis=0)
+    return pltpu.roll(jnp.broadcast_to(row, (PATCH, LANES)), 0, 1, stride=1, stride_axis=0)
 
 
 def warp(patch, row_base, col_base, row_swing, col_swing, nyquist):
@@ -133,45 +138,63 @@
         jnp.concatenate([patch, patch], axis=1), jnp.concatenate([col_high, col_low], axis=0)
     )
     in_high, in_low = split(inner)
+    upper = jnp.concatenate([in_high, in_low], axis=1)
+    lower = jnp.concatenate([in_high, jnp.zeros_like(in_low)], axis=1)
     out = dot(
-        jnp.concatenate([row_high, row_low], axis=1), jnp.concatenate([in_high, in_high], axis=0)
-    ) + dot(row_high, in_low)
+        jnp.concatenate([row_high, row_low], axis=1), jnp.concatenate([upper, lower], axis=0)
+    )
+    out = out[:, :LANES] + out[:, LANES:]
     factor = row_swing * col_swing * nyquist * (1.0 / (PATCH * PATCH))
     return out - factor * sign_tile((PATCH, LANES))
 
 
-def correlate(own, prev, base, column_offset, band_ref):
-    half, edge, third = PATCH // 2, 16, 3
+def lag_layout(shape, axis):
+    spot = (iota(shape, axis) + 16) % (2 * LANES)
+    return spot // SPAN, 8 - spot % SPAN
+
+
+def correlate(own, prev, level, column_offset, band_ref):
     own32, prev32 = own.astype(f32), prev.astype(f32)
-    left = []
-    for i in range(third):
+    half = PATCH // 2
+    left, right = [], []
+    for i in range(THIRD):
         amount = (PATCH + HALF - i - column_offset) % PATCH
-        turned = pltpu.roll(own32, amount, 1).astype(bf16)
-        left.append(jnp.concatenate([turned[:half], turned[half:]], axis=1))
-    right = []
-    for j in range(third):
-        turned = pltpu.roll(prev32, third * j, 1).astype(bf16) if j else prev
-        low = jnp.concatenate([turned[PATCH - edge :], turned[: PATCH - edge]], axis=0)
-        high = jnp.concatenate([turned[half - edge :], turned[: half - edge]], axis=0)
-        right.append(jnp.concatenate([low, high], axis=1))
+        turned = pltpu.roll(own32, amount, 1)
+        low = jnp.concatenate([turned[PATCH - 8 :], turned[: half + 8]], axis=0)
+        high = jnp.concatenate([turned[half - 8 :], turned[:8]], axis=0)
+        left.append(jnp.concatenate([low, high], axis=1).astype(bf16))
+    for j in range(THIRD):
+        turned = pltpu.roll(prev32, THIRD * j, 1).astype(bf16) if j else prev
+        right.append(jnp.concatenate([turned[:half], turned[half:]], axis=1))
+        right.append(jnp.zeros((SPAN - half, 2 * LANES), bf16))
+    right.append(jnp.zeros((2 * LANES - THIRD * SPAN, 2 * LANES), bf16))
     product = dot_t(jnp.concatenate(left, axis=0), jnp.concatenate(right, axis=0))
-    lane = iota((8, LANES), 1)
-    for j in range(third):
-        for i in range(third):
-            block = product[i * half : (i + 1) * half, j * LANES : (j + 1) * LANES]
-            band = None
-            for k in range(4):
-                later = (lane >= 8 * k + 32) & (lane < 8 * k + 64)
-                kept = jnp.where(later, block[8 * k + 32 : 8 * k + 40], block[8 * k : 8 * k + 8])
-                kept = pltpu.roll(kept, LANES - 8 * k, 1) if k else kept
-                band = kept if band is None else band + kept
-            band_ref[8 * (i + third * j) : 8 * (i + third * j) + 8, :] = band - base
+    spot = iota((8, 2 * LANES), 1) % SPAN
+    base = jnp.where((spot < half) & (iota((8, 2 * LANES), 1) < THIRD * SPAN), level * (2.0 * LANES), 0.0)
+    unused = lag_layout(spot.shape, 1)[1] >= 8 - iota(spot.shape, 0)
+    for i in range(THIRD):
+        tile = lambda r: product[i * SPAN + 8 * r : i * SPAN + 8 * r + 8]
+        band = None
+        for k in range(3):
+            kept = tile(k)
+            for m in range(1, 4 if k == 0 else 3):
+                kept = jnp.where(spot >= 8 * k + 24 * m - 16, tile(k + 3 * m), kept)
+            kept = kept - base
+            kept = pltpu.roll(kept, 2 * LANES - 8 * k, 1) if k else kept
+            band = kept if band is None else band + kept
+        band = jnp.where(unused, 0.0, band)
+        for side in range(2):
+            band_ref[side, 8 * i : 8 * i + 8, :] = band[:, side * LANES : (side + 1) * LANES]
     out = None
     for row in range(8):
-        part = band_ref[pl.ds(row, WIDTH, stride=8), :]
-        part = pltpu.roll(part, LANES - row, 1) if row else part
+        part = jnp.concatenate(
+            [band_ref[side, pl.ds(row, THIRD, stride=8), :] for side in range(2)], axis=1
+        )
+        part = pltpu.roll(part, 2 * LANES - row, 1) if row else part
         out = part if out is None else out + part
-    return out + pltpu.roll(out, LANES - 32, 1)
+    back = lambda lanes: pltpu.roll(out, 2 * LANES - lanes, 1)
+    _, row_lag = lag_layout(out.shape, 1)
+    return out + back(24) + back(48) + jnp.where(row_lag > 0, back(72), 0.0)
 
 
 def moments(values, corner):
@@ -216,7 +239,7 @@
     area = float(PATCH * PATCH)
 
     if step > 1:
-        row_shift = own_row(relax(refs[0][...], rows, nodes), row_index)
+        row_shift = own_row(relax(section_grid(refs[0][...], step - 1, rows), rows, nodes), row_index)
         base_ref[...], swing_ref[...] = kernels_of(row_shift, first, cols, nodes)
 
         def warp_one(index):
@@ -235,8 +258,8 @@
         sums = moments(own, own_corner) + moments(prev, prev_corner)
         for k, value in enumerate(sums):
             sums_ref[k, pl.ds(index, 1)] = value[None]
-        base = own_corner * prev_corner * (8.0 * LANES)
-        score_ref[pl.ds(index, 1)] = correlate(own, prev, base, col_offset, band_ref.at[index])[None]
+        level = own_corner * prev_corner
+        score_ref[pl.ds(index, 1)] = correlate(own, prev, level, col_offset, band_ref.at[index])[None]
 
     looped(cols, one)
     reduce = lambda value: jnp.sum(jnp.sum(value, axis=1), axis=1, keepdims=True)
@@ -247,15 +270,17 @@
     )
     scale = sharpness / area / spread
     level = corner_ref[0] * prev_sum + corner_ref[1] * own_sum + own_sum * prev_sum
-    shape = (cols, WIDTH, LANES)
-    line, lane = iota(shape, 1), iota(shape, 2)
-    row_step = 16 - lane - row_offset
-    inside = (row_step >= -HALF) & (row_step <= HALF)
-    score = (score_ref[...] - (level * area)[:, None, :]) * jnp.broadcast_to(scale, (cols, LANES))[:, None, :]
+    shape = (cols, THIRD, 2 * LANES)
+    third, row_lag = lag_layout(shape, 2)
+    col_lag = iota(shape, 1) + THIRD * third - HALF + col_offset
+    inside = (jnp.abs(row_lag - row_offset) <= HALF) & (third < THIRD)
+    level = jnp.concatenate([level, level], axis=1) * area
+    scale = jnp.broadcast_to(scale, (cols, 2 * LANES))
+    score = (score_ref[...] - level[:, None, :]) * scale[:, None, :]
     weights = jnp.where(inside, jnp.exp(jnp.where(inside, score, 0.0)), 0.0)
     inverse = 1.0 / reduce(weights)
-    flow_row = reduce(weights * (row_step + row_offset).astype(f32)) * inverse
-    flow_col = reduce(weights * (line - HALF + col_offset).astype(f32)) * inverse
+    flow_row = reduce(weights * row_lag.astype(f32)) * inverse
+    flow_col = reduce(weights * col_lag.astype(f32)) * inverse
     shape = (cols, LANES)
     node, lane = iota(shape, 0) + first, iota(shape, 1)
     sent = jnp.where(lane == node, flow_row, jnp.where(lane == node + nodes, flow_col, 0.0))
@@ -266,8 +291,7 @@
         axis=1,
     )
     sent = sent + jnp.where(is_upper, masks, 0.0)
-    sends = (iota(out_ref.shape, 0) == row_index) & (is_upper | (group == step - 1))
-    out_ref[...] = jnp.where(sends, sent, 0.0)
+    out_ref[...] = jnp.broadcast_to(sent, out_ref.shape)
 
 
 def home_kernel(rows, nodes, own_ref, *refs):
@@ -277,7 +301,7 @@
     group, row_index = rotated // rows, rotated % rows
     grid = None
     for step in range(1, SECTIONS):
-        part = refs[step - 1][...]
+        part = section_grid(refs[step - 1][...], step, rows)
         grid = part if grid is None else jnp.where(group == step, part, grid)
     row_shift = own_row(relax(grid, rows, nodes), row_index)
     row_shift = jnp.where(group == 0, 0.0, row_shift)
@@ -319,12 +343,12 @@
         extra = gathered[-1:]
         sent = pl.pallas_call(
             functools.partial(chain_kernel, step, rows, nodes),
-            out_shape=jax.ShapeDtypeStruct((rows, LANES), f32),
+            out_shape=jax.ShapeDtypeStruct((count, LANES), f32),
             in_specs=[smem] + [vmem] * (3 + len(extra)),
             out_specs=vmem,
             scratch_shapes=[
-                pltpu.VMEM((cols, WIDTH, LANES), f32),
-                pltpu.VMEM((cols, 8 * WIDTH, LANES), f32),
+                pltpu.VMEM((cols, THIRD, 2 * LANES), f32),
+                pltpu.VMEM((cols, 2, 8 * THIRD, LANES), f32),
                 pltpu.VMEM((4, cols, 8, LANES), f32),
                 pltpu.VMEM((2, cols, LANES), f32),
                 pltpu.VMEM((cols, PATCH, PATCH), bf16),
@@ -334,7 +358,7 @@
             compiler_params=params,
             name=f"chain{step}",
         )(coarse_offsets, sections, others[step - 1], valid_mask, *extra)
-        gathered.append(lax.psum(sent, "tile"))
+        gathered.append(lax.all_to_all(sent, "tile", 0, 0, tiled=True))
         if step + 1 < SECTIONS - 1:
             others.append(swapped(step + 1, sent))
     return pl.pallas_call(

time: 122 us -> 55.9 us (0.46)
  blocking collectives: 91.1 us -> 18 us
  waiting for transfers between devices: 0.01 us -> 6.33 us
  starting transfers between devices: 11.7 us -> 15.9 us
  Pallas kernels: 16.5 us -> 13.3 us
    psum x3 -> x0, blocking collectives: 91.1 us -> none  [shards(): gathered.append(lax.psum(sent, 'tile'))]
    all_to_all x0 -> x2, blocking collectives: none -> 18 us  [shards(): gathered.append(lax.all_to_all(sent, 'tile', 0, 0, tiled=True))]
    all_to_all x0 -> x1, waiting for transfers between devices: none -> 6.32 us  [shards(): gathered.append(lax.all_to_all(sent, 'tile', 0, 0, tiled=True))]
    all_to_all x0 -> x1, starting transfers between devices: none -> 4.24 us  [shards(): gathered.append(lax.all_to_all(sent, 'tile', 0, 0, tiled=True))]
    pallas_call x1, Pallas kernels: 4.91 us -> 3.27 us  [shards(): pl.pallas_call(functools.partial(home_kernel, rows, nodes), out_shape=(ja...]
    pallas_call x3, Pallas kernels: 11.6 us -> 10 us  [shards(): pl.pallas_call(functools.partial(chain_kernel, step, rows, nodes), out_sh...]
  transfers between devices with their start and end apart: 3 -> 4, of which waited for: 0 -> 1; matrix products, arithmetic and copies ran while one was open for 0% -> 0% of each run, Pallas kernels for 6% -> 12%
where the time goes in v4:
time: 55.9 us; the launch traced here: 55.6 us
  blocking collectives  18 us (32%)
  starting transfers between devices  15.9 us (28%)
  Pallas kernels  13.3 us (24%)
  waiting for transfers between devices  6.33 us (11%)
  local copies, waits for them, and re-layouts  1.33 us (2%)
  between operations  0.76 us (1%)
    all_to_all x2, blocking collectives, shards(): gathered.append(lax.all_to_all(sent, 'tile', 0, 0, tiled=True))  18 us
    ppermute x3, starting transfers between devices, shards(): moved = lambda value, pairs: lax.ppermute(value, 'tile', pairs)  11.7 us
    pallas_call x3, Pallas kernels, shards(): pl.pallas_call(functools.partial(chain_kernel, step, rows, nodes), out_sh...  10 us
    all_to_all x1, waiting for transfers between devices, shards(): gathered.append(lax.all_to_all(sent, 'tile', 0, 0, tiled=True))  6.32 us
    all_to_all x1, starting transfers between devices, shards(): gathered.append(lax.all_to_all(sent, 'tile', 0, 0, tiled=True))  4.24 us
    pallas_call x1, Pallas kernels, shards(): pl.pallas_call(functools.partial(home_kernel, rows, nodes), out_shape=(ja...  3.27 us
    dynamic_slice x1, local copies, waits for them, and re-layouts, swapped(): lax.dynamic_slice_in_dim(sections, jnp.where(group == lower, width, 0), w...  1.22 us
  transfers between devices with their start and end apart: 4, of which 1 were waited for; matrix products, arithmetic and copies ran while one was open for 0% of the time, Pallas kernels for 12%

profile of v4, /device:TPU:0, one launch (start us, length us, event | category | flops | bytes accessed | tf_op | source)
XLA Modules:
  0.0 55.6 jit_solution(7696153629480012552)
XLA Ops:
  0.7 0.0 copy-start
  0.7 1.2 %constant_dynamic-slice_fusion = (bf16[128,1024]{1,0:T(8,128)(2,1)S(1)}, bf16[128,1024]{1,0:T(8,128)(2,1)S(1)}, bf16[128,1024]{1,0:T(8,128)(2,1)S(1)}) fusion(bf16[128,2048]{1,0:T(8,128)(2,1)} %own_ref.7, s32[]{:T(128)S(6)} %select_n.28, s32[]{:T(128)S(6)} %select_n.27, s32[]{:T(128)S(6)} %select_n.26), kind=kLoop, calls=%fused_computation | loop fusion | bytes 1572876 | tf_op jit(solution)/shard_map/dynamic_slice | solution.py:330
  1.9 0.0 copy-start.2
  1.9 0.7 %collective-permute-start = (bf16[128,1024]{1,0:T(8,128)(2,1)S(1)}, bf16[128,1024]{1,0:T(8,128)(2,1)S(1)}, u32[]{:S(2)}, u32[]{:S(2)}) collective-permute-start(bf16[128,1024]{1,0:T(8,128)(2,1)S(1)} %get-tuple-element.6), channel_id=1, source_target_pairs={{2,6},{3,7},{4,8},{5,9},{6,2},{7,3},{8,4},{9,5},{18,22},{19,23},{2... | collective-permute-start | bytes 786440 | tf_op jit(solution)/shard_map/ppermute | solution.py:327
  2.6 0.0 copy-start.1
  2.6 0.7 %collective-permute-start.1 = (bf16[128,1024]{1,0:T(8,128)(2,1)S(1)}, bf16[128,1024]{1,0:T(8,128)(2,1)S(1)}, u32[]{:S(2)}, u32[]{:S(2)}) collective-permute-start(bf16[128,1024]{1,0:T(8,128)(2,1)S(1)} %get-tuple-element.5), channel_id=1, source_target_pairs={{6,10},{7,11},{8,12},{9,13},{10,6},{11,7},{12,8},{13,9},{22,26},{2... | collective-permute-start | bytes 786440 | tf_op jit(solution)/shard_map/ppermute | solution.py:327
  3.3 0.0 copy-done.2
  3.3 0.1 copy.8.offsets_ref
  3.4 0.0 collective-permute-done.other_ref
  3.4 0.0 copy-done
  3.4 0.0 copy-done.1
  3.4 2.8 %chain1.1 = f32[16,128]{1,0:T(8,128)} custom-call(s32[4,2]{1,0:T(4,128)S(1)} %copy.8.offsets_ref, bf16[128,2048]{1,0:T(8,128)(2,1)S(1)} %copy-done, bf16[128,1024]{1,0:T(8,128)(2,1)S(1)} %collective-permute-done.other_ref, s32[1,16]{1,0:T(1,128)S(1)} %copy-done.1), custom_call_target="tpu_custom_call" | custom-call | tf_op jit(solution)/shard_map/chain1/pallas_call | solution.py:344
  6.3 10.3 %collective-permute-start.2 = (bf16[128,1024]{1,0:T(8,128)(2,1)S(1)}, bf16[128,1024]{1,0:T(8,128)(2,1)S(1)}, u32[]{:S(2)}, u32[]{:S(2)}) collective-permute-start(bf16[128,1024]{1,0:T(8,128)(2,1)S(1)} %get-tuple-element.3), channel_id=1, source_target_pairs={{10,14},{11,15},{12,0},{13,1},{14,10},{15,11},{0,12},{1,13},{26,30... | collective-permute-start | bytes 786440 | tf_op jit(solution)/shard_map/ppermute | solution.py:327
  16.6 4.2 %all-to-all-start = ((f32[16,1,128]{2,1,0:T(1,128)}), f32[16,1,128]{2,1,0:T(1,128)S(1)}, u32[]{:S(2)}, u32[]{:S(2)}) async-start(f32[16,1,128]{2,1,0:T(1,128)} %bitcast.1), calls=%async_computation | async-start | bytes 16384 | tf_op jit(solution)/shard_map/all_to_all | solution.py:361
  20.8 0.0 collective-permute-done.1.other_ref
  20.8 6.3 %all-to-all-done = f32[16,1,128]{2,1,0:T(1,128)S(1)} async-done(((f32[16,1,128]{2,1,0:T(1,128)}), f32[16,1,128]{2,1,0:T(1,128)S(1)}, u32[]{:S(2)}, u32[]{:S(2)}) %all-to-all-start) | async-done | bytes 8224 | tf_op jit(solution)/shard_map/all_to_all | solution.py:361
  27.2 3.6 %chain2.1 = f32[16,128]{1,0:T(8,128)S(1)} custom-call(s32[4,2]{1,0:T(4,128)S(1)} %copy.8.offsets_ref, bf16[128,2048]{1,0:T(8,128)(2,1)S(1)} %copy-done, bf16[128,1024]{1,0:T(8,128)(2,1)S(1)} %collective-permute-done.1.other_ref, s32[1,16]{1,0:T(1,128)S(1)} %copy-done.1, f32[16,128]{1,0:T(8,128)S(1)} %bitcast.12), custom_call_target="tpu_custom_call" | custom-call | tf_op jit(solution)/shard_map/chain2/pallas_call | solution.py:344
  30.8 9.0 %all_to_all.33 = f32[16,1,128]{2,1,0:T(1,128)S(1)} all-to-all(f32[16,1,128]{2,1,0:T(1,128)S(1)} %bitcast.18), channel_id=1, replica_groups=mesh['parts'=2,'tile'=16] {'tile'}, dimensions={0} | all-to-all | bytes 16384 | tf_op jit(solution)/shard_map/all_to_all | solution.py:361
  39.7 0.0 collective-permute-done.2.other_ref
  39.7 3.6 %chain3.1 = f32[16,128]{1,0:T(8,128)S(1)} custom-call(s32[4,2]{1,0:T(4,128)S(1)} %copy.8.offsets_ref, bf16[128,2048]{1,0:T(8,128)(2,1)S(1)} %copy-done, bf16[128,1024]{1,0:T(8,128)(2,1)S(1)} %collective-permute-done.2.other_ref, s32[1,16]{1,0:T(1,128)S(1)} %copy-done.1, f32[16,128]{1,0:T(8,128)S(1)} %bitcast.14), custom_call_target="tpu_custom_call" | custom-call | tf_op jit(solution)/shard_map/chain3/pallas_call | solution.py:344
  43.3 9.0 %all_to_all.34 = f32[16,1,128]{2,1,0:T(1,128)S(1)} all-to-all(f32[16,1,128]{2,1,0:T(1,128)S(1)} %bitcast.17), channel_id=1, replica_groups=mesh['parts'=2,'tile'=16] {'tile'}, dimensions={0} | all-to-all | bytes 16384 | tf_op jit(solution)/shard_map/all_to_all | solution.py:361
  52.3 3.3 %home.1 = (bf16[128,2048]{1,0:T(8,128)(2,1)}, f32[2,1,16]{2,1,0:T(1,128)}) custom-call(bf16[128,2048]{1,0:T(8,128)(2,1)S(1)} %copy-done, f32[16,128]{1,0:T(8,128)S(1)} %bitcast.13, f32[16,128]{1,0:T(8,128)S(1)} %bitcast.15, f32[16,128]{1,0:T(8,128)S(1)} %bitcast.16), custom_call_target="tpu_custom_call" | custom-call | tf_op jit(solution)/shard_map/home/pallas_call | solution.py:364
Async XLA Ops:
  0.7 2.7 %copy-start = (bf16[128,2048]{1,0:T(8,128)(2,1)S(1)}, bf16[128,2048]{1,0:T(8,128)(2,1)}, u32[]{:S(2)}) copy-start(bf16[128,2048]{1,0:T(8,128)(2,1)} %own_ref.7) | copy-start | bytes 1572868
  1.9 1.4 %copy-start.2 = (s32[4,2]{0,1:T(2,128)S(1)}, s32[4,2]{0,1:T(2,128)}, u32[]{:S(2)}) copy-start(s32[4,2]{0,1:T(2,128)} %param.5) | copy-start | bytes 100
  1.9 1.5 %collective-permute-start = (bf16[128,1024]{1,0:T(8,128)(2,1)S(1)}, bf16[128,1024]{1,0:T(8,128)(2,1)S(1)}, u32[]{:S(2)}, u32[]{:S(2)}) collective-permute-start(bf16[128,1024]{1,0:T(8,128)(2,1)S(1)} %get-tuple-element.6), channel_id=1, source_target_pairs={{2,6},{3,7},{4,8},{5,9},{6,2},{7,3},{8,4},{9,5},{18,22},{19,23},{2... | collective-permute-start | bytes 786440 | tf_op jit(solution)/shard_map/ppermute | solution.py:327
  2.6 0.8 %copy-start.1 = (s32[1,16]{1,0:T(1,128)S(1)}, s32[1,16]{1,0:T(1,128)}, u32[]{:S(2)}) copy-start(s32[1,16]{1,0:T(1,128)} %mask_ref.5) | copy-start | bytes 196
  2.6 18.2 %collective-permute-start.1 = (bf16[128,1024]{1,0:T(8,128)(2,1)S(1)}, bf16[128,1024]{1,0:T(8,128)(2,1)S(1)}, u32[]{:S(2)}, u32[]{:S(2)}) collective-permute-start(bf16[128,1024]{1,0:T(8,128)(2,1)S(1)} %get-tuple-element.5), channel_id=1, source_target_pairs={{6,10},{7,11},{8,12},{9,13},{10,6},{11,7},{12,8},{13,9},{22,26},{2... | collective-permute-start | bytes 786440 | tf_op jit(solution)/shard_map/ppermute | solution.py:327
  6.3 33.5 %collective-permute-start.2 = (bf16[128,1024]{1,0:T(8,128)(2,1)S(1)}, bf16[128,1024]{1,0:T(8,128)(2,1)S(1)}, u32[]{:S(2)}, u32[]{:S(2)}) collective-permute-start(bf16[128,1024]{1,0:T(8,128)(2,1)S(1)} %get-tuple-element.3), channel_id=1, source_target_pairs={{10,14},{11,15},{12,0},{13,1},{14,10},{15,11},{0,12},{1,13},{26,30... | collective-permute-start | bytes 786440 | tf_op jit(solution)/shard_map/ppermute | solution.py:327
  16.6 10.6 %all-to-all-start = ((f32[16,1,128]{2,1,0:T(1,128)}), f32[16,1,128]{2,1,0:T(1,128)S(1)}, u32[]{:S(2)}, u32[]{:S(2)}) async-start(f32[16,1,128]{2,1,0:T(1,128)} %bitcast.1), calls=%async_computation | async-start | bytes 16384 | tf_op jit(solution)/shard_map/all_to_all | solution.py:361

commit v5 on v4

--- a/solution.py
+++ b/solution.py
@@ -205,7 +205,7 @@
 def looped(count, one):
     def body(turn, carry):
         for k in range(GROUP):
-            one(turn * GROUP + k)
+            one(turn * GROUP + k, k)
         return carry
 
     lax.fori_loop(0, count // GROUP, body, 0)
@@ -227,14 +227,13 @@
     ).astype(bf16)
 
 
-def chain_kernel(step, rows, nodes, offsets_ref, own_ref, other_ref, mask_ref, *refs):
+def chain_kernel(step, rows, nodes, begin, cols, offsets_ref, own_ref, other_ref, mask_ref, *refs):
     out_ref, score_ref, band_ref, sums_ref, corner_ref, prev_ref, base_ref, swing_ref = refs[-8:]
-    cols = nodes // 2
     count = lax.axis_size("tile")
     rotated = (lax.axis_index("tile") + count - rows // 2) % count
     group, row_index = rotated // rows, rotated % rows
     is_upper = group == step
-    first = jnp.where(is_upper, cols, 0)
+    first = begin + jnp.where(is_upper, nodes // 2, 0)
     row_offset, col_offset = offsets_ref[step, 0], offsets_ref[step, 1]
     area = float(PATCH * PATCH)
 
@@ -242,16 +241,19 @@
         row_shift = own_row(relax(section_grid(refs[0][...], step - 1, rows), rows, nodes), row_index)
         base_ref[...], swing_ref[...] = kernels_of(row_shift, first, cols, nodes)
 
-        def warp_one(index):
-            patch = jnp.where(is_upper, other_ref[:, columns(index)], own_ref[:, columns(index)])
+        def warp_one(index, slot):
+            patch = jnp.where(is_upper, other_ref[:, columns(index)], own_ref[:, columns(index + begin)])
             prev_ref[index] = warp_indexed(patch, base_ref, swing_ref, index, cols)
 
         looped(cols, warp_one)
 
-    def one(index):
+    def one(index, slot):
         other = other_ref[:, columns(index)]
-        own = jnp.where(is_upper, own_ref[:, columns(index + cols)], other)
-        prev = prev_ref[index] if step > 1 else jnp.where(is_upper, other, own_ref[:, columns(index)])
+        own = jnp.where(is_upper, own_ref[:, columns(index + begin + nodes // 2)], other)
+        if step > 1:
+            prev = prev_ref[index]
+        else:
+            prev = jnp.where(is_upper, other, own_ref[:, columns(index + begin)])
         own_corner, prev_corner = (x[0:1, 0:1].astype(f32) for x in (own, prev))
         corner_ref[0, pl.ds(index, 1), :] = jnp.broadcast_to(own_corner, (1, LANES))
         corner_ref[1, pl.ds(index, 1), :] = jnp.broadcast_to(prev_corner, (1, LANES))
@@ -259,7 +261,7 @@
         for k, value in enumerate(sums):
             sums_ref[k, pl.ds(index, 1)] = value[None]
         level = own_corner * prev_corner
-        score_ref[pl.ds(index, 1)] = correlate(own, prev, level, col_offset, band_ref.at[index])[None]
+        score_ref[pl.ds(index, 1)] = correlate(own, prev, level, col_offset, band_ref.at[slot])[None]
 
     looped(cols, one)
     reduce = lambda value: jnp.sum(jnp.sum(value, axis=1), axis=1, keepdims=True)
@@ -285,12 +287,15 @@
     node, lane = iota(shape, 0) + first, iota(shape, 1)
     sent = jnp.where(lane == node, flow_row, jnp.where(lane == node + nodes, flow_col, 0.0))
     sent = jnp.sum(sent, axis=0, keepdims=True)
-    masks = mask_ref[...].astype(f32)
-    masks = jnp.concatenate(
-        [jnp.zeros((1, MASK_LANE), f32), masks, masks, jnp.zeros((1, LANES - MASK_LANE - 2 * nodes), f32)],
-        axis=1,
-    )
-    sent = sent + jnp.where(is_upper, masks, 0.0)
+    if begin == 0:
+        masks = mask_ref[...].astype(f32)
+        masks = jnp.concatenate(
+            [jnp.zeros((1, MASK_LANE), f32), masks, masks, jnp.zeros((1, LANES - MASK_LANE - 2 * nodes), f32)],
+            axis=1,
+        )
+        sent = sent + jnp.where(is_upper, masks, 0.0)
+    else:
+        sent = sent + refs[0][0:1, :]
     out_ref[...] = jnp.broadcast_to(sent, out_ref.shape)
 
 
@@ -309,7 +314,7 @@
     shift_ref[1, :, :] = pltpu.roll(row_shift, LANES - nodes, 1)[:, :nodes]
     base_ref[...], swing_ref[...] = kernels_of(row_shift, 0, nodes, nodes)
 
-    def one(index):
+    def one(index, slot):
         here = columns(index)
         out_ref[:, here] = warp_indexed(own_ref[:, here], base_ref, swing_ref, index, nodes)
 
@@ -320,20 +325,29 @@
     count = lax.axis_size("tile")
     rows = count // SECTIONS
     nodes = valid_mask.shape[1]
-    cols = nodes // 2
-    width = cols * PATCH
     place = lambda group, row: (group * rows + row + rows // 2) % count
     group = (lax.axis_index("tile") + count - rows // 2) % count // rows
     moved = lambda value, pairs: lax.ppermute(value, "tile", pairs)
 
-    def swapped(lower, after=None):
-        half = lax.dynamic_slice_in_dim(sections, jnp.where(group == lower, width, 0), width, 1)
+    def swapped(source, lower, begin, cols, after=None):
+        start = (begin + jnp.where(group == lower, nodes // 2, 0)) * PATCH
+        half = lax.dynamic_slice_in_dim(source, start, cols * PATCH, 1)
         if after is not None:
             half, after = lax.optimization_barrier((half, after))
         ends = [(place(lower, i), place(lower + 1, i)) for i in range(rows)]
-        return moved(half, ends + [(d, s) for s, d in ends])
-
-    others = [swapped(0), swapped(1)]
+        idle = [
+            (place(s, i),) * 2 for s in range(SECTIONS) if s not in (lower, lower + 1) for i in range(rows)
+        ]
+        return half, moved(half, ends + [(d, s) for s, d in ends] + idle)
+
+    half = nodes // 2
+    chunk = half // 2
+    head, first_chunk = swapped(sections, 0, 0, chunk)
+    source, head = lax.optimization_barrier((sections, head))
+    others = {
+        1: [(0, chunk, first_chunk), (chunk, chunk, swapped(source, 0, chunk, chunk)[1])],
+        2: [(0, half, swapped(source, 1, 0, half)[1])],
+    }
 
     vmem = pl.BlockSpec(memory_space=pltpu.VMEM)
     smem = pl.BlockSpec(memory_space=pltpu.SMEM)
@@ -341,26 +355,28 @@
     gathered = []
     for step in range(1, SECTIONS):
         extra = gathered[-1:]
-        sent = pl.pallas_call(
-            functools.partial(chain_kernel, step, rows, nodes),
-            out_shape=jax.ShapeDtypeStruct((count, LANES), f32),
-            in_specs=[smem] + [vmem] * (3 + len(extra)),
-            out_specs=vmem,
-            scratch_shapes=[
-                pltpu.VMEM((cols, THIRD, 2 * LANES), f32),
-                pltpu.VMEM((cols, 2, 8 * THIRD, LANES), f32),
-                pltpu.VMEM((4, cols, 8, LANES), f32),
-                pltpu.VMEM((2, cols, LANES), f32),
-                pltpu.VMEM((cols, PATCH, PATCH), bf16),
-                pltpu.VMEM((2 * cols, LANES), f32),
-                pltpu.VMEM((2 * cols, LANES), f32),
-            ],
-            compiler_params=params,
-            name=f"chain{step}",
-        )(coarse_offsets, sections, others[step - 1], valid_mask, *extra)
+        for begin, cols, other in others[step]:
+            sent = pl.pallas_call(
+                functools.partial(chain_kernel, step, rows, nodes, begin, cols),
+                out_shape=jax.ShapeDtypeStruct((count, LANES), f32),
+                in_specs=[smem] + [vmem] * (3 + len(extra)),
+                out_specs=vmem,
+                scratch_shapes=[
+                    pltpu.VMEM((cols, THIRD, 2 * LANES), f32),
+                    pltpu.VMEM((GROUP, 2, 8 * THIRD, LANES), f32),
+                    pltpu.VMEM((4, cols, 8, LANES), f32),
+                    pltpu.VMEM((2, cols, LANES), f32),
+                    pltpu.VMEM((cols, PATCH, PATCH), bf16),
+                    pltpu.VMEM((2 * cols, LANES), f32),
+                    pltpu.VMEM((2 * cols, LANES), f32),
+                ],
+                compiler_params=params,
+                name=f"chain{step}_{begin}",
+            )(coarse_offsets, sections, other, valid_mask, *extra)
+            extra = [sent]
         gathered.append(lax.all_to_all(sent, "tile", 0, 0, tiled=True))
         if step + 1 < SECTIONS - 1:
-            others.append(swapped(step + 1, sent))
+            others[step + 2] = [(0, half, swapped(source, step + 1, 0, half, sent)[1])]
     return pl.pallas_call(
         functools.partial(home_kernel, rows, nodes),
         out_shape=(

time: 55.9 us -> 58.5 us (1.047)
  blocking collectives: 18 us -> 27 us
  waiting for transfers between devices: 6.33 us -> 0.01 us
  local copies, waits for them, and re-layouts: 1.33 us -> 2.04 us
  starting transfers between devices: 15.9 us -> 15.2 us
    all_to_all x2 -> x3, blocking collectives: 18 us -> 27 us  [shards(): gathered.append(lax.all_to_all(sent, 'tile', 0, 0, tiled=True))]
    all_to_all x1 -> x0, waiting for transfers between devices: 6.32 us -> none  [shards(): gathered.append(lax.all_to_all(sent, 'tile', 0, 0, tiled=True))]
    all_to_all x1 -> x0, starting transfers between devices: 4.24 us -> none  [shards(): gathered.append(lax.all_to_all(sent, 'tile', 0, 0, tiled=True))]
    ppermute x3 -> x4, starting transfers between devices: 11.7 us -> 15.2 us  [shards(): moved = lambda value, pairs: lax.ppermute(value, 'tile', pairs)]
    dynamic_slice x1 -> x3, local copies, waits for them, and re-layouts: 1.22 us -> 1.93 us  [swapped(): half = lax.dynamic_slice_in_dim(source, start, cols * PATCH, 1)]
    pallas_call x3 -> x4, Pallas kernels: 10 us -> 9.95 us  [shards(): pl.pallas_call(functools.partial(chain_kernel, step, rows, nodes, begin,...]
  transfers between devices with their start and end apart: 4 -> 4, of which waited for: 1 -> 0; matrix products, arithmetic and copies ran while one was open for 0% -> 2% of each run, Pallas kernels for 12% -> 11%
where the time goes in v5:
time: 58.5 us; the launch traced here: 58.2 us
  blocking collectives  27 us (46%)
  starting transfers between devices  15.2 us (26%)
  Pallas kernels  13.2 us (23%)
  local copies, waits for them, and re-layouts  2.04 us (3%)
  between operations  0.8 us (1%)
    all_to_all x3, blocking collectives, shards(): gathered.append(lax.all_to_all(sent, 'tile', 0, 0, tiled=True))  27 us
    ppermute x4, starting transfers between devices, shards(): moved = lambda value, pairs: lax.ppermute(value, 'tile', pairs)  15.2 us
    pallas_call x4, Pallas kernels, shards(): pl.pallas_call(functools.partial(chain_kernel, step, rows, nodes, begin,...  9.95 us
    pallas_call x1, Pallas kernels, shards(): pl.pallas_call(functools.partial(home_kernel, rows, nodes), out_shape=(ja...  3.27 us
    dynamic_slice x3, local copies, waits for them, and re-layouts, swapped(): half = lax.dynamic_slice_in_dim(source, start, cols * PATCH, 1)  1.93 us
  transfers between devices with their start and end apart: 4, of which 0 were waited for; matrix products, arithmetic and copies ran while one was open for 2% of the time, Pallas kernels for 11%

profile of v5, /device:TPU:0, one launch (start us, length us, event | category | flops | bytes accessed | tf_op | source)
XLA Modules:
  0.0 58.2 jit_solution(12408997227136639819)
XLA Ops:
  0.6 0.0 copy-start
  0.7 1.0 %constant_dynamic-slice_fusion.3 = bf16[128,512]{1,0:T(8,128)(2,1)S(1)} fusion(bf16[128,2048]{1,0:T(8,128)(2,1)} %own_ref.9, s32[]{:T(128)S(6)} %select_n.37), kind=kLoop, calls=%fused_computation.3 | loop fusion | bytes 262148 | tf_op jit(solution)/shard_map/dynamic_slice | solution.py:334
  1.6 0.7 %collective-permute-start.1 = (bf16[128,512]{1,0:T(8,128)(2,1)S(1)}, bf16[128,512]{1,0:T(8,128)(2,1)S(1)}, u32[]{:S(2)}, u32[]{:S(2)}) collective-permute-start(bf16[128,512]{1,0:T(8,128)(2,1)S(1)} %constant_dynamic-slice_fusion.3), channel_id=1, source_target_pairs={{2,6},{3,7},{4,8},{5,9},{6,2},{7,3},{8,4},{9,5},{10,10},{11,11},{1... | collective-permute-start | bytes 393224 | tf_op jit(solution)/shard_map/ppermute | solution.py:330
  2.3 0.9 %constant_dynamic-slice_fusion.2 = bf16[128,512]{1,0:T(8,128)(2,1)S(1)} fusion(bf16[128,2048]{1,0:T(8,128)(2,1)} %own_ref.9, s32[]{:T(128)S(6)} %select_n.38), kind=kLoop, calls=%fused_computation.2 | loop fusion | bytes 262148 | tf_op jit(solution)/shard_map/dynamic_slice | solution.py:334
  3.3 0.7 %collective-permute-start = (bf16[128,512]{1,0:T(8,128)(2,1)S(1)}, bf16[128,512]{1,0:T(8,128)(2,1)S(1)}, u32[]{:S(2)}, u32[]{:S(2)}) collective-permute-start(bf16[128,512]{1,0:T(8,128)(2,1)S(1)} %constant_dynamic-slice_fusion.2), channel_id=1, source_target_pairs={{2,6},{3,7},{4,8},{5,9},{6,2},{7,3},{8,4},{9,5},{10,10},{11,11},{1... | collective-permute-start | bytes 393224 | tf_op jit(solution)/shard_map/ppermute | solution.py:330
  3.9 0.0 copy-done
  4.0 0.0 copy-start.2
  4.0 0.0 copy-start.1
  4.0 0.7 %collective-permute-start.2 = (bf16[128,1024]{1,0:T(8,128)(2,1)S(1)}, bf16[128,1024]{1,0:T(8,128)(2,1)S(1)}, u32[]{:S(2)}, u32[]{:S(2)}) collective-permute-start(bf16[128,1024]{1,0:T(8,128)(2,1)S(1)} %get-tuple-element.7), channel_id=1, source_target_pairs={{6,10},{7,11},{8,12},{9,13},{10,6},{11,7},{12,8},{13,9},{2,2},{3,3... | collective-permute-start | bytes 786440 | tf_op jit(solution)/shard_map/ppermute | solution.py:330
  4.7 0.0 copy-done.2
  4.7 0.1 copy.10.offsets_ref
  4.8 0.0 collective-permute-done.1.other_ref
  4.8 0.0 copy-done.1
  4.8 1.4 %chain1_0.1.refs_0_ = f32[16,128]{1,0:T(8,128)S(1)} custom-call(s32[4,2]{1,0:T(4,128)S(1)} %copy.10.offsets_ref, bf16[128,2048]{1,0:T(8,128)(2,1)S(1)} %copy-done, bf16[128,512]{1,0:T(8,128)(2,1)S(1)} %collective-permute-done.1.other_ref, s32[1,16]{1,0:T(1,128)S(1)} %copy-done.1), custom_call_target="tpu_custom_call" | custom-call | tf_op jit(solution)/shard_map/chain1_0/pallas_call | solution.py:359
  6.2 0.0 collective-permute-done.other_ref
  6.2 1.4 %chain1_4.1 = f32[16,128]{1,0:T(8,128)S(1)} custom-call(s32[4,2]{1,0:T(4,128)S(1)} %copy.10.offsets_ref, bf16[128,2048]{1,0:T(8,128)(2,1)S(1)} %copy-done, bf16[128,512]{1,0:T(8,128)(2,1)S(1)} %collective-permute-done.other_ref, s32[1,16]{1,0:T(1,128)S(1)} %copy-done.1, f32[16,128]{1,0:T(8,128)S(1)} %chain1_0.1.refs_0_), custom_call_target="tpu_custom_call" | custom-call | tf_op jit(solution)/shard_map/chain1_4/pallas_call | solution.py:359
  7.6 13.1 %collective-permute-start.3 = (bf16[128,1024]{1,0:T(8,128)(2,1)S(1)}, bf16[128,1024]{1,0:T(8,128)(2,1)S(1)}, u32[]{:S(2)}, u32[]{:S(2)}) collective-permute-start(bf16[128,1024]{1,0:T(8,128)(2,1)S(1)} %get-tuple-element.5), channel_id=1, source_target_pairs={{10,14},{11,15},{12,0},{13,1},{14,10},{15,11},{0,12},{1,13},{2,2},... | collective-permute-start | bytes 786440 | tf_op jit(solution)/shard_map/ppermute | solution.py:330
  20.7 9.0 %all_to_all.33 = f32[16,1,128]{2,1,0:T(1,128)S(1)} all-to-all(f32[16,1,128]{2,1,0:T(1,128)S(1)} %bitcast.16), channel_id=1, replica_groups=mesh['parts'=2,'tile'=16] {'tile'}, dimensions={0} | all-to-all | bytes 16384 | tf_op jit(solution)/shard_map/all_to_all | solution.py:377
  29.7 0.0 collective-permute-done.2.other_ref
  29.7 3.6 %chain2_0.1 = f32[16,128]{1,0:T(8,128)S(1)} custom-call(s32[4,2]{1,0:T(4,128)S(1)} %copy.10.offsets_ref, bf16[128,2048]{1,0:T(8,128)(2,1)S(1)} %copy-done, bf16[128,1024]{1,0:T(8,128)(2,1)S(1)} %collective-permute-done.2.other_ref, s32[1,16]{1,0:T(1,128)S(1)} %copy-done.1, f32[16,128]{1,0:T(8,128)S(1)} %bitcast.12), custom_call_target="tpu_custom_call" | custom-call | tf_op jit(solution)/shard_map/chain2_0/pallas_call | solution.py:359
  33.3 9.0 %all_to_all.34 = f32[16,1,128]{2,1,0:T(1,128)S(1)} all-to-all(f32[16,1,128]{2,1,0:T(1,128)S(1)} %bitcast.19), channel_id=1, replica_groups=mesh['parts'=2,'tile'=16] {'tile'}, dimensions={0} | all-to-all | bytes 16384 | tf_op jit(solution)/shard_map/all_to_all | solution.py:377
  42.3 0.0 collective-permute-done.3.other_ref
  42.3 3.6 %chain3_0.1 = f32[16,128]{1,0:T(8,128)S(1)} custom-call(s32[4,2]{1,0:T(4,128)S(1)} %copy.10.offsets_ref, bf16[128,2048]{1,0:T(8,128)(2,1)S(1)} %copy-done, bf16[128,1024]{1,0:T(8,128)(2,1)S(1)} %collective-permute-done.3.other_ref, s32[1,16]{1,0:T(1,128)S(1)} %copy-done.1, f32[16,128]{1,0:T(8,128)S(1)} %bitcast.14), custom_call_target="tpu_custom_call" | custom-call | tf_op jit(solution)/shard_map/chain3_0/pallas_call | solution.py:359
  45.9 9.0 %all_to_all.35 = f32[16,1,128]{2,1,0:T(1,128)S(1)} all-to-all(f32[16,1,128]{2,1,0:T(1,128)S(1)} %bitcast.18), channel_id=1, replica_groups=mesh['parts'=2,'tile'=16] {'tile'}, dimensions={0} | all-to-all | bytes 16384 | tf_op jit(solution)/shard_map/all_to_all | solution.py:377
  54.9 3.3 %home.1 = (bf16[128,2048]{1,0:T(8,128)(2,1)}, f32[2,1,16]{2,1,0:T(1,128)}) custom-call(bf16[128,2048]{1,0:T(8,128)(2,1)S(1)} %copy-done, f32[16,128]{1,0:T(8,128)S(1)} %bitcast.13, f32[16,128]{1,0:T(8,128)S(1)} %bitcast.15, f32[16,128]{1,0:T(8,128)S(1)} %bitcast.17), custom_call_target="tpu_custom_call" | custom-call | tf_op jit(solution)/shard_map/home/pallas_call | solution.py:380
  (1 shorter events, 0.0 us)
Async XLA Ops:
  0.6 3.3 %copy-start = (bf16[128,2048]{1,0:T(8,128)(2,1)S(1)}, bf16[128,2048]{1,0:T(8,128)(2,1)}, u32[]{:S(2)}) copy-start(bf16[128,2048]{1,0:T(8,128)(2,1)} %own_ref.9) | copy-start | bytes 1572868
  1.6 3.2 %collective-permute-start.1 = (bf16[128,512]{1,0:T(8,128)(2,1)S(1)}, bf16[128,512]{1,0:T(8,128)(2,1)S(1)}, u32[]{:S(2)}, u32[]{:S(2)}) collective-permute-start(bf16[128,512]{1,0:T(8,128)(2,1)S(1)} %constant_dynamic-slice_fusion.3), channel_id=1, source_target_pairs={{2,6},{3,7},{4,8},{5,9},{6,2},{7,3},{8,4},{9,5},{10,10},{11,11},{1... | collective-permute-start | bytes 393224 | tf_op jit(solution)/shard_map/ppermute | solution.py:330
  3.3 3.0 %collective-permute-start = (bf16[128,512]{1,0:T(8,128)(2,1)S(1)}, bf16[128,512]{1,0:T(8,128)(2,1)S(1)}, u32[]{:S(2)}, u32[]{:S(2)}) collective-permute-start(bf16[128,512]{1,0:T(8,128)(2,1)S(1)} %constant_dynamic-slice_fusion.2), channel_id=1, source_target_pairs={{2,6},{3,7},{4,8},{5,9},{6,2},{7,3},{8,4},{9,5},{10,10},{11,11},{1... | collective-permute-start | bytes 393224 | tf_op jit(solution)/shard_map/ppermute | solution.py:330
  4.0 0.7 %copy-start.2 = (s32[4,2]{0,1:T(2,128)S(1)}, s32[4,2]{0,1:T(2,128)}, u32[]{:S(2)}) copy-start(s32[4,2]{0,1:T(2,128)} %param.5) | copy-start | bytes 100
  4.0 0.8 %copy-start.1 = (s32[1,16]{1,0:T(1,128)S(1)}, s32[1,16]{1,0:T(1,128)}, u32[]{:S(2)}) copy-start(s32[1,16]{1,0:T(1,128)} %mask_ref.7) | copy-start | bytes 196
  4.0 25.7 %collective-permute-start.2 = (bf16[128,1024]{1,0:T(8,128)(2,1)S(1)}, bf16[128,1024]{1,0:T(8,128)(2,1)S(1)}, u32[]{:S(2)}, u32[]{:S(2)}) collective-permute-start(bf16[128,1024]{1,0:T(8,128)(2,1)S(1)} %get-tuple-element.7), channel_id=1, source_target_pairs={{6,10},{7,11},{8,12},{9,13},{10,6},{11,7},{12,8},{13,9},{2,2},{3,3... | collective-permute-start | bytes 786440 | tf_op jit(solution)/shard_map/ppermute | solution.py:330
  7.6 34.7 %collective-permute-start.3 = (bf16[128,1024]{1,0:T(8,128)(2,1)S(1)}, bf16[128,1024]{1,0:T(8,128)(2,1)S(1)}, u32[]{:S(2)}, u32[]{:S(2)}) collective-permute-start(bf16[128,1024]{1,0:T(8,128)(2,1)S(1)} %get-tuple-element.5), channel_id=1, source_target_pairs={{10,14},{11,15},{12,0},{13,1},{14,10},{15,11},{0,12},{1,13},{2,2},... | collective-permute-start | bytes 786440 | tf_op jit(solution)/shard_map/ppermute | solution.py:330

commit v6 on v5

--- a/solution.py
+++ b/solution.py
@@ -15,7 +15,7 @@
 LANES = 128
 WIDTH = 2 * HALF + 1
 MASK_LANE = 64
-GROUP = 4
+GROUP = 8
 THIRD = WIDTH // 3
 SPAN = PATCH // 2 + 16
 
@@ -203,16 +203,22 @@
 
 
 def looped(count, one):
+    width = min(GROUP, count)
+
     def body(turn, carry):
-        for k in range(GROUP):
-            one(turn * GROUP + k, k)
+        for k in range(width):
+            one(turn * width + k, k)
         return carry
 
-    lax.fori_loop(0, count // GROUP, body, 0)
+    if count == width:
+        body(0, 0)
+    else:
+        lax.fori_loop(0, count // width, body, 0)
 
 
 def columns(index):
-    return pl.ds(pl.multiple_of(index * PATCH, PATCH), PATCH)
+    start = index * PATCH
+    return pl.ds(start if isinstance(start, int) else pl.multiple_of(start, PATCH), PATCH)
 
 
 def warp_indexed(patch, base_ref, swing_ref, index, cols):
@@ -234,69 +240,72 @@
     group, row_index = rotated // rows, rotated % rows
     is_upper = group == step
     first = begin + jnp.where(is_upper, nodes // 2, 0)
-    row_offset, col_offset = offsets_ref[step, 0], offsets_ref[step, 1]
-    area = float(PATCH * PATCH)
-
-    if step > 1:
-        row_shift = own_row(relax(section_grid(refs[0][...], step - 1, rows), rows, nodes), row_index)
-        base_ref[...], swing_ref[...] = kernels_of(row_shift, first, cols, nodes)
-
-        def warp_one(index, slot):
-            patch = jnp.where(is_upper, other_ref[:, columns(index)], own_ref[:, columns(index + begin)])
-            prev_ref[index] = warp_indexed(patch, base_ref, swing_ref, index, cols)
-
-        looped(cols, warp_one)
-
-    def one(index, slot):
-        other = other_ref[:, columns(index)]
-        own = jnp.where(is_upper, own_ref[:, columns(index + begin + nodes // 2)], other)
+
+    @pl.when(is_upper | (group == step - 1))
+    def _():
+        row_offset, col_offset = offsets_ref[step, 0], offsets_ref[step, 1]
+        area = float(PATCH * PATCH)
+
         if step > 1:
-            prev = prev_ref[index]
+            row_shift = own_row(relax(section_grid(refs[0][...], step - 1, rows), rows, nodes), row_index)
+            base_ref[...], swing_ref[...] = kernels_of(row_shift, first, cols, nodes)
+
+            def warp_one(index, slot):
+                patch = jnp.where(is_upper, other_ref[:, columns(index)], own_ref[:, columns(index + begin)])
+                prev_ref[index] = warp_indexed(patch, base_ref, swing_ref, index, cols)
+
+            looped(cols, warp_one)
+
+        def one(index, slot):
+            other = other_ref[:, columns(index)]
+            own = jnp.where(is_upper, own_ref[:, columns(index + begin + nodes // 2)], other)
+            if step > 1:
+                prev = prev_ref[index]
+            else:
+                prev = jnp.where(is_upper, other, own_ref[:, columns(index + begin)])
+            own_corner, prev_corner = (x[0:1, 0:1].astype(f32) for x in (own, prev))
+            corner_ref[0, pl.ds(index, 1), :] = jnp.broadcast_to(own_corner, (1, LANES))
+            corner_ref[1, pl.ds(index, 1), :] = jnp.broadcast_to(prev_corner, (1, LANES))
+            sums = moments(own, own_corner) + moments(prev, prev_corner)
+            for k, value in enumerate(sums):
+                sums_ref[k, pl.ds(index, 1)] = value[None]
+            level = own_corner * prev_corner
+            score_ref[pl.ds(index, 1)] = correlate(own, prev, level, col_offset, band_ref.at[slot])[None]
+
+        looped(cols, one)
+        reduce = lambda value: jnp.sum(jnp.sum(value, axis=1), axis=1, keepdims=True)
+        own_sum, own_square, prev_sum, prev_square = (reduce(sums_ref[k]) * (1.0 / area) for k in range(4))
+        spread = jnp.sqrt(
+            (jnp.maximum(own_square - own_sum * own_sum, 0.0) + 1e-5)
+            * (jnp.maximum(prev_square - prev_sum * prev_sum, 0.0) + 1e-5)
+        )
+        scale = sharpness / area / spread
+        level = corner_ref[0] * prev_sum + corner_ref[1] * own_sum + own_sum * prev_sum
+        shape = (cols, THIRD, 2 * LANES)
+        third, row_lag = lag_layout(shape, 2)
+        col_lag = iota(shape, 1) + THIRD * third - HALF + col_offset
+        inside = (jnp.abs(row_lag - row_offset) <= HALF) & (third < THIRD)
+        level = jnp.concatenate([level, level], axis=1) * area
+        scale = jnp.broadcast_to(scale, (cols, 2 * LANES))
+        score = (score_ref[...] - level[:, None, :]) * scale[:, None, :]
+        weights = jnp.where(inside, jnp.exp(jnp.where(inside, score, 0.0)), 0.0)
+        inverse = 1.0 / reduce(weights)
+        flow_row = reduce(weights * row_lag.astype(f32)) * inverse
+        flow_col = reduce(weights * col_lag.astype(f32)) * inverse
+        shape = (cols, LANES)
+        node, lane = iota(shape, 0) + first, iota(shape, 1)
+        sent = jnp.where(lane == node, flow_row, jnp.where(lane == node + nodes, flow_col, 0.0))
+        sent = jnp.sum(sent, axis=0, keepdims=True)
+        if begin == 0:
+            masks = mask_ref[...].astype(f32)
+            masks = jnp.concatenate(
+                [jnp.zeros((1, MASK_LANE), f32), masks, masks, jnp.zeros((1, LANES - MASK_LANE - 2 * nodes), f32)],
+                axis=1,
+            )
+            sent = sent + jnp.where(is_upper, masks, 0.0)
         else:
-            prev = jnp.where(is_upper, other, own_ref[:, columns(index + begin)])
-        own_corner, prev_corner = (x[0:1, 0:1].astype(f32) for x in (own, prev))
-        corner_ref[0, pl.ds(index, 1), :] = jnp.broadcast_to(own_corner, (1, LANES))
-        corner_ref[1, pl.ds(index, 1), :] = jnp.broadcast_to(prev_corner, (1, LANES))
-        sums = moments(own, own_corner) + moments(prev, prev_corner)
-        for k, value in enumerate(sums):
-            sums_ref[k, pl.ds(index, 1)] = value[None]
-        level = own_corner * prev_corner
-        score_ref[pl.ds(index, 1)] = correlate(own, prev, level, col_offset, band_ref.at[slot])[None]
-
-    looped(cols, one)
-    reduce = lambda value: jnp.sum(jnp.sum(value, axis=1), axis=1, keepdims=True)
-    own_sum, own_square, prev_sum, prev_square = (reduce(sums_ref[k]) * (1.0 / area) for k in range(4))
-    spread = jnp.sqrt(
-        (jnp.maximum(own_square - own_sum * own_sum, 0.0) + 1e-5)
-        * (jnp.maximum(prev_square - prev_sum * prev_sum, 0.0) + 1e-5)
-    )
-    scale = sharpness / area / spread
-    level = corner_ref[0] * prev_sum + corner_ref[1] * own_sum + own_sum * prev_sum
-    shape = (cols, THIRD, 2 * LANES)
-    third, row_lag = lag_layout(shape, 2)
-    col_lag = iota(shape, 1) + THIRD * third - HALF + col_offset
-    inside = (jnp.abs(row_lag - row_offset) <= HALF) & (third < THIRD)
-    level = jnp.concatenate([level, level], axis=1) * area
-    scale = jnp.broadcast_to(scale, (cols, 2 * LANES))
-    score = (score_ref[...] - level[:, None, :]) * scale[:, None, :]
-    weights = jnp.where(inside, jnp.exp(jnp.where(inside, score, 0.0)), 0.0)
-    inverse = 1.0 / reduce(weights)
-    flow_row = reduce(weights * row_lag.astype(f32)) * inverse
-    flow_col = reduce(weights * col_lag.astype(f32)) * inverse
-    shape = (cols, LANES)
-    node, lane = iota(shape, 0) + first, iota(shape, 1)
-    sent = jnp.where(lane == node, flow_row, jnp.where(lane == node + nodes, flow_col, 0.0))
-    sent = jnp.sum(sent, axis=0, keepdims=True)
-    if begin == 0:
-        masks = mask_ref[...].astype(f32)
-        masks = jnp.concatenate(
-            [jnp.zeros((1, MASK_LANE), f32), masks, masks, jnp.zeros((1, LANES - MASK_LANE - 2 * nodes), f32)],
-            axis=1,
-        )
-        sent = sent + jnp.where(is_upper, masks, 0.0)
-    else:
-        sent = sent + refs[0][0:1, :]
-    out_ref[...] = jnp.broadcast_to(sent, out_ref.shape)
+            sent = sent + refs[0][0:1, :]
+        out_ref[...] = jnp.broadcast_to(sent, out_ref.shape)
 
 
 def home_kernel(rows, nodes, own_ref, *refs):
@@ -335,19 +344,13 @@
         if after is not None:
             half, after = lax.optimization_barrier((half, after))
         ends = [(place(lower, i), place(lower + 1, i)) for i in range(rows)]
-        idle = [
-            (place(s, i),) * 2 for s in range(SECTIONS) if s not in (lower, lower + 1) for i in range(rows)
-        ]
-        return half, moved(half, ends + [(d, s) for s, d in ends] + idle)
+        return half, moved(half, ends + [(d, s) for s, d in ends])
 
     half = nodes // 2
     chunk = half // 2
-    head, first_chunk = swapped(sections, 0, 0, chunk)
-    source, head = lax.optimization_barrier((sections, head))
-    others = {
-        1: [(0, chunk, first_chunk), (chunk, chunk, swapped(source, 0, chunk, chunk)[1])],
-        2: [(0, half, swapped(source, 1, 0, half)[1])],
-    }
+    heads, chunks = zip(*(swapped(sections, 0, k * chunk, chunk) for k in range(2)))
+    source, heads = lax.optimization_barrier((sections, heads))
+    others = {1: [(k * chunk, chunk, chunks[k]) for k in range(2)]}
 
     vmem = pl.BlockSpec(memory_space=pltpu.VMEM)
     smem = pl.BlockSpec(memory_space=pltpu.SMEM)
@@ -374,9 +377,10 @@
                 name=f"chain{step}_{begin}",
             )(coarse_offsets, sections, other, valid_mask, *extra)
             extra = [sent]
+            waiting = max(others) + 1
+            if waiting < SECTIONS:
+                others[waiting] = [(0, half, swapped(source, waiting - 1, 0, half, sent)[1])]
         gathered.append(lax.all_to_all(sent, "tile", 0, 0, tiled=True))
-        if step + 1 < SECTIONS - 1:
-            others[step + 2] = [(0, half, swapped(source, step + 1, 0, half, sent)[1])]
     return pl.pallas_call(
         functools.partial(home_kernel, rows, nodes),
         out_shape=(

time: 58.5 us -> 55.8 us (0.954)
  blocking collectives: 27 us -> 18 us
  waiting for transfers between devices: 0.01 us -> 6.33 us
  Pallas kernels: 13.2 us -> 7.48 us
  starting transfers between devices: 15.2 us -> 20.5 us
    all_to_all x3 -> x2, blocking collectives: 27 us -> 18 us  [shards(): gathered.append(lax.all_to_all(sent, 'tile', 0, 0, tiled=True))]
    all_to_all x0 -> x1, waiting for transfers between devices: none -> 6.32 us  [shards(): gathered.append(lax.all_to_all(sent, 'tile', 0, 0, tiled=True))]
    pallas_call x4, Pallas kernels: 9.95 us -> 4.94 us  [shards(): pl.pallas_call(functools.partial(chain_kernel, step, rows, nodes, begin,...]
    all_to_all x0 -> x1, starting transfers between devices: none -> 3.94 us  [shards(): gathered.append(lax.all_to_all(sent, 'tile', 0, 0, tiled=True))]
    ppermute x4, starting transfers between devices: 15.2 us -> 16.5 us  [shards(): moved = lambda value, pairs: lax.ppermute(value, 'tile', pairs)]
    unnamed x7, local copies, waits for them, and re-layouts: 0.11 us -> 1.38 us
    dynamic_slice x3 -> x2, local copies, waits for them, and re-layouts: 1.93 us -> 1.08 us  [swapped(): half = lax.dynamic_slice_in_dim(source, start, cols * PATCH, 1)]
    pallas_call x1, Pallas kernels: 3.27 us -> 2.54 us  [shards(): pl.pallas_call(functools.partial(home_kernel, rows, nodes), out_shape=(ja...]
  transfers between devices with their start and end apart: 4 -> 5, of which waited for: 0 -> 1; matrix products, arithmetic and copies ran while one was open for 2% -> 0% of each run, Pallas kernels for 11% -> 4%
where the time goes in v6:
time: 55.8 us; the launch traced here: 55.5 us
  starting transfers between devices  20.5 us (37%)
  blocking collectives  18 us (32%)
  Pallas kernels  7.48 us (13%)
  waiting for transfers between devices  6.33 us (11%)
  local copies, waits for them, and re-layouts  2.45 us (4%)
  between operations  0.8 us (1%)
    all_to_all x2, blocking collectives, shards(): gathered.append(lax.all_to_all(sent, 'tile', 0, 0, tiled=True))  18 us
    ppermute x4, starting transfers between devices, shards(): moved = lambda value, pairs: lax.ppermute(value, 'tile', pairs)  16.5 us
    all_to_all x1, waiting for transfers between devices, shards(): gathered.append(lax.all_to_all(sent, 'tile', 0, 0, tiled=True))  6.32 us
    pallas_call x4, Pallas kernels, shards(): pl.pallas_call(functools.partial(chain_kernel, step, rows, nodes, begin,...  4.94 us
    all_to_all x1, starting transfers between devices, shards(): gathered.append(lax.all_to_all(sent, 'tile', 0, 0, tiled=True))  3.94 us
    pallas_call x1, Pallas kernels, shards(): pl.pallas_call(functools.partial(home_kernel, rows, nodes), out_shape=(ja...  2.54 us
    unnamed x7, local copies, waits for them, and re-layouts  1.38 us
  transfers between devices with their start and end apart: 5, of which 1 were waited for; matrix products, arithmetic and copies ran while one was open for 0% of the time, Pallas kernels for 4%

profile of v6, /device:TPU:0, one launch (start us, length us, event | category | flops | bytes accessed | tf_op | source)
XLA Modules:
  0.0 55.5 jit_solution(1541360991403674316)
XLA Ops:
  0.6 0.0 copy-start
  0.7 1.0 %constant_dynamic-slice_fusion.2 = (bf16[128,512]{1,0:T(8,128)(2,1)S(1)}, bf16[128,512]{1,0:T(8,128)(2,1)S(1)}) fusion(bf16[128,2048]{1,0:T(8,128)(2,1)} %own_ref.9, s32[]{:T(128)S(6)} %select_n.38, s32[]{:T(128)S(6)} %select_n.37), kind=kLoop, calls=%fused_computation.2 | loop fusion | bytes 524296 | tf_op jit(solution)/shard_map/dynamic_slice | solution.py:343
  1.7 0.7 %collective-permute-start.1 = (bf16[128,512]{1,0:T(8,128)(2,1)S(1)}, bf16[128,512]{1,0:T(8,128)(2,1)S(1)}, u32[]{:S(2)}, u32[]{:S(2)}) collective-permute-start(bf16[128,512]{1,0:T(8,128)(2,1)S(1)} %get-tuple-element.10), channel_id=1, source_target_pairs={{2,6},{3,7},{4,8},{5,9},{6,2},{7,3},{8,4},{9,5},{18,22},{19,23},{2... | collective-permute-start | bytes 393224 | tf_op jit(solution)/shard_map/ppermute | solution.py:339
  2.4 0.7 %collective-permute-start = (bf16[128,512]{1,0:T(8,128)(2,1)S(1)}, bf16[128,512]{1,0:T(8,128)(2,1)S(1)}, u32[]{:S(2)}, u32[]{:S(2)}) collective-permute-start(bf16[128,512]{1,0:T(8,128)(2,1)S(1)} %get-tuple-element.11), channel_id=1, source_target_pairs={{2,6},{3,7},{4,8},{5,9},{6,2},{7,3},{8,4},{9,5},{18,22},{19,23},{2... | collective-permute-start | bytes 393224 | tf_op jit(solution)/shard_map/ppermute | solution.py:339
  3.1 0.0 copy-start.2
  3.1 0.7 %copy-done.2 = s32[4,2]{0,1:T(2,128)S(1)} copy-done((s32[4,2]{0,1:T(2,128)S(1)}, s32[4,2]{0,1:T(2,128)}, u32[]{:S(2)}) %copy-start.2) | copy-done | bytes 56
  3.8 0.1 copy.10.offsets_ref
  3.9 0.0 copy-done
  3.9 0.0 copy-start.1
  3.9 0.0 collective-permute-done.1.other_ref
  3.9 0.6 %copy-done.1 = s32[1,16]{1,0:T(1,128)S(1)} copy-done((s32[1,16]{1,0:T(1,128)S(1)}, s32[1,16]{1,0:T(1,128)}, u32[]{:S(2)}) %copy-start.1) | copy-done | bytes 88
  4.5 0.6 %chain1_0.1.refs_0_ = f32[16,128]{1,0:T(8,128)S(1)} custom-call(s32[4,2]{1,0:T(4,128)S(1)} %copy.10.offsets_ref, bf16[128,2048]{1,0:T(8,128)(2,1)S(1)} %copy-done, bf16[128,512]{1,0:T(8,128)(2,1)S(1)} %collective-permute-done.1.other_ref, s32[1,16]{1,0:T(1,128)S(1)} %copy-done.1), custom_call_target="tpu_custom_call" | custom-call | tf_op jit(solution)/shard_map/chain1_0/pallas_call | solution.py:362
  5.1 0.7 %collective-permute-start.2 = (bf16[128,1024]{1,0:T(8,128)(2,1)S(1)}, bf16[128,1024]{1,0:T(8,128)(2,1)S(1)}, u32[]{:S(2)}, u32[]{:S(2)}) collective-permute-start(bf16[128,1024]{1,0:T(8,128)(2,1)S(1)} %get-tuple-element.6), channel_id=1, source_target_pairs={{6,10},{7,11},{8,12},{9,13},{10,6},{11,7},{12,8},{13,9},{22,26},{2... | collective-permute-start | bytes 786440 | tf_op jit(solution)/shard_map/ppermute | solution.py:339
  5.8 0.0 collective-permute-done.other_ref
  5.8 0.6 %chain1_4.1 = f32[16,128]{1,0:T(8,128)S(1)} custom-call(s32[4,2]{1,0:T(4,128)S(1)} %copy.10.offsets_ref, bf16[128,2048]{1,0:T(8,128)(2,1)S(1)} %copy-done, bf16[128,512]{1,0:T(8,128)(2,1)S(1)} %collective-permute-done.other_ref, s32[1,16]{1,0:T(1,128)S(1)} %copy-done.1, f32[16,128]{1,0:T(8,128)S(1)} %chain1_0.1.refs_0_), custom_call_target="tpu_custom_call" | custom-call | tf_op jit(solution)/shard_map/chain1_4/pallas_call | solution.py:362
  6.4 14.5 %collective-permute-start.3 = (bf16[128,1024]{1,0:T(8,128)(2,1)S(1)}, bf16[128,1024]{1,0:T(8,128)(2,1)S(1)}, u32[]{:S(2)}, u32[]{:S(2)}) collective-permute-start(bf16[128,1024]{1,0:T(8,128)(2,1)S(1)} %get-tuple-element.7), channel_id=1, source_target_pairs={{10,14},{11,15},{12,0},{13,1},{14,10},{15,11},{0,12},{1,13},{26,30... | collective-permute-start | bytes 786440 | tf_op jit(solution)/shard_map/ppermute | solution.py:339
  20.9 9.0 %all_to_all.33 = f32[16,1,128]{2,1,0:T(1,128)S(1)} all-to-all(f32[16,1,128]{2,1,0:T(1,128)S(1)} %bitcast.16), channel_id=1, replica_groups=mesh['parts'=2,'tile'=16] {'tile'}, dimensions={0} | all-to-all | bytes 16384 | tf_op jit(solution)/shard_map/all_to_all | solution.py:383
  29.9 0.0 collective-permute-done.2.other_ref
  29.9 1.2 %chain2_0.1 = f32[16,128]{1,0:T(8,128)} custom-call(s32[4,2]{1,0:T(4,128)S(1)} %copy.10.offsets_ref, bf16[128,2048]{1,0:T(8,128)(2,1)S(1)} %copy-done, bf16[128,1024]{1,0:T(8,128)(2,1)S(1)} %collective-permute-done.2.other_ref, s32[1,16]{1,0:T(1,128)S(1)} %copy-done.1, f32[16,128]{1,0:T(8,128)S(1)} %bitcast.12), custom_call_target="tpu_custom_call" | custom-call | tf_op jit(solution)/shard_map/chain2_0/pallas_call | solution.py:362
  31.1 3.9 %all-to-all-start.1 = ((f32[16,1,128]{2,1,0:T(1,128)}), f32[16,1,128]{2,1,0:T(1,128)S(1)}, u32[]{:S(2)}, u32[]{:S(2)}) async-start(f32[16,1,128]{2,1,0:T(1,128)} %bitcast.4), calls=%async_computation.1 | async-start | bytes 16384 | tf_op jit(solution)/shard_map/all_to_all | solution.py:383
  35.0 0.0 collective-permute-done.3.other_ref
  35.1 6.3 %all-to-all-done.1 = f32[16,1,128]{2,1,0:T(1,128)S(1)} async-done(((f32[16,1,128]{2,1,0:T(1,128)}), f32[16,1,128]{2,1,0:T(1,128)S(1)}, u32[]{:S(2)}, u32[]{:S(2)}) %all-to-all-start.1) | async-done | bytes 8224 | tf_op jit(solution)/shard_map/all_to_all | solution.py:383
  41.4 2.6 %chain3_0.1 = f32[16,128]{1,0:T(8,128)S(1)} custom-call(s32[4,2]{1,0:T(4,128)S(1)} %copy.10.offsets_ref, bf16[128,2048]{1,0:T(8,128)(2,1)S(1)} %copy-done, bf16[128,1024]{1,0:T(8,128)(2,1)S(1)} %collective-permute-done.3.other_ref, s32[1,16]{1,0:T(1,128)S(1)} %copy-done.1, f32[16,128]{1,0:T(8,128)S(1)} %bitcast.14), custom_call_target="tpu_custom_call" | custom-call | tf_op jit(solution)/shard_map/chain3_0/pallas_call | solution.py:362
  44.0 9.0 %all_to_all.34 = f32[16,1,128]{2,1,0:T(1,128)S(1)} all-to-all(f32[16,1,128]{2,1,0:T(1,128)S(1)} %bitcast.18), channel_id=1, replica_groups=mesh['parts'=2,'tile'=16] {'tile'}, dimensions={0} | all-to-all | bytes 16384 | tf_op jit(solution)/shard_map/all_to_all | solution.py:383
  52.9 2.5 %home.1 = (bf16[128,2048]{1,0:T(8,128)(2,1)}, f32[2,1,16]{2,1,0:T(1,128)}) custom-call(bf16[128,2048]{1,0:T(8,128)(2,1)S(1)} %copy-done, f32[16,128]{1,0:T(8,128)S(1)} %bitcast.13, f32[16,128]{1,0:T(8,128)S(1)} %bitcast.15, f32[16,128]{1,0:T(8,128)S(1)} %bitcast.17), custom_call_target="tpu_custom_call" | custom-call | tf_op jit(solution)/shard_map/home/pallas_call | solution.py:384
  (1 shorter events, 0.0 us)
Async XLA Ops:
  0.6 3.2 %copy-start = (bf16[128,2048]{1,0:T(8,128)(2,1)S(1)}, bf16[128,2048]{1,0:T(8,128)(2,1)}, u32[]{:S(2)}) copy-start(bf16[128,2048]{1,0:T(8,128)(2,1)} %own_ref.9) | copy-start | bytes 1572868
  1.7 2.2 %collective-permute-start.1 = (bf16[128,512]{1,0:T(8,128)(2,1)S(1)}, bf16[128,512]{1,0:T(8,128)(2,1)S(1)}, u32[]{:S(2)}, u32[]{:S(2)}) collective-permute-start(bf16[128,512]{1,0:T(8,128)(2,1)S(1)} %get-tuple-element.10), channel_id=1, source_target_pairs={{2,6},{3,7},{4,8},{5,9},{6,2},{7,3},{8,4},{9,5},{18,22},{19,23},{2... | collective-permute-start | bytes 393224 | tf_op jit(solution)/shard_map/ppermute | solution.py:339
  2.4 3.4 %collective-permute-start = (bf16[128,512]{1,0:T(8,128)(2,1)S(1)}, bf16[128,512]{1,0:T(8,128)(2,1)S(1)}, u32[]{:S(2)}, u32[]{:S(2)}) collective-permute-start(bf16[128,512]{1,0:T(8,128)(2,1)S(1)} %get-tuple-element.11), channel_id=1, source_target_pairs={{2,6},{3,7},{4,8},{5,9},{6,2},{7,3},{8,4},{9,5},{18,22},{19,23},{2... | collective-permute-start | bytes 393224 | tf_op jit(solution)/shard_map/ppermute | solution.py:339
  3.1 0.7 %copy-start.2 = (s32[4,2]{0,1:T(2,128)S(1)}, s32[4,2]{0,1:T(2,128)}, u32[]{:S(2)}) copy-start(s32[4,2]{0,1:T(2,128)} %param.5) | copy-start | bytes 100
  3.9 0.7 %copy-start.1 = (s32[1,16]{1,0:T(1,128)S(1)}, s32[1,16]{1,0:T(1,128)}, u32[]{:S(2)}) copy-start(s32[1,16]{1,0:T(1,128)} %mask_ref.7) | copy-start | bytes 196
  5.1 24.8 %collective-permute-start.2 = (bf16[128,1024]{1,0:T(8,128)(2,1)S(1)}, bf16[128,1024]{1,0:T(8,128)(2,1)S(1)}, u32[]{:S(2)}, u32[]{:S(2)}) collective-permute-start(bf16[128,1024]{1,0:T(8,128)(2,1)S(1)} %get-tuple-element.6), channel_id=1, source_target_pairs={{6,10},{7,11},{8,12},{9,13},{10,6},{11,7},{12,8},{13,9},{22,26},{2... | collective-permute-start | bytes 786440 | tf_op jit(solution)/shard_map/ppermute | solution.py:339
  6.4 28.6 %collective-permute-start.3 = (bf16[128,1024]{1,0:T(8,128)(2,1)S(1)}, bf16[128,1024]{1,0:T(8,128)(2,1)S(1)}, u32[]{:S(2)}, u32[]{:S(2)}) collective-permute-start(bf16[128,1024]{1,0:T(8,128)(2,1)S(1)} %get-tuple-element.7), channel_id=1, source_target_pairs={{10,14},{11,15},{12,0},{13,1},{14,10},{15,11},{0,12},{1,13},{26,30... | collective-permute-start | bytes 786440 | tf_op jit(solution)/shard_map/ppermute | solution.py:339
  31.1 10.3 %all-to-all-start.1 = ((f32[16,1,128]{2,1,0:T(1,128)}), f32[16,1,128]{2,1,0:T(1,128)S(1)}, u32[]{:S(2)}, u32[]{:S(2)}) async-start(f32[16,1,128]{2,1,0:T(1,128)} %bitcast.4), calls=%async_computation.1 | async-start | bytes 16384 | tf_op jit(solution)/shard_map/all_to_all | solution.py:383

commit v7 on v6

--- a/solution.py
+++ b/solution.py
@@ -233,15 +233,16 @@
     ).astype(bf16)
 
 
-def chain_kernel(step, rows, nodes, begin, cols, offsets_ref, own_ref, other_ref, mask_ref, *refs):
+def chain_kernel(step, rows, nodes, offsets_ref, own_ref, other_ref, mask_ref, *refs):
     out_ref, score_ref, band_ref, sums_ref, corner_ref, prev_ref, base_ref, swing_ref = refs[-8:]
+    cols = nodes // 2
     count = lax.axis_size("tile")
     rotated = (lax.axis_index("tile") + count - rows // 2) % count
     group, row_index = rotated // rows, rotated % rows
     is_upper = group == step
-    first = begin + jnp.where(is_upper, nodes // 2, 0)
-
-    @pl.when(is_upper | (group == step - 1))
+    first = jnp.where(is_upper, cols, 0)
+
+    @pl.when(is_upper | (group == step - 1) | (step == 1))
     def _():
         row_offset, col_offset = offsets_ref[step, 0], offsets_ref[step, 1]
         area = float(PATCH * PATCH)
@@ -251,18 +252,18 @@
             base_ref[...], swing_ref[...] = kernels_of(row_shift, first, cols, nodes)
 
             def warp_one(index, slot):
-                patch = jnp.where(is_upper, other_ref[:, columns(index)], own_ref[:, columns(index + begin)])
+                patch = jnp.where(is_upper, other_ref[:, columns(index)], own_ref[:, columns(index)])
                 prev_ref[index] = warp_indexed(patch, base_ref, swing_ref, index, cols)
 
             looped(cols, warp_one)
 
         def one(index, slot):
             other = other_ref[:, columns(index)]
-            own = jnp.where(is_upper, own_ref[:, columns(index + begin + nodes // 2)], other)
+            own = jnp.where(is_upper, own_ref[:, columns(index + cols)], other)
             if step > 1:
                 prev = prev_ref[index]
             else:
-                prev = jnp.where(is_upper, other, own_ref[:, columns(index + begin)])
+                prev = jnp.where(is_upper, other, own_ref[:, columns(index)])
             own_corner, prev_corner = (x[0:1, 0:1].astype(f32) for x in (own, prev))
             corner_ref[0, pl.ds(index, 1), :] = jnp.broadcast_to(own_corner, (1, LANES))
             corner_ref[1, pl.ds(index, 1), :] = jnp.broadcast_to(prev_corner, (1, LANES))
@@ -296,15 +297,10 @@
         node, lane = iota(shape, 0) + first, iota(shape, 1)
         sent = jnp.where(lane == node, flow_row, jnp.where(lane == node + nodes, flow_col, 0.0))
         sent = jnp.sum(sent, axis=0, keepdims=True)
-        if begin == 0:
-            masks = mask_ref[...].astype(f32)
-            masks = jnp.concatenate(
-                [jnp.zeros((1, MASK_LANE), f32), masks, masks, jnp.zeros((1, LANES - MASK_LANE - 2 * nodes), f32)],
-                axis=1,
-            )
-            sent = sent + jnp.where(is_upper, masks, 0.0)
-        else:
-            sent = sent + refs[0][0:1, :]
+        masks = mask_ref[...].astype(f32)
+        gap = jnp.zeros((1, MASK_LANE - 2 * nodes), f32)
+        masks = jnp.concatenate([gap, jnp.zeros((1, 2 * nodes), f32), masks, masks, gap], axis=1)
+        sent = sent + jnp.where(is_upper, masks, 0.0)
         out_ref[...] = jnp.broadcast_to(sent, out_ref.shape)
 
 
@@ -338,19 +334,16 @@
     group = (lax.axis_index("tile") + count - rows // 2) % count // rows
     moved = lambda value, pairs: lax.ppermute(value, "tile", pairs)
 
-    def swapped(source, lower, begin, cols, after=None):
-        start = (begin + jnp.where(group == lower, nodes // 2, 0)) * PATCH
-        half = lax.dynamic_slice_in_dim(source, start, cols * PATCH, 1)
+    def swapped(lower, after=None):
+        start = jnp.where(group == lower, half * PATCH, 0)
+        sent = lax.dynamic_slice_in_dim(sections, start, half * PATCH, 1)
         if after is not None:
-            half, after = lax.optimization_barrier((half, after))
+            sent, after = lax.optimization_barrier((sent, after))
         ends = [(place(lower, i), place(lower + 1, i)) for i in range(rows)]
-        return half, moved(half, ends + [(d, s) for s, d in ends])
+        return moved(sent, ends + [(d, s) for s, d in ends])
 
     half = nodes // 2
-    chunk = half // 2
-    heads, chunks = zip(*(swapped(sections, 0, k * chunk, chunk) for k in range(2)))
-    source, heads = lax.optimization_barrier((sections, heads))
-    others = {1: [(k * chunk, chunk, chunks[k]) for k in range(2)]}
+    others = [swapped(0), swapped(1)]
 
     vmem = pl.BlockSpec(memory_space=pltpu.VMEM)
     smem = pl.BlockSpec(memory_space=pltpu.SMEM)
@@ -358,29 +351,26 @@
     gathered = []
     for step in range(1, SECTIONS):
         extra = gathered[-1:]
-        for begin, cols, other in others[step]:
-            sent = pl.pallas_call(
-                functools.partial(chain_kernel, step, rows, nodes, begin, cols),
-                out_shape=jax.ShapeDtypeStruct((count, LANES), f32),
-                in_specs=[smem] + [vmem] * (3 + len(extra)),
-                out_specs=vmem,
-                scratch_shapes=[
-                    pltpu.VMEM((cols, THIRD, 2 * LANES), f32),
-                    pltpu.VMEM((GROUP, 2, 8 * THIRD, LANES), f32),
-                    pltpu.VMEM((4, cols, 8, LANES), f32),
-                    pltpu.VMEM((2, cols, LANES), f32),
-                    pltpu.VMEM((cols, PATCH, PATCH), bf16),
-                    pltpu.VMEM((2 * cols, LANES), f32),
-                    pltpu.VMEM((2 * cols, LANES), f32),
-                ],
-                compiler_params=params,
-                name=f"chain{step}_{begin}",
-            )(coarse_offsets, sections, other, valid_mask, *extra)
-            extra = [sent]
-            waiting = max(others) + 1
-            if waiting < SECTIONS:
-                others[waiting] = [(0, half, swapped(source, waiting - 1, 0, half, sent)[1])]
+        sent = pl.pallas_call(
+            functools.partial(chain_kernel, step, rows, nodes),
+            out_shape=jax.ShapeDtypeStruct((count, LANES), f32),
+            in_specs=[smem] + [vmem] * (3 + len(extra)),
+            out_specs=vmem,
+            scratch_shapes=[
+                pltpu.VMEM((half, THIRD, 2 * LANES), f32),
+                pltpu.VMEM((GROUP, 2, 8 * THIRD, LANES), f32),
+                pltpu.VMEM((4, half, 8, LANES), f32),
+                pltpu.VMEM((2, half, LANES), f32),
+                pltpu.VMEM((half, PATCH, PATCH), bf16),
+                pltpu.VMEM((2 * half, LANES), f32),
+                pltpu.VMEM((2 * half, LANES), f32),
+            ],
+            compiler_params=params,
+            name=f"chain{step}",
+        )(coarse_offsets, sections, others[step - 1], valid_mask, *extra)
         gathered.append(lax.all_to_all(sent, "tile", 0, 0, tiled=True))
+        if step + 1 < SECTIONS - 1:
+            others.append(swapped(step + 1, sent))
     return pl.pallas_call(
         functools.partial(home_kernel, rows, nodes),
         out_shape=(

time: 55.8 us -> 51.9 us (0.930)
  starting transfers between devices: 20.5 us -> 15.9 us
  local copies, waits for them, and re-layouts: 2.45 us -> 1.33 us
  blocking collectives: 18 us -> 19.1 us
  Pallas kernels: 7.48 us -> 8.2 us
    ppermute x4 -> x3, starting transfers between devices: 16.5 us -> 11.7 us  [shards(): moved = lambda value, pairs: lax.ppermute(value, 'tile', pairs)]
    unnamed x7, local copies, waits for them, and re-layouts: 1.38 us -> 0.11 us
    all_to_all x2, blocking collectives: 18 us -> 19.1 us  [shards(): gathered.append(lax.all_to_all(sent, 'tile', 0, 0, tiled=True))]
    pallas_call x4 -> x3, Pallas kernels: 4.94 us -> 5.66 us  [shards(): pl.pallas_call(functools.partial(chain_kernel, step, rows, nodes), out_sh...]
    dynamic_slice x2 -> x1, local copies, waits for them, and re-layouts: 1.08 us -> 1.22 us  [swapped(): sent = lax.dynamic_slice_in_dim(sections, start, half * PATCH, 1)]
  transfers between devices with their start and end apart: 5 -> 4, of which waited for: 1 -> 1; matrix products, arithmetic and copies ran while one was open for 0% -> 0% of each run, Pallas kernels for 4% -> 6%
where the time goes in v7:
time: 51.9 us; the launch traced here: 51.6 us
  blocking collectives  19.1 us (37%)
  starting transfers between devices  15.9 us (31%)
  Pallas kernels  8.2 us (16%)
  waiting for transfers between devices  6.33 us (12%)
  local copies, waits for them, and re-layouts  1.33 us (3%)
  between operations  0.77 us (1%)
    all_to_all x2, blocking collectives, shards(): gathered.append(lax.all_to_all(sent, 'tile', 0, 0, tiled=True))  19.1 us
    ppermute x3, starting transfers between devices, shards(): moved = lambda value, pairs: lax.ppermute(value, 'tile', pairs)  11.7 us
    all_to_all x1, waiting for transfers between devices, shards(): gathered.append(lax.all_to_all(sent, 'tile', 0, 0, tiled=True))  6.32 us
    pallas_call x3, Pallas kernels, shards(): pl.pallas_call(functools.partial(chain_kernel, step, rows, nodes), out_sh...  5.66 us
    all_to_all x1, starting transfers between devices, shards(): gathered.append(lax.all_to_all(sent, 'tile', 0, 0, tiled=True))  4.24 us
    pallas_call x1, Pallas kernels, shards(): pl.pallas_call(functools.partial(home_kernel, rows, nodes), out_shape=(ja...  2.54 us
    dynamic_slice x1, local copies, waits for them, and re-layouts, swapped(): sent = lax.dynamic_slice_in_dim(sections, start, half * PATCH, 1)  1.22 us
  transfers between devices with their start and end apart: 4, of which 1 were waited for; matrix products, arithmetic and copies ran while one was open for 0% of the time, Pallas kernels for 6%

profile of v7, /device:TPU:0, one launch (start us, length us, event | category | flops | bytes accessed | tf_op | source)
XLA Modules:
  0.0 51.6 jit_solution(17699157274236239569)
XLA Ops:
  0.7 0.0 copy-start
  0.7 1.2 %constant_dynamic-slice_fusion = (bf16[128,1024]{1,0:T(8,128)(2,1)S(1)}, bf16[128,1024]{1,0:T(8,128)(2,1)S(1)}, bf16[128,1024]{1,0:T(8,128)(2,1)S(1)}) fusion(bf16[128,2048]{1,0:T(8,128)(2,1)} %own_ref.7, s32[]{:T(128)S(6)} %select_n.28, s32[]{:T(128)S(6)} %select_n.27, s32[]{:T(128)S(6)} %select_n.26), kind=kLoop, calls=%fused_computation | loop fusion | bytes 1572876 | tf_op jit(solution)/shard_map/dynamic_slice | solution.py:339
  1.9 0.0 copy-start.2
  1.9 0.7 %collective-permute-start = (bf16[128,1024]{1,0:T(8,128)(2,1)S(1)}, bf16[128,1024]{1,0:T(8,128)(2,1)S(1)}, u32[]{:S(2)}, u32[]{:S(2)}) collective-permute-start(bf16[128,1024]{1,0:T(8,128)(2,1)S(1)} %get-tuple-element.6), channel_id=1, source_target_pairs={{2,6},{3,7},{4,8},{5,9},{6,2},{7,3},{8,4},{9,5},{18,22},{19,23},{2... | collective-permute-start | bytes 786440 | tf_op jit(solution)/shard_map/ppermute | solution.py:335
  2.6 0.0 copy-start.1
  2.6 0.7 %collective-permute-start.1 = (bf16[128,1024]{1,0:T(8,128)(2,1)S(1)}, bf16[128,1024]{1,0:T(8,128)(2,1)S(1)}, u32[]{:S(2)}, u32[]{:S(2)}) collective-permute-start(bf16[128,1024]{1,0:T(8,128)(2,1)S(1)} %get-tuple-element.5), channel_id=1, source_target_pairs={{6,10},{7,11},{8,12},{9,13},{10,6},{11,7},{12,8},{13,9},{22,26},{2... | collective-permute-start | bytes 786440 | tf_op jit(solution)/shard_map/ppermute | solution.py:335
  3.3 0.0 copy-done.2
  3.3 0.1 copy.8.offsets_ref
  3.4 0.0 collective-permute-done.other_ref
  3.4 0.0 copy-done
  3.4 0.0 copy-done.1
  3.4 2.5 %chain1.1 = f32[16,128]{1,0:T(8,128)} custom-call(s32[4,2]{1,0:T(4,128)S(1)} %copy.8.offsets_ref, bf16[128,2048]{1,0:T(8,128)(2,1)S(1)} %copy-done, bf16[128,1024]{1,0:T(8,128)(2,1)S(1)} %collective-permute-done.other_ref, s32[1,16]{1,0:T(1,128)S(1)} %copy-done.1), custom_call_target="tpu_custom_call" | custom-call | tf_op jit(solution)/shard_map/chain1/pallas_call | solution.py:354
  5.9 10.3 %collective-permute-start.2 = (bf16[128,1024]{1,0:T(8,128)(2,1)S(1)}, bf16[128,1024]{1,0:T(8,128)(2,1)S(1)}, u32[]{:S(2)}, u32[]{:S(2)}) collective-permute-start(bf16[128,1024]{1,0:T(8,128)(2,1)S(1)} %get-tuple-element.3), channel_id=1, source_target_pairs={{10,14},{11,15},{12,0},{13,1},{14,10},{15,11},{0,12},{1,13},{26,30... | collective-permute-start | bytes 786440 | tf_op jit(solution)/shard_map/ppermute | solution.py:335
  16.2 4.2 %all-to-all-start = ((f32[16,1,128]{2,1,0:T(1,128)}), f32[16,1,128]{2,1,0:T(1,128)S(1)}, u32[]{:S(2)}, u32[]{:S(2)}) async-start(f32[16,1,128]{2,1,0:T(1,128)} %bitcast.1), calls=%async_computation | async-start | bytes 16384 | tf_op jit(solution)/shard_map/all_to_all | solution.py:371
  20.5 0.0 collective-permute-done.1.other_ref
  20.5 6.3 %all-to-all-done = f32[16,1,128]{2,1,0:T(1,128)S(1)} async-done(((f32[16,1,128]{2,1,0:T(1,128)}), f32[16,1,128]{2,1,0:T(1,128)S(1)}, u32[]{:S(2)}, u32[]{:S(2)}) %all-to-all-start) | async-done | bytes 8224 | tf_op jit(solution)/shard_map/all_to_all | solution.py:371
  26.8 0.6 %chain2.1 = f32[16,128]{1,0:T(8,128)S(1)} custom-call(s32[4,2]{1,0:T(4,128)S(1)} %copy.8.offsets_ref, bf16[128,2048]{1,0:T(8,128)(2,1)S(1)} %copy-done, bf16[128,1024]{1,0:T(8,128)(2,1)S(1)} %collective-permute-done.1.other_ref, s32[1,16]{1,0:T(1,128)S(1)} %copy-done.1, f32[16,128]{1,0:T(8,128)S(1)} %bitcast.12), custom_call_target="tpu_custom_call" | custom-call | tf_op jit(solution)/shard_map/chain2/pallas_call | solution.py:354
  27.4 10.1 %all_to_all.33 = f32[16,1,128]{2,1,0:T(1,128)S(1)} all-to-all(f32[16,1,128]{2,1,0:T(1,128)S(1)} %bitcast.18), channel_id=1, replica_groups=mesh['parts'=2,'tile'=16] {'tile'}, dimensions={0} | all-to-all | bytes 16384 | tf_op jit(solution)/shard_map/all_to_all | solution.py:371
  37.5 0.0 collective-permute-done.2.other_ref
  37.5 2.6 %chain3.1 = f32[16,128]{1,0:T(8,128)S(1)} custom-call(s32[4,2]{1,0:T(4,128)S(1)} %copy.8.offsets_ref, bf16[128,2048]{1,0:T(8,128)(2,1)S(1)} %copy-done, bf16[128,1024]{1,0:T(8,128)(2,1)S(1)} %collective-permute-done.2.other_ref, s32[1,16]{1,0:T(1,128)S(1)} %copy-done.1, f32[16,128]{1,0:T(8,128)S(1)} %bitcast.14), custom_call_target="tpu_custom_call" | custom-call | tf_op jit(solution)/shard_map/chain3/pallas_call | solution.py:354
  40.1 9.0 %all_to_all.34 = f32[16,1,128]{2,1,0:T(1,128)S(1)} all-to-all(f32[16,1,128]{2,1,0:T(1,128)S(1)} %bitcast.17), channel_id=1, replica_groups=mesh['parts'=2,'tile'=16] {'tile'}, dimensions={0} | all-to-all | bytes 16384 | tf_op jit(solution)/shard_map/all_to_all | solution.py:371
  49.1 2.5 %home.1 = (bf16[128,2048]{1,0:T(8,128)(2,1)}, f32[2,1,16]{2,1,0:T(1,128)}) custom-call(bf16[128,2048]{1,0:T(8,128)(2,1)S(1)} %copy-done, f32[16,128]{1,0:T(8,128)S(1)} %bitcast.13, f32[16,128]{1,0:T(8,128)S(1)} %bitcast.15, f32[16,128]{1,0:T(8,128)S(1)} %bitcast.16), custom_call_target="tpu_custom_call" | custom-call | tf_op jit(solution)/shard_map/home/pallas_call | solution.py:374
Async XLA Ops:
  0.7 2.7 %copy-start = (bf16[128,2048]{1,0:T(8,128)(2,1)S(1)}, bf16[128,2048]{1,0:T(8,128)(2,1)}, u32[]{:S(2)}) copy-start(bf16[128,2048]{1,0:T(8,128)(2,1)} %own_ref.7) | copy-start | bytes 1572868
  1.9 1.4 %copy-start.2 = (s32[4,2]{0,1:T(2,128)S(1)}, s32[4,2]{0,1:T(2,128)}, u32[]{:S(2)}) copy-start(s32[4,2]{0,1:T(2,128)} %param.5) | copy-start | bytes 100
  1.9 1.5 %collective-permute-start = (bf16[128,1024]{1,0:T(8,128)(2,1)S(1)}, bf16[128,1024]{1,0:T(8,128)(2,1)S(1)}, u32[]{:S(2)}, u32[]{:S(2)}) collective-permute-start(bf16[128,1024]{1,0:T(8,128)(2,1)S(1)} %get-tuple-element.6), channel_id=1, source_target_pairs={{2,6},{3,7},{4,8},{5,9},{6,2},{7,3},{8,4},{9,5},{18,22},{19,23},{2... | collective-permute-start | bytes 786440 | tf_op jit(solution)/shard_map/ppermute | solution.py:335
  2.6 0.8 %copy-start.1 = (s32[1,16]{1,0:T(1,128)S(1)}, s32[1,16]{1,0:T(1,128)}, u32[]{:S(2)}) copy-start(s32[1,16]{1,0:T(1,128)} %mask_ref.5) | copy-start | bytes 196
  2.6 17.9 %collective-permute-start.1 = (bf16[128,1024]{1,0:T(8,128)(2,1)S(1)}, bf16[128,1024]{1,0:T(8,128)(2,1)S(1)}, u32[]{:S(2)}, u32[]{:S(2)}) collective-permute-start(bf16[128,1024]{1,0:T(8,128)(2,1)S(1)} %get-tuple-element.5), channel_id=1, source_target_pairs={{6,10},{7,11},{8,12},{9,13},{10,6},{11,7},{12,8},{13,9},{22,26},{2... | collective-permute-start | bytes 786440 | tf_op jit(solution)/shard_map/ppermute | solution.py:335
  5.9 31.6 %collective-permute-start.2 = (bf16[128,1024]{1,0:T(8,128)(2,1)S(1)}, bf16[128,1024]{1,0:T(8,128)(2,1)S(1)}, u32[]{:S(2)}, u32[]{:S(2)}) collective-permute-start(bf16[128,1024]{1,0:T(8,128)(2,1)S(1)} %get-tuple-element.3), channel_id=1, source_target_pairs={{10,14},{11,15},{12,0},{13,1},{14,10},{15,11},{0,12},{1,13},{26,30... | collective-permute-start | bytes 786440 | tf_op jit(solution)/shard_map/ppermute | solution.py:335
  16.2 10.6 %all-to-all-start = ((f32[16,1,128]{2,1,0:T(1,128)}), f32[16,1,128]{2,1,0:T(1,128)S(1)}, u32[]{:S(2)}, u32[]{:S(2)}) async-start(f32[16,1,128]{2,1,0:T(1,128)} %bitcast.1), calls=%async_computation | async-start | bytes 16384 | tf_op jit(solution)/shard_map/all_to_all | solution.py:371

commit v8 on v7

--- a/solution.py
+++ b/solution.py
@@ -15,7 +15,7 @@
 LANES = 128
 WIDTH = 2 * HALF + 1
 MASK_LANE = 64
-GROUP = 8
+GROUP = 16
 THIRD = WIDTH // 3
 SPAN = PATCH // 2 + 16
 
@@ -251,19 +251,17 @@
             row_shift = own_row(relax(section_grid(refs[0][...], step - 1, rows), rows, nodes), row_index)
             base_ref[...], swing_ref[...] = kernels_of(row_shift, first, cols, nodes)
 
-            def warp_one(index, slot):
-                patch = jnp.where(is_upper, other_ref[:, columns(index)], own_ref[:, columns(index)])
-                prev_ref[index] = warp_indexed(patch, base_ref, swing_ref, index, cols)
-
-            looped(cols, warp_one)
+        def stage(index, slot):
+            patch = jnp.where(is_upper, other_ref[:, columns(index)], own_ref[:, columns(index)])
+            if step > 1:
+                patch = warp_indexed(patch, base_ref, swing_ref, index, cols)
+            prev_ref[index] = patch
+
+        looped(cols, stage)
 
         def one(index, slot):
-            other = other_ref[:, columns(index)]
-            own = jnp.where(is_upper, own_ref[:, columns(index + cols)], other)
-            if step > 1:
-                prev = prev_ref[index]
-            else:
-                prev = jnp.where(is_upper, other, own_ref[:, columns(index)])
+            own = jnp.where(is_upper, own_ref[:, columns(index + cols)], other_ref[:, columns(index)])
+            prev = prev_ref[index]
             own_corner, prev_corner = (x[0:1, 0:1].astype(f32) for x in (own, prev))
             corner_ref[0, pl.ds(index, 1), :] = jnp.broadcast_to(own_corner, (1, LANES))
             corner_ref[1, pl.ds(index, 1), :] = jnp.broadcast_to(prev_corner, (1, LANES))
@@ -358,7 +356,7 @@
             out_specs=vmem,
             scratch_shapes=[
                 pltpu.VMEM((half, THIRD, 2 * LANES), f32),
-                pltpu.VMEM((GROUP, 2, 8 * THIRD, LANES), f32),
+                pltpu.VMEM((half, 2, 8 * THIRD, LANES), f32),
                 pltpu.VMEM((4, half, 8, LANES), f32),
                 pltpu.VMEM((2, half, LANES), f32),
                 pltpu.VMEM((half, PATCH, PATCH), bf16),

time: 51.9 us -> 51.7 us (level)
  no operation moved by 1% of the time
where the time goes in v8:
time: 51.7 us; the launch traced here: 51.4 us
  blocking collectives  19.1 us (37%)
  starting transfers between devices  15.9 us (31%)
  Pallas kernels  7.94 us (15%)
  waiting for transfers between devices  6.33 us (12%)
  local copies, waits for them, and re-layouts  1.33 us (3%)
  between operations  0.77 us (1%)
    all_to_all x2, blocking collectives, shards(): gathered.append(lax.all_to_all(sent, 'tile', 0, 0, tiled=True))  19.1 us
    ppermute x3, starting transfers between devices, shards(): moved = lambda value, pairs: lax.ppermute(value, 'tile', pairs)  11.7 us
    all_to_all x1, waiting for transfers between devices, shards(): gathered.append(lax.all_to_all(sent, 'tile', 0, 0, tiled=True))  6.32 us
    pallas_call x3, Pallas kernels, shards(): pl.pallas_call(functools.partial(chain_kernel, step, rows, nodes), out_sh...  5.64 us
    all_to_all x1, starting transfers between devices, shards(): gathered.append(lax.all_to_all(sent, 'tile', 0, 0, tiled=True))  4.24 us
    pallas_call x1, Pallas kernels, shards(): pl.pallas_call(functools.partial(home_kernel, rows, nodes), out_shape=(ja...  2.3 us
    dynamic_slice x1, local copies, waits for them, and re-layouts, swapped(): sent = lax.dynamic_slice_in_dim(sections, start, half * PATCH, 1)  1.22 us
  transfers between devices with their start and end apart: 4, of which 1 were waited for; matrix products, arithmetic and copies ran while one was open for 0% of the time, Pallas kernels for 6%

profile of v8, /device:TPU:0, one launch (start us, length us, event | category | flops | bytes accessed | tf_op | source)
XLA Modules:
  0.0 51.4 jit_solution(13689548195157496792)
XLA Ops:
  0.7 0.0 copy-start
  0.7 1.2 %constant_dynamic-slice_fusion = (bf16[128,1024]{1,0:T(8,128)(2,1)S(1)}, bf16[128,1024]{1,0:T(8,128)(2,1)S(1)}, bf16[128,1024]{1,0:T(8,128)(2,1)S(1)}) fusion(bf16[128,2048]{1,0:T(8,128)(2,1)} %own_ref.7, s32[]{:T(128)S(6)} %select_n.28, s32[]{:T(128)S(6)} %select_n.27, s32[]{:T(128)S(6)} %select_n.26), kind=kLoop, calls=%fused_computation | loop fusion | bytes 1572876 | tf_op jit(solution)/shard_map/dynamic_slice | solution.py:337
  1.9 0.0 copy-start.2
  1.9 0.7 %collective-permute-start = (bf16[128,1024]{1,0:T(8,128)(2,1)S(1)}, bf16[128,1024]{1,0:T(8,128)(2,1)S(1)}, u32[]{:S(2)}, u32[]{:S(2)}) collective-permute-start(bf16[128,1024]{1,0:T(8,128)(2,1)S(1)} %get-tuple-element.6), channel_id=1, source_target_pairs={{2,6},{3,7},{4,8},{5,9},{6,2},{7,3},{8,4},{9,5},{18,22},{19,23},{2... | collective-permute-start | bytes 786440 | tf_op jit(solution)/shard_map/ppermute | solution.py:333
  2.6 0.0 copy-start.1
  2.6 0.7 %collective-permute-start.1 = (bf16[128,1024]{1,0:T(8,128)(2,1)S(1)}, bf16[128,1024]{1,0:T(8,128)(2,1)S(1)}, u32[]{:S(2)}, u32[]{:S(2)}) collective-permute-start(bf16[128,1024]{1,0:T(8,128)(2,1)S(1)} %get-tuple-element.5), channel_id=1, source_target_pairs={{6,10},{7,11},{8,12},{9,13},{10,6},{11,7},{12,8},{13,9},{22,26},{2... | collective-permute-start | bytes 786440 | tf_op jit(solution)/shard_map/ppermute | solution.py:333
  3.3 0.0 copy-done.2
  3.3 0.1 copy.8.offsets_ref
  3.4 0.0 collective-permute-done.other_ref
  3.4 0.0 copy-done
  3.4 0.0 copy-done.1
  3.4 2.5 %chain1.1 = f32[16,128]{1,0:T(8,128)} custom-call(s32[4,2]{1,0:T(4,128)S(1)} %copy.8.offsets_ref, bf16[128,2048]{1,0:T(8,128)(2,1)S(1)} %copy-done, bf16[128,1024]{1,0:T(8,128)(2,1)S(1)} %collective-permute-done.other_ref, s32[1,16]{1,0:T(1,128)S(1)} %copy-done.1), custom_call_target="tpu_custom_call" | custom-call | tf_op jit(solution)/shard_map/chain1/pallas_call | solution.py:352
  5.9 10.3 %collective-permute-start.2 = (bf16[128,1024]{1,0:T(8,128)(2,1)S(1)}, bf16[128,1024]{1,0:T(8,128)(2,1)S(1)}, u32[]{:S(2)}, u32[]{:S(2)}) collective-permute-start(bf16[128,1024]{1,0:T(8,128)(2,1)S(1)} %get-tuple-element.3), channel_id=1, source_target_pairs={{10,14},{11,15},{12,0},{13,1},{14,10},{15,11},{0,12},{1,13},{26,30... | collective-permute-start | bytes 786440 | tf_op jit(solution)/shard_map/ppermute | solution.py:333
  16.2 4.2 %all-to-all-start = ((f32[16,1,128]{2,1,0:T(1,128)}), f32[16,1,128]{2,1,0:T(1,128)S(1)}, u32[]{:S(2)}, u32[]{:S(2)}) async-start(f32[16,1,128]{2,1,0:T(1,128)} %bitcast.1), calls=%async_computation | async-start | bytes 16384 | tf_op jit(solution)/shard_map/all_to_all | solution.py:369
  20.4 0.0 collective-permute-done.1.other_ref
  20.5 6.3 %all-to-all-done = f32[16,1,128]{2,1,0:T(1,128)S(1)} async-done(((f32[16,1,128]{2,1,0:T(1,128)}), f32[16,1,128]{2,1,0:T(1,128)S(1)}, u32[]{:S(2)}, u32[]{:S(2)}) %all-to-all-start) | async-done | bytes 8224 | tf_op jit(solution)/shard_map/all_to_all | solution.py:369
  26.8 0.6 %chain2.1 = f32[16,128]{1,0:T(8,128)S(1)} custom-call(s32[4,2]{1,0:T(4,128)S(1)} %copy.8.offsets_ref, bf16[128,2048]{1,0:T(8,128)(2,1)S(1)} %copy-done, bf16[128,1024]{1,0:T(8,128)(2,1)S(1)} %collective-permute-done.1.other_ref, s32[1,16]{1,0:T(1,128)S(1)} %copy-done.1, f32[16,128]{1,0:T(8,128)S(1)} %bitcast.12), custom_call_target="tpu_custom_call" | custom-call | tf_op jit(solution)/shard_map/chain2/pallas_call | solution.py:352
  27.4 10.1 %all_to_all.33 = f32[16,1,128]{2,1,0:T(1,128)S(1)} all-to-all(f32[16,1,128]{2,1,0:T(1,128)S(1)} %bitcast.18), channel_id=1, replica_groups=mesh['parts'=2,'tile'=16] {'tile'}, dimensions={0} | all-to-all | bytes 16384 | tf_op jit(solution)/shard_map/all_to_all | solution.py:369
  37.5 0.0 collective-permute-done.2.other_ref
  37.5 2.6 %chain3.1 = f32[16,128]{1,0:T(8,128)S(1)} custom-call(s32[4,2]{1,0:T(4,128)S(1)} %copy.8.offsets_ref, bf16[128,2048]{1,0:T(8,128)(2,1)S(1)} %copy-done, bf16[128,1024]{1,0:T(8,128)(2,1)S(1)} %collective-permute-done.2.other_ref, s32[1,16]{1,0:T(1,128)S(1)} %copy-done.1, f32[16,128]{1,0:T(8,128)S(1)} %bitcast.14), custom_call_target="tpu_custom_call" | custom-call | tf_op jit(solution)/shard_map/chain3/pallas_call | solution.py:352
  40.1 9.0 %all_to_all.34 = f32[16,1,128]{2,1,0:T(1,128)S(1)} all-to-all(f32[16,1,128]{2,1,0:T(1,128)S(1)} %bitcast.17), channel_id=1, replica_groups=mesh['parts'=2,'tile'=16] {'tile'}, dimensions={0} | all-to-all | bytes 16384 | tf_op jit(solution)/shard_map/all_to_all | solution.py:369
  49.1 2.3 %home.1 = (bf16[128,2048]{1,0:T(8,128)(2,1)}, f32[2,1,16]{2,1,0:T(1,128)}) custom-call(bf16[128,2048]{1,0:T(8,128)(2,1)S(1)} %copy-done, f32[16,128]{1,0:T(8,128)S(1)} %bitcast.13, f32[16,128]{1,0:T(8,128)S(1)} %bitcast.15, f32[16,128]{1,0:T(8,128)S(1)} %bitcast.16), custom_call_target="tpu_custom_call" | custom-call | tf_op jit(solution)/shard_map/home/pallas_call | solution.py:372
Async XLA Ops:
  0.7 2.7 %copy-start = (bf16[128,2048]{1,0:T(8,128)(2,1)S(1)}, bf16[128,2048]{1,0:T(8,128)(2,1)}, u32[]{:S(2)}) copy-start(bf16[128,2048]{1,0:T(8,128)(2,1)} %own_ref.7) | copy-start | bytes 1572868
  1.9 1.4 %copy-start.2 = (s32[4,2]{0,1:T(2,128)S(1)}, s32[4,2]{0,1:T(2,128)}, u32[]{:S(2)}) copy-start(s32[4,2]{0,1:T(2,128)} %param.5) | copy-start | bytes 100
  1.9 1.5 %collective-permute-start = (bf16[128,1024]{1,0:T(8,128)(2,1)S(1)}, bf16[128,1024]{1,0:T(8,128)(2,1)S(1)}, u32[]{:S(2)}, u32[]{:S(2)}) collective-permute-start(bf16[128,1024]{1,0:T(8,128)(2,1)S(1)} %get-tuple-element.6), channel_id=1, source_target_pairs={{2,6},{3,7},{4,8},{5,9},{6,2},{7,3},{8,4},{9,5},{18,22},{19,23},{2... | collective-permute-start | bytes 786440 | tf_op jit(solution)/shard_map/ppermute | solution.py:333
  2.6 0.8 %copy-start.1 = (s32[1,16]{1,0:T(1,128)S(1)}, s32[1,16]{1,0:T(1,128)}, u32[]{:S(2)}) copy-start(s32[1,16]{1,0:T(1,128)} %mask_ref.5) | copy-start | bytes 196
  2.6 17.8 %collective-permute-start.1 = (bf16[128,1024]{1,0:T(8,128)(2,1)S(1)}, bf16[128,1024]{1,0:T(8,128)(2,1)S(1)}, u32[]{:S(2)}, u32[]{:S(2)}) collective-permute-start(bf16[128,1024]{1,0:T(8,128)(2,1)S(1)} %get-tuple-element.5), channel_id=1, source_target_pairs={{6,10},{7,11},{8,12},{9,13},{10,6},{11,7},{12,8},{13,9},{22,26},{2... | collective-permute-start | bytes 786440 | tf_op jit(solution)/shard_map/ppermute | solution.py:333
  5.9 31.6 %collective-permute-start.2 = (bf16[128,1024]{1,0:T(8,128)(2,1)S(1)}, bf16[128,1024]{1,0:T(8,128)(2,1)S(1)}, u32[]{:S(2)}, u32[]{:S(2)}) collective-permute-start(bf16[128,1024]{1,0:T(8,128)(2,1)S(1)} %get-tuple-element.3), channel_id=1, source_target_pairs={{10,14},{11,15},{12,0},{13,1},{14,10},{15,11},{0,12},{1,13},{26,30... | collective-permute-start | bytes 786440 | tf_op jit(solution)/shard_map/ppermute | solution.py:333
  16.2 10.6 %all-to-all-start = ((f32[16,1,128]{2,1,0:T(1,128)}), f32[16,1,128]{2,1,0:T(1,128)S(1)}, u32[]{:S(2)}, u32[]{:S(2)}) async-start(f32[16,1,128]{2,1,0:T(1,128)} %bitcast.1), calls=%async_computation | async-start | bytes 16384 | tf_op jit(solution)/shard_map/all_to_all | solution.py:369

commit v9 on v8

--- a/solution.py
+++ b/solution.py
@@ -332,19 +332,20 @@
     group = (lax.axis_index("tile") + count - rows // 2) % count // rows
     moved = lambda value, pairs: lax.ppermute(value, "tile", pairs)
 
-    def swapped(lower, after=None):
+    def half_of(source, lower):
         start = jnp.where(group == lower, half * PATCH, 0)
-        sent = lax.dynamic_slice_in_dim(sections, start, half * PATCH, 1)
-        if after is not None:
-            sent, after = lax.optimization_barrier((sent, after))
+        return lax.dynamic_slice_in_dim(source, start, half * PATCH, 1)
+
+    def swapped(sent, lower):
         ends = [(place(lower, i), place(lower + 1, i)) for i in range(rows)]
         return moved(sent, ends + [(d, s) for s, d in ends])
 
     half = nodes // 2
-    others = [swapped(0), swapped(1)]
+    first_half = half_of(sections, 0)
+    source, first_half = lax.optimization_barrier((sections, first_half))
+    others = [swapped(first_half, 0), swapped(half_of(source, 1), 1)]
 
     vmem = pl.BlockSpec(memory_space=pltpu.VMEM)
-    smem = pl.BlockSpec(memory_space=pltpu.SMEM)
     params = pltpu.CompilerParams(vmem_limit_bytes=16 * 2**20)
     gathered = []
     for step in range(1, SECTIONS):
@@ -352,7 +353,7 @@
         sent = pl.pallas_call(
             functools.partial(chain_kernel, step, rows, nodes),
             out_shape=jax.ShapeDtypeStruct((count, LANES), f32),
-            in_specs=[smem] + [vmem] * (3 + len(extra)),
+            in_specs=[vmem] * (4 + len(extra)),
             out_specs=vmem,
             scratch_shapes=[
                 pltpu.VMEM((half, THIRD, 2 * LANES), f32),
@@ -368,7 +369,8 @@
         )(coarse_offsets, sections, others[step - 1], valid_mask, *extra)
         gathered.append(lax.all_to_all(sent, "tile", 0, 0, tiled=True))
         if step + 1 < SECTIONS - 1:
-            others.append(swapped(step + 1, sent))
+            later, sent = lax.optimization_barrier((half_of(source, step + 1), sent))
+            others.append(swapped(later, step + 1))
     return pl.pallas_call(
         functools.partial(home_kernel, rows, nodes),
         out_shape=(

time: 51.7 us -> 49.7 us (0.961)
  Pallas kernels: 7.94 us -> 6.12 us
    pallas_call x3, Pallas kernels: 5.64 us -> 3.82 us  [shards(): pl.pallas_call(functools.partial(chain_kernel, step, rows, nodes), out_sh...]
    dynamic_slice x1 -> x2, local copies, waits for them, and re-layouts: 1.22 us -> 1.06 us  [half_of(): return lax.dynamic_slice_in_dim(source, start, half * PATCH, 1)]
  transfers between devices with their start and end apart: 4 -> 4, of which waited for: 1 -> 1; matrix products, arithmetic and copies ran while one was open for 0% -> 0% of each run, Pallas kernels for 6% -> 4%
where the time goes in v9:
time: 49.7 us; the launch traced here: 49.4 us
  blocking collectives  19.2 us (39%)
  starting transfers between devices  15.8 us (32%)
  waiting for transfers between devices  6.33 us (13%)
  Pallas kernels  6.12 us (12%)
  local copies, waits for them, and re-layouts  1.17 us (2%)
  between operations  0.78 us (2%)
    all_to_all x2, blocking collectives, shards(): gathered.append(lax.all_to_all(sent, 'tile', 0, 0, tiled=True))  19.2 us
    ppermute x3, starting transfers between devices, shards(): moved = lambda value, pairs: lax.ppermute(value, 'tile', pairs)  11.7 us
    all_to_all x1, waiting for transfers between devices, shards(): gathered.append(lax.all_to_all(sent, 'tile', 0, 0, tiled=True))  6.32 us
    all_to_all x1, starting transfers between devices, shards(): gathered.append(lax.all_to_all(sent, 'tile', 0, 0, tiled=True))  4.16 us
    pallas_call x3, Pallas kernels, shards(): pl.pallas_call(functools.partial(chain_kernel, step, rows, nodes), out_sh...  3.82 us
    pallas_call x1, Pallas kernels, shards(): pl.pallas_call(functools.partial(home_kernel, rows, nodes), out_shape=(ja...  2.3 us
    dynamic_slice x2, local copies, waits for them, and re-layouts, half_of(): return lax.dynamic_slice_in_dim(source, start, half * PATCH, 1)  1.06 us
  transfers between devices with their start and end apart: 4, of which 1 were waited for; matrix products, arithmetic and copies ran while one was open for 0% of the time, Pallas kernels for 4%

profile of v9, /device:TPU:0, one launch (start us, length us, event | category | flops | bytes accessed | tf_op | source)
XLA Modules:
  0.0 49.4 jit_solution(12798662734039161975)
XLA Ops:
  0.6 0.0 copy-start
  0.7 1.0 %constant_dynamic-slice_fusion.2 = bf16[128,1024]{1,0:T(8,128)(2,1)S(1)} fusion(bf16[128,2048]{1,0:T(8,128)(2,1)} %own_ref.7, s32[]{:T(128)S(6)} %select_n.26), kind=kLoop, calls=%fused_computation.2 | loop fusion | bytes 524292 | tf_op jit(solution)/shard_map/dynamic_slice | solution.py:337
  1.7 0.7 %collective-permute-start = (bf16[128,1024]{1,0:T(8,128)(2,1)S(1)}, bf16[128,1024]{1,0:T(8,128)(2,1)S(1)}, u32[]{:S(2)}, u32[]{:S(2)}) collective-permute-start(bf16[128,1024]{1,0:T(8,128)(2,1)S(1)} %constant_dynamic-slice_fusion.2), channel_id=1, source_target_pairs={{2,6},{3,7},{4,8},{5,9},{6,2},{7,3},{8,4},{9,5},{18,22},{19,23},{2... | collective-permute-start | bytes 786440 | tf_op jit(solution)/shard_map/ppermute | solution.py:333
  2.4 0.0 copy-done
  2.5 0.0 copy-start.2
  2.5 0.0 copy-start.1
  2.5 0.7 %collective-permute-start.1 = (bf16[128,1024]{1,0:T(8,128)(2,1)S(1)}, bf16[128,1024]{1,0:T(8,128)(2,1)S(1)}, u32[]{:S(2)}, u32[]{:S(2)}) collective-permute-start(bf16[128,1024]{1,0:T(8,128)(2,1)S(1)} %get-tuple-element.9), channel_id=1, source_target_pairs={{6,10},{7,11},{8,12},{9,13},{10,6},{11,7},{12,8},{13,9},{22,26},{2... | collective-permute-start | bytes 786440 | tf_op jit(solution)/shard_map/ppermute | solution.py:333
  3.2 0.0 copy-done.2
  3.2 0.1 copy.8.offsets_ref
  3.3 0.0 collective-permute-done.other_ref
  3.3 0.0 copy-done.1
  3.3 1.8 %chain1.1 = f32[16,128]{1,0:T(8,128)} custom-call(s32[4,2]{1,0:T(4,128)S(1)} %copy.8.offsets_ref, bf16[128,2048]{1,0:T(8,128)(2,1)S(1)} %copy-done, bf16[128,1024]{1,0:T(8,128)(2,1)S(1)} %collective-permute-done.other_ref, s32[1,16]{1,0:T(1,128)S(1)} %copy-done.1), custom_call_target="tpu_custom_call" | custom-call | tf_op jit(solution)/shard_map/chain1/pallas_call | solution.py:353
  5.1 10.3 %collective-permute-start.2 = (bf16[128,1024]{1,0:T(8,128)(2,1)S(1)}, bf16[128,1024]{1,0:T(8,128)(2,1)S(1)}, u32[]{:S(2)}, u32[]{:S(2)}) collective-permute-start(bf16[128,1024]{1,0:T(8,128)(2,1)S(1)} %get-tuple-element.7), channel_id=1, source_target_pairs={{10,14},{11,15},{12,0},{13,1},{14,10},{15,11},{0,12},{1,13},{26,30... | collective-permute-start | bytes 786440 | tf_op jit(solution)/shard_map/ppermute | solution.py:333
  15.4 4.2 %all-to-all-start = ((f32[16,1,128]{2,1,0:T(1,128)}), f32[16,1,128]{2,1,0:T(1,128)S(1)}, u32[]{:S(2)}, u32[]{:S(2)}) async-start(f32[16,1,128]{2,1,0:T(1,128)} %bitcast.1), calls=%async_computation | async-start | bytes 16384 | tf_op jit(solution)/shard_map/all_to_all | solution.py:370
  19.5 0.0 collective-permute-done.1.other_ref
  19.5 6.3 %all-to-all-done = f32[16,1,128]{2,1,0:T(1,128)S(1)} async-done(((f32[16,1,128]{2,1,0:T(1,128)}), f32[16,1,128]{2,1,0:T(1,128)S(1)}, u32[]{:S(2)}, u32[]{:S(2)}) %all-to-all-start) | async-done | bytes 8224 | tf_op jit(solution)/shard_map/all_to_all | solution.py:370
  25.9 10.2 %all_to_all.33 = f32[16,1,128]{2,1,0:T(1,128)S(1)} all-to-all(f32[16,1,128]{2,1,0:T(1,128)S(1)} %bitcast.18), channel_id=1, replica_groups=mesh['parts'=2,'tile'=16] {'tile'}, dimensions={0} | all-to-all | bytes 16384 | tf_op jit(solution)/shard_map/all_to_all | solution.py:370
  36.1 0.0 collective-permute-done.2.other_ref
  36.1 2.0 %chain3.1 = f32[16,128]{1,0:T(8,128)S(1)} custom-call(s32[4,2]{1,0:T(4,128)S(1)} %copy.8.offsets_ref, bf16[128,2048]{1,0:T(8,128)(2,1)S(1)} %copy-done, bf16[128,1024]{1,0:T(8,128)(2,1)S(1)} %collective-permute-done.2.other_ref, s32[1,16]{1,0:T(1,128)S(1)} %copy-done.1, f32[16,128]{1,0:T(8,128)S(1)} %bitcast.14), custom_call_target="tpu_custom_call" | custom-call | tf_op jit(solution)/shard_map/chain3/pallas_call | solution.py:353
  38.1 9.0 %all_to_all.34 = f32[16,1,128]{2,1,0:T(1,128)S(1)} all-to-all(f32[16,1,128]{2,1,0:T(1,128)S(1)} %bitcast.17), channel_id=1, replica_groups=mesh['parts'=2,'tile'=16] {'tile'}, dimensions={0} | all-to-all | bytes 16384 | tf_op jit(solution)/shard_map/all_to_all | solution.py:370
  47.1 2.3 %home.1 = (bf16[128,2048]{1,0:T(8,128)(2,1)}, f32[2,1,16]{2,1,0:T(1,128)}) custom-call(bf16[128,2048]{1,0:T(8,128)(2,1)S(1)} %copy-done, f32[16,128]{1,0:T(8,128)S(1)} %bitcast.13, f32[16,128]{1,0:T(8,128)S(1)} %bitcast.15, f32[16,128]{1,0:T(8,128)S(1)} %bitcast.16), custom_call_target="tpu_custom_call" | custom-call | tf_op jit(solution)/shard_map/home/pallas_call | solution.py:374
  (2 shorter events, 0.0 us)
Async XLA Ops:
  0.6 1.8 %copy-start = (bf16[128,2048]{1,0:T(8,128)(2,1)S(1)}, bf16[128,2048]{1,0:T(8,128)(2,1)}, u32[]{:S(2)}) copy-start(bf16[128,2048]{1,0:T(8,128)(2,1)} %own_ref.7) | copy-start | bytes 1572868
  1.7 1.6 %collective-permute-start = (bf16[128,1024]{1,0:T(8,128)(2,1)S(1)}, bf16[128,1024]{1,0:T(8,128)(2,1)S(1)}, u32[]{:S(2)}, u32[]{:S(2)}) collective-permute-start(bf16[128,1024]{1,0:T(8,128)(2,1)S(1)} %constant_dynamic-slice_fusion.2), channel_id=1, source_target_pairs={{2,6},{3,7},{4,8},{5,9},{6,2},{7,3},{8,4},{9,5},{18,22},{19,23},{2... | collective-permute-start | bytes 786440 | tf_op jit(solution)/shard_map/ppermute | solution.py:333
  2.5 0.7 %copy-start.2 = (s32[4,2]{0,1:T(2,128)S(1)}, s32[4,2]{0,1:T(2,128)}, u32[]{:S(2)}) copy-start(s32[4,2]{0,1:T(2,128)} %param.5) | copy-start | bytes 100
  2.5 0.8 %copy-start.1 = (s32[1,16]{1,0:T(1,128)S(1)}, s32[1,16]{1,0:T(1,128)}, u32[]{:S(2)}) copy-start(s32[1,16]{1,0:T(1,128)} %mask_ref.5) | copy-start | bytes 196
  2.5 17.1 %collective-permute-start.1 = (bf16[128,1024]{1,0:T(8,128)(2,1)S(1)}, bf16[128,1024]{1,0:T(8,128)(2,1)S(1)}, u32[]{:S(2)}, u32[]{:S(2)}) collective-permute-start(bf16[128,1024]{1,0:T(8,128)(2,1)S(1)} %get-tuple-element.9), channel_id=1, source_target_pairs={{6,10},{7,11},{8,12},{9,13},{10,6},{11,7},{12,8},{13,9},{22,26},{2... | collective-permute-start | bytes 786440 | tf_op jit(solution)/shard_map/ppermute | solution.py:333
  5.1 31.0 %collective-permute-start.2 = (bf16[128,1024]{1,0:T(8,128)(2,1)S(1)}, bf16[128,1024]{1,0:T(8,128)(2,1)S(1)}, u32[]{:S(2)}, u32[]{:S(2)}) collective-permute-start(bf16[128,1024]{1,0:T(8,128)(2,1)S(1)} %get-tuple-element.7), channel_id=1, source_target_pairs={{10,14},{11,15},{12,0},{13,1},{14,10},{15,11},{0,12},{1,13},{26,30... | collective-permute-start | bytes 786440 | tf_op jit(solution)/shard_map/ppermute | solution.py:333
  15.4 10.5 %all-to-all-start = ((f32[16,1,128]{2,1,0:T(1,128)}), f32[16,1,128]{2,1,0:T(1,128)S(1)}, u32[]{:S(2)}, u32[]{:S(2)}) async-start(f32[16,1,128]{2,1,0:T(1,128)} %bitcast.1), calls=%async_computation | async-start | bytes 16384 | tf_op jit(solution)/shard_map/all_to_all | solution.py:370

commit v10 on v9

--- a/solution.py
+++ b/solution.py
@@ -153,7 +153,7 @@
     return spot // SPAN, 8 - spot % SPAN
 
 
-def correlate(own, prev, level, column_offset, band_ref):
+def correlate(own, prev, level, column_offset, put):
     own32, prev32 = own.astype(f32), prev.astype(f32)
     half = PATCH // 2
     left, right = [], []
@@ -183,13 +183,14 @@
             kept = pltpu.roll(kept, 2 * LANES - 8 * k, 1) if k else kept
             band = kept if band is None else band + kept
         band = jnp.where(unused, 0.0, band)
-        for side in range(2):
-            band_ref[side, 8 * i : 8 * i + 8, :] = band[:, side * LANES : (side + 1) * LANES]
+        put(i, band)
+
+
+def band_sum(band_ref, first, cols):
     out = None
     for row in range(8):
-        part = jnp.concatenate(
-            [band_ref[side, pl.ds(row, THIRD, stride=8), :] for side in range(2)], axis=1
-        )
+        rows = pl.ds(first + row, cols, stride=8)
+        part = jnp.concatenate([band_ref[side, rows, :] for side in range(2)], axis=1)
         part = pltpu.roll(part, 2 * LANES - row, 1) if row else part
         out = part if out is None else out + part
     back = lambda lanes: pltpu.roll(out, 2 * LANES - lanes, 1)
@@ -214,6 +215,10 @@
         body(0, 0)
     else:
         lax.fori_loop(0, count // width, body, 0)
+
+
+def rows_of(index):
+    return pl.ds(index * 8 if isinstance(index, int) else pl.multiple_of(index * 8, 8), 8)
 
 
 def columns(index):
@@ -234,7 +239,7 @@
 
 
 def chain_kernel(step, rows, nodes, offsets_ref, own_ref, other_ref, mask_ref, *refs):
-    out_ref, score_ref, band_ref, sums_ref, corner_ref, prev_ref, base_ref, swing_ref = refs[-8:]
+    out_ref, band_ref, sums_ref, corner_ref, prev_ref, base_ref, swing_ref = refs[-7:]
     cols = nodes // 2
     count = lax.axis_size("tile")
     rotated = (lax.axis_index("tile") + count - rows // 2) % count
@@ -267,30 +272,41 @@
             corner_ref[1, pl.ds(index, 1), :] = jnp.broadcast_to(prev_corner, (1, LANES))
             sums = moments(own, own_corner) + moments(prev, prev_corner)
             for k, value in enumerate(sums):
-                sums_ref[k, pl.ds(index, 1)] = value[None]
+                sums_ref[k, rows_of(index), :] = value
             level = own_corner * prev_corner
-            score_ref[pl.ds(index, 1)] = correlate(own, prev, level, col_offset, band_ref.at[slot])[None]
+
+            def put(third, band):
+                for side in range(2):
+                    band_ref[side, rows_of(third * cols + index), :] = band[:, side * LANES : (side + 1) * LANES]
+
+            correlate(own, prev, level, col_offset, put)
 
         looped(cols, one)
-        reduce = lambda value: jnp.sum(jnp.sum(value, axis=1), axis=1, keepdims=True)
-        own_sum, own_square, prev_sum, prev_square = (reduce(sums_ref[k]) * (1.0 / area) for k in range(4))
+        reduce = lambda value: jnp.sum(value, axis=1, keepdims=True)
+        mean = lambda k: reduce(
+            functools.reduce(jnp.add, [sums_ref[k, pl.ds(row, cols, stride=8), :] for row in range(8)])
+        ) * (1.0 / area)
+        own_sum, own_square, prev_sum, prev_square = (mean(k) for k in range(4))
         spread = jnp.sqrt(
             (jnp.maximum(own_square - own_sum * own_sum, 0.0) + 1e-5)
             * (jnp.maximum(prev_square - prev_sum * prev_sum, 0.0) + 1e-5)
         )
         scale = sharpness / area / spread
         level = corner_ref[0] * prev_sum + corner_ref[1] * own_sum + own_sum * prev_sum
-        shape = (cols, THIRD, 2 * LANES)
-        third, row_lag = lag_layout(shape, 2)
-        col_lag = iota(shape, 1) + THIRD * third - HALF + col_offset
+        level = jnp.concatenate([level, level], axis=1) * area
+        third, row_lag = lag_layout((cols, 2 * LANES), 1)
         inside = (jnp.abs(row_lag - row_offset) <= HALF) & (third < THIRD)
-        level = jnp.concatenate([level, level], axis=1) * area
-        scale = jnp.broadcast_to(scale, (cols, 2 * LANES))
-        score = (score_ref[...] - level[:, None, :]) * scale[:, None, :]
-        weights = jnp.where(inside, jnp.exp(jnp.where(inside, score, 0.0)), 0.0)
-        inverse = 1.0 / reduce(weights)
-        flow_row = reduce(weights * row_lag.astype(f32)) * inverse
-        flow_col = reduce(weights * col_lag.astype(f32)) * inverse
+        weight = row_moment = col_moment = 0.0
+        for i in range(THIRD):
+            score = (band_sum(band_ref, 8 * cols * i, cols) - level) * scale
+            weights = jnp.where(inside, jnp.exp(jnp.where(inside, score, 0.0)), 0.0)
+            col_lag = i + THIRD * third - HALF + col_offset
+            weight = weight + weights
+            row_moment = row_moment + weights * row_lag.astype(f32)
+            col_moment = col_moment + weights * col_lag.astype(f32)
+        inverse = 1.0 / reduce(weight)
+        flow_row = reduce(row_moment) * inverse
+        flow_col = reduce(col_moment) * inverse
         shape = (cols, LANES)
         node, lane = iota(shape, 0) + first, iota(shape, 1)
         sent = jnp.where(lane == node, flow_row, jnp.where(lane == node + nodes, flow_col, 0.0))
@@ -356,9 +372,8 @@
             in_specs=[vmem] * (4 + len(extra)),
             out_specs=vmem,
             scratch_shapes=[
-                pltpu.VMEM((half, THIRD, 2 * LANES), f32),
-                pltpu.VMEM((half, 2, 8 * THIRD, LANES), f32),
-                pltpu.VMEM((4, half, 8, LANES), f32),
+                pltpu.VMEM((2, THIRD * half * 8, LANES), f32),
+                pltpu.VMEM((4, half * 8, LANES), f32),
                 pltpu.VMEM((2, half, LANES), f32),
                 pltpu.VMEM((half, PATCH, PATCH), bf16),
                 pltpu.VMEM((2 * half, LANES), f32),

time: 49.7 us -> 49.5 us (level)
  transfers between devices with their start and end apart: 4 -> 4, of which waited for: 1 -> 1; matrix products, arithmetic and copies ran while one was open for 0% -> 0% of each run, Pallas kernels for 4% -> 3%
where the time goes in v10:
time: 49.5 us; the launch traced here: 49.2 us
  blocking collectives  19.1 us (39%)
  starting transfers between devices  15.8 us (32%)
  waiting for transfers between devices  6.33 us (13%)
  Pallas kernels  5.99 us (12%)
  local copies, waits for them, and re-layouts  1.17 us (2%)
  between operations  0.78 us (2%)
    all_to_all x2, blocking collectives, shards(): gathered.append(lax.all_to_all(sent, 'tile', 0, 0, tiled=True))  19.1 us
    ppermute x3, starting transfers between devices, shards(): moved = lambda value, pairs: lax.ppermute(value, 'tile', pairs)  11.7 us
    all_to_all x1, waiting for transfers between devices, shards(): gathered.append(lax.all_to_all(sent, 'tile', 0, 0, tiled=True))  6.32 us
    all_to_all x1, starting transfers between devices, shards(): gathered.append(lax.all_to_all(sent, 'tile', 0, 0, tiled=True))  4.15 us
    pallas_call x3, Pallas kernels, shards(): pl.pallas_call(functools.partial(chain_kernel, step, rows, nodes), out_sh...  3.69 us
    pallas_call x1, Pallas kernels, shards(): pl.pallas_call(functools.partial(home_kernel, rows, nodes), out_shape=(ja...  2.3 us
    dynamic_slice x2, local copies, waits for them, and re-layouts, half_of(): return lax.dynamic_slice_in_dim(source, start, half * PATCH, 1)  1.06 us
  transfers between devices with their start and end apart: 4, of which 1 were waited for; matrix products, arithmetic and copies ran while one was open for 0% of the time, Pallas kernels for 3%

profile of v10, /device:TPU:0, one launch (start us, length us, event | category | flops | bytes accessed | tf_op | source)
XLA Modules:
  0.0 49.2 jit_solution(9391496655341814782)
XLA Ops:
  0.6 0.0 copy-start
  0.7 1.0 %constant_dynamic-slice_fusion.2 = bf16[128,1024]{1,0:T(8,128)(2,1)S(1)} fusion(bf16[128,2048]{1,0:T(8,128)(2,1)} %own_ref.7, s32[]{:T(128)S(6)} %select_n.26), kind=kLoop, calls=%fused_computation.2 | loop fusion | bytes 524292 | tf_op jit(solution)/shard_map/dynamic_slice | solution.py:353
  1.7 0.7 %collective-permute-start = (bf16[128,1024]{1,0:T(8,128)(2,1)S(1)}, bf16[128,1024]{1,0:T(8,128)(2,1)S(1)}, u32[]{:S(2)}, u32[]{:S(2)}) collective-permute-start(bf16[128,1024]{1,0:T(8,128)(2,1)S(1)} %constant_dynamic-slice_fusion.2), channel_id=1, source_target_pairs={{2,6},{3,7},{4,8},{5,9},{6,2},{7,3},{8,4},{9,5},{18,22},{19,23},{2... | collective-permute-start | bytes 786440 | tf_op jit(solution)/shard_map/ppermute | solution.py:349
  2.4 0.0 copy-done
  2.5 0.0 copy-start.2
  2.5 0.0 copy-start.1
  2.5 0.7 %collective-permute-start.1 = (bf16[128,1024]{1,0:T(8,128)(2,1)S(1)}, bf16[128,1024]{1,0:T(8,128)(2,1)S(1)}, u32[]{:S(2)}, u32[]{:S(2)}) collective-permute-start(bf16[128,1024]{1,0:T(8,128)(2,1)S(1)} %get-tuple-element.9), channel_id=1, source_target_pairs={{6,10},{7,11},{8,12},{9,13},{10,6},{11,7},{12,8},{13,9},{22,26},{2... | collective-permute-start | bytes 786440 | tf_op jit(solution)/shard_map/ppermute | solution.py:349
  3.2 0.0 copy-done.2
  3.2 0.1 copy.8.offsets_ref
  3.3 0.0 collective-permute-done.other_ref
  3.3 0.0 copy-done.1
  3.3 1.7 %chain1.1 = f32[16,128]{1,0:T(8,128)} custom-call(s32[4,2]{1,0:T(4,128)S(1)} %copy.8.offsets_ref, bf16[128,2048]{1,0:T(8,128)(2,1)S(1)} %copy-done, bf16[128,1024]{1,0:T(8,128)(2,1)S(1)} %collective-permute-done.other_ref, s32[1,16]{1,0:T(1,128)S(1)} %copy-done.1), custom_call_target="tpu_custom_call" | custom-call | tf_op jit(solution)/shard_map/chain1/pallas_call | solution.py:369
  5.0 10.3 %collective-permute-start.2 = (bf16[128,1024]{1,0:T(8,128)(2,1)S(1)}, bf16[128,1024]{1,0:T(8,128)(2,1)S(1)}, u32[]{:S(2)}, u32[]{:S(2)}) collective-permute-start(bf16[128,1024]{1,0:T(8,128)(2,1)S(1)} %get-tuple-element.7), channel_id=1, source_target_pairs={{10,14},{11,15},{12,0},{13,1},{14,10},{15,11},{0,12},{1,13},{26,30... | collective-permute-start | bytes 786440 | tf_op jit(solution)/shard_map/ppermute | solution.py:349
  15.3 4.2 %all-to-all-start = ((f32[16,1,128]{2,1,0:T(1,128)}), f32[16,1,128]{2,1,0:T(1,128)S(1)}, u32[]{:S(2)}, u32[]{:S(2)}) async-start(f32[16,1,128]{2,1,0:T(1,128)} %bitcast.1), calls=%async_computation | async-start | bytes 16384 | tf_op jit(solution)/shard_map/all_to_all | solution.py:385
  19.5 0.0 collective-permute-done.1.other_ref
  19.5 6.3 %all-to-all-done = f32[16,1,128]{2,1,0:T(1,128)S(1)} async-done(((f32[16,1,128]{2,1,0:T(1,128)}), f32[16,1,128]{2,1,0:T(1,128)S(1)}, u32[]{:S(2)}, u32[]{:S(2)}) %all-to-all-start) | async-done | bytes 8224 | tf_op jit(solution)/shard_map/all_to_all | solution.py:385
  25.8 10.1 %all_to_all.33 = f32[16,1,128]{2,1,0:T(1,128)S(1)} all-to-all(f32[16,1,128]{2,1,0:T(1,128)S(1)} %bitcast.18), channel_id=1, replica_groups=mesh['parts'=2,'tile'=16] {'tile'}, dimensions={0} | all-to-all | bytes 16384 | tf_op jit(solution)/shard_map/all_to_all | solution.py:385
  35.9 0.0 collective-permute-done.2.other_ref
  35.9 2.0 %chain3.1 = f32[16,128]{1,0:T(8,128)S(1)} custom-call(s32[4,2]{1,0:T(4,128)S(1)} %copy.8.offsets_ref, bf16[128,2048]{1,0:T(8,128)(2,1)S(1)} %copy-done, bf16[128,1024]{1,0:T(8,128)(2,1)S(1)} %collective-permute-done.2.other_ref, s32[1,16]{1,0:T(1,128)S(1)} %copy-done.1, f32[16,128]{1,0:T(8,128)S(1)} %bitcast.14), custom_call_target="tpu_custom_call" | custom-call | tf_op jit(solution)/shard_map/chain3/pallas_call | solution.py:369
  37.9 9.0 %all_to_all.34 = f32[16,1,128]{2,1,0:T(1,128)S(1)} all-to-all(f32[16,1,128]{2,1,0:T(1,128)S(1)} %bitcast.17), channel_id=1, replica_groups=mesh['parts'=2,'tile'=16] {'tile'}, dimensions={0} | all-to-all | bytes 16384 | tf_op jit(solution)/shard_map/all_to_all | solution.py:385
  46.9 2.3 %home.1 = (bf16[128,2048]{1,0:T(8,128)(2,1)}, f32[2,1,16]{2,1,0:T(1,128)}) custom-call(bf16[128,2048]{1,0:T(8,128)(2,1)S(1)} %copy-done, f32[16,128]{1,0:T(8,128)S(1)} %bitcast.13, f32[16,128]{1,0:T(8,128)S(1)} %bitcast.15, f32[16,128]{1,0:T(8,128)S(1)} %bitcast.16), custom_call_target="tpu_custom_call" | custom-call | tf_op jit(solution)/shard_map/home/pallas_call | solution.py:389
  (2 shorter events, 0.0 us)
Async XLA Ops:
  0.6 1.8 %copy-start = (bf16[128,2048]{1,0:T(8,128)(2,1)S(1)}, bf16[128,2048]{1,0:T(8,128)(2,1)}, u32[]{:S(2)}) copy-start(bf16[128,2048]{1,0:T(8,128)(2,1)} %own_ref.7) | copy-start | bytes 1572868
  1.7 1.6 %collective-permute-start = (bf16[128,1024]{1,0:T(8,128)(2,1)S(1)}, bf16[128,1024]{1,0:T(8,128)(2,1)S(1)}, u32[]{:S(2)}, u32[]{:S(2)}) collective-permute-start(bf16[128,1024]{1,0:T(8,128)(2,1)S(1)} %constant_dynamic-slice_fusion.2), channel_id=1, source_target_pairs={{2,6},{3,7},{4,8},{5,9},{6,2},{7,3},{8,4},{9,5},{18,22},{19,23},{2... | collective-permute-start | bytes 786440 | tf_op jit(solution)/shard_map/ppermute | solution.py:349
  2.5 0.7 %copy-start.2 = (s32[4,2]{0,1:T(2,128)S(1)}, s32[4,2]{0,1:T(2,128)}, u32[]{:S(2)}) copy-start(s32[4,2]{0,1:T(2,128)} %param.5) | copy-start | bytes 100
  2.5 0.8 %copy-start.1 = (s32[1,16]{1,0:T(1,128)S(1)}, s32[1,16]{1,0:T(1,128)}, u32[]{:S(2)}) copy-start(s32[1,16]{1,0:T(1,128)} %mask_ref.5) | copy-start | bytes 196
  2.5 17.0 %collective-permute-start.1 = (bf16[128,1024]{1,0:T(8,128)(2,1)S(1)}, bf16[128,1024]{1,0:T(8,128)(2,1)S(1)}, u32[]{:S(2)}, u32[]{:S(2)}) collective-permute-start(bf16[128,1024]{1,0:T(8,128)(2,1)S(1)} %get-tuple-element.9), channel_id=1, source_target_pairs={{6,10},{7,11},{8,12},{9,13},{10,6},{11,7},{12,8},{13,9},{22,26},{2... | collective-permute-start | bytes 786440 | tf_op jit(solution)/shard_map/ppermute | solution.py:349
  5.0 30.9 %collective-permute-start.2 = (bf16[128,1024]{1,0:T(8,128)(2,1)S(1)}, bf16[128,1024]{1,0:T(8,128)(2,1)S(1)}, u32[]{:S(2)}, u32[]{:S(2)}) collective-permute-start(bf16[128,1024]{1,0:T(8,128)(2,1)S(1)} %get-tuple-element.7), channel_id=1, source_target_pairs={{10,14},{11,15},{12,0},{13,1},{14,10},{15,11},{0,12},{1,13},{26,30... | collective-permute-start | bytes 786440 | tf_op jit(solution)/shard_map/ppermute | solution.py:349
  15.3 10.5 %all-to-all-start = ((f32[16,1,128]{2,1,0:T(1,128)}), f32[16,1,128]{2,1,0:T(1,128)S(1)}, u32[]{:S(2)}, u32[]{:S(2)}) async-start(f32[16,1,128]{2,1,0:T(1,128)} %bitcast.1), calls=%async_computation | async-start | bytes 16384 | tf_op jit(solution)/shard_map/all_to_all | solution.py:385

commit v11 on v10

--- a/solution.py
+++ b/solution.py
@@ -340,6 +340,16 @@
     looped(nodes, one)
 
 
+def half_kernel(rows, own_ref, out_ref, semaphore):
+    count = lax.axis_size("tile")
+    rotated = (lax.axis_index("tile") + count - rows // 2) % count
+    width = out_ref.shape[1]
+    start = pl.multiple_of(jnp.where(rotated // rows == 0, width, 0), PATCH)
+    copy = pltpu.make_async_copy(own_ref.at[:, pl.ds(start, width)], out_ref, semaphore)
+    copy.start()
+    copy.wait()
+
+
 def shards(sections, valid_mask, coarse_offsets):
     count = lax.axis_size("tile")
     rows = count // SECTIONS
@@ -356,13 +366,21 @@
         ends = [(place(lower, i), place(lower + 1, i)) for i in range(rows)]
         return moved(sent, ends + [(d, s) for s, d in ends])
 
+    vmem = pl.BlockSpec(memory_space=pltpu.VMEM)
+    params = pltpu.CompilerParams(vmem_limit_bytes=16 * 2**20)
     half = nodes // 2
-    first_half = half_of(sections, 0)
+    first_half = pl.pallas_call(
+        functools.partial(half_kernel, rows),
+        out_shape=jax.ShapeDtypeStruct((PATCH, half * PATCH), bf16),
+        in_specs=[pl.BlockSpec(memory_space=pltpu.HBM)],
+        out_specs=pl.BlockSpec(memory_space=pltpu.HBM),
+        scratch_shapes=[pltpu.SemaphoreType.DMA],
+        compiler_params=pltpu.CompilerParams(vmem_limit_bytes=60 * 2**20),
+        name="half",
+    )(sections)
     source, first_half = lax.optimization_barrier((sections, first_half))
     others = [swapped(first_half, 0), swapped(half_of(source, 1), 1)]
 
-    vmem = pl.BlockSpec(memory_space=pltpu.VMEM)
-    params = pltpu.CompilerParams(vmem_limit_bytes=16 * 2**20)
     gathered = []
     for step in range(1, SECTIONS):
         extra = gathered[-1:]

time: 49.5 us -> 57.7 us (1.17)
  Pallas kernels: 5.99 us -> 15.1 us
  local copies, waits for them, and re-layouts: 1.17 us -> 0.15 us
    pallas_call x0 -> x1, Pallas kernels: none -> 9.07 us  [shards(): pl.pallas_call(functools.partial(half_kernel, rows), out_shape=jax.ShapeD...]
    dynamic_slice x2 -> x1, local copies, waits for them, and re-layouts: 1.06 us -> 0.04 us  [half_of(): return lax.dynamic_slice_in_dim(source, start, half * PATCH, 1)]
where the time goes in v11:
time: 57.7 us; the launch traced here: 57.4 us
  blocking collectives  19.1 us (33%)
  starting transfers between devices  16 us (28%)
  Pallas kernels  15.1 us (26%)
  waiting for transfers between devices  6.33 us (11%)
  between operations  0.78 us (1%)
    all_to_all x2, blocking collectives, shards(): gathered.append(lax.all_to_all(sent, 'tile', 0, 0, tiled=True))  19.1 us
    ppermute x3, starting transfers between devices, shards(): moved = lambda value, pairs: lax.ppermute(value, 'tile', pairs)  11.7 us
    pallas_call x1, Pallas kernels, shards(): pl.pallas_call(functools.partial(half_kernel, rows), out_shape=jax.ShapeD...  9.07 us
    all_to_all x1, waiting for transfers between devices, shards(): gathered.append(lax.all_to_all(sent, 'tile', 0, 0, tiled=True))  6.32 us
    all_to_all x1, starting transfers between devices, shards(): gathered.append(lax.all_to_all(sent, 'tile', 0, 0, tiled=True))  4.34 us
    pallas_call x3, Pallas kernels, shards(): pl.pallas_call(functools.partial(chain_kernel, step, rows, nodes), out_sh...  3.69 us
    pallas_call x1, Pallas kernels, shards(): pl.pallas_call(functools.partial(home_kernel, rows, nodes), out_shape=(ja...  2.3 us
  transfers between devices with their start and end apart: 4, of which 1 were waited for; matrix products, arithmetic and copies ran while one was open for 0% of the time, Pallas kernels for 3%

profile of v11, /device:TPU:0, one launch (start us, length us, event | category | flops | bytes accessed | tf_op | source)
XLA Modules:
  0.0 57.4 jit_solution(6996359701717192932)
XLA Ops:
  0.6 0.0 copy-start
  0.6 9.1 %half.1 = bf16[128,1024]{1,0:T(8,128)(2,1)} custom-call(bf16[128,2048]{1,0:T(8,128)(2,1)} %own_ref.9), custom_call_target="tpu_custom_call" | custom-call | tf_op jit(solution)/shard_map/half/pallas_call | solution.py:372
  9.7 0.7 %collective-permute-start = (bf16[128,1024]{1,0:T(8,128)(2,1)}, bf16[128,1024]{1,0:T(8,128)(2,1)S(1)}, u32[]{:S(2)}, u32[]{:S(2)}) collective-permute-start(bf16[128,1024]{1,0:T(8,128)(2,1)} %half.1), channel_id=1, source_target_pairs={{2,6},{3,7},{4,8},{5,9},{6,2},{7,3},{8,4},{9,5},{18,22},{19,23},{2... | collective-permute-start | bytes 786440 | tf_op jit(solution)/shard_map/ppermute | solution.py:359
  10.4 0.0 copy-done
  10.5 0.0 copy-start.2
  10.5 0.0 copy-start.1
  10.5 0.7 %collective-permute-start.1 = (bf16[128,1024]{1,0:T(8,128)(2,1)S(1)}, bf16[128,1024]{1,0:T(8,128)(2,1)S(1)}, u32[]{:S(2)}, u32[]{:S(2)}) collective-permute-start(bf16[128,1024]{1,0:T(8,128)(2,1)S(1)} %get-tuple-element.9), channel_id=1, source_target_pairs={{6,10},{7,11},{8,12},{9,13},{10,6},{11,7},{12,8},{13,9},{22,26},{2... | collective-permute-start | bytes 786440 | tf_op jit(solution)/shard_map/ppermute | solution.py:359
  11.2 0.0 copy-done.2
  11.2 0.1 copy.8.offsets_ref
  11.3 0.0 collective-permute-done.other_ref
  11.3 0.0 copy-done.1
  11.3 1.7 %chain1.1 = f32[16,128]{1,0:T(8,128)} custom-call(s32[4,2]{1,0:T(4,128)S(1)} %copy.8.offsets_ref, bf16[128,2048]{1,0:T(8,128)(2,1)S(1)} %copy-done, bf16[128,1024]{1,0:T(8,128)(2,1)S(1)} %collective-permute-done.other_ref, s32[1,16]{1,0:T(1,128)S(1)} %copy-done.1), custom_call_target="tpu_custom_call" | custom-call | tf_op jit(solution)/shard_map/chain1/pallas_call | solution.py:387
  13.0 10.3 %collective-permute-start.2 = (bf16[128,1024]{1,0:T(8,128)(2,1)S(1)}, bf16[128,1024]{1,0:T(8,128)(2,1)S(1)}, u32[]{:S(2)}, u32[]{:S(2)}) collective-permute-start(bf16[128,1024]{1,0:T(8,128)(2,1)S(1)} %get-tuple-element.7), channel_id=1, source_target_pairs={{10,14},{11,15},{12,0},{13,1},{14,10},{15,11},{0,12},{1,13},{26,30... | collective-permute-start | bytes 786440 | tf_op jit(solution)/shard_map/ppermute | solution.py:359
  23.3 4.3 %all-to-all-start = ((f32[16,1,128]{2,1,0:T(1,128)}), f32[16,1,128]{2,1,0:T(1,128)S(1)}, u32[]{:S(2)}, u32[]{:S(2)}) async-start(f32[16,1,128]{2,1,0:T(1,128)} %bitcast.1), calls=%async_computation | async-start | bytes 16384 | tf_op jit(solution)/shard_map/all_to_all | solution.py:403
  27.7 0.0 collective-permute-done.1.other_ref
  27.7 6.3 %all-to-all-done = f32[16,1,128]{2,1,0:T(1,128)S(1)} async-done(((f32[16,1,128]{2,1,0:T(1,128)}), f32[16,1,128]{2,1,0:T(1,128)S(1)}, u32[]{:S(2)}, u32[]{:S(2)}) %all-to-all-start) | async-done | bytes 8224 | tf_op jit(solution)/shard_map/all_to_all | solution.py:403
  34.0 10.1 %all_to_all.33 = f32[16,1,128]{2,1,0:T(1,128)S(1)} all-to-all(f32[16,1,128]{2,1,0:T(1,128)S(1)} %bitcast.18), channel_id=1, replica_groups=mesh['parts'=2,'tile'=16] {'tile'}, dimensions={0} | all-to-all | bytes 16384 | tf_op jit(solution)/shard_map/all_to_all | solution.py:403
  44.2 0.0 collective-permute-done.2.other_ref
  44.2 2.0 %chain3.1 = f32[16,128]{1,0:T(8,128)S(1)} custom-call(s32[4,2]{1,0:T(4,128)S(1)} %copy.8.offsets_ref, bf16[128,2048]{1,0:T(8,128)(2,1)S(1)} %copy-done, bf16[128,1024]{1,0:T(8,128)(2,1)S(1)} %collective-permute-done.2.other_ref, s32[1,16]{1,0:T(1,128)S(1)} %copy-done.1, f32[16,128]{1,0:T(8,128)S(1)} %bitcast.14), custom_call_target="tpu_custom_call" | custom-call | tf_op jit(solution)/shard_map/chain3/pallas_call | solution.py:387
  46.1 9.0 %all_to_all.34 = f32[16,1,128]{2,1,0:T(1,128)S(1)} all-to-all(f32[16,1,128]{2,1,0:T(1,128)S(1)} %bitcast.17), channel_id=1, replica_groups=mesh['parts'=2,'tile'=16] {'tile'}, dimensions={0} | all-to-all | bytes 16384 | tf_op jit(solution)/shard_map/all_to_all | solution.py:403
  55.1 2.3 %home.1 = (bf16[128,2048]{1,0:T(8,128)(2,1)}, f32[2,1,16]{2,1,0:T(1,128)}) custom-call(bf16[128,2048]{1,0:T(8,128)(2,1)S(1)} %copy-done, f32[16,128]{1,0:T(8,128)S(1)} %bitcast.13, f32[16,128]{1,0:T(8,128)S(1)} %bitcast.15, f32[16,128]{1,0:T(8,128)S(1)} %bitcast.16), custom_call_target="tpu_custom_call" | custom-call | tf_op jit(solution)/shard_map/home/pallas_call | solution.py:407
  (2 shorter events, 0.0 us)
Async XLA Ops:
  0.6 9.8 %copy-start = (bf16[128,2048]{1,0:T(8,128)(2,1)S(1)}, bf16[128,2048]{1,0:T(8,128)(2,1)}, u32[]{:S(2)}) copy-start(bf16[128,2048]{1,0:T(8,128)(2,1)} %own_ref.9) | copy-start | bytes 1572868
  9.7 1.6 %collective-permute-start = (bf16[128,1024]{1,0:T(8,128)(2,1)}, bf16[128,1024]{1,0:T(8,128)(2,1)S(1)}, u32[]{:S(2)}, u32[]{:S(2)}) collective-permute-start(bf16[128,1024]{1,0:T(8,128)(2,1)} %half.1), channel_id=1, source_target_pairs={{2,6},{3,7},{4,8},{5,9},{6,2},{7,3},{8,4},{9,5},{18,22},{19,23},{2... | collective-permute-start | bytes 786440 | tf_op jit(solution)/shard_map/ppermute | solution.py:359
  10.5 0.7 %copy-start.2 = (s32[4,2]{0,1:T(2,128)S(1)}, s32[4,2]{0,1:T(2,128)}, u32[]{:S(2)}) copy-start(s32[4,2]{0,1:T(2,128)} %param.5) | copy-start | bytes 100
  10.5 0.8 %copy-start.1 = (s32[1,16]{1,0:T(1,128)S(1)}, s32[1,16]{1,0:T(1,128)}, u32[]{:S(2)}) copy-start(s32[1,16]{1,0:T(1,128)} %mask_ref.5) | copy-start | bytes 196
  10.5 17.2 %collective-permute-start.1 = (bf16[128,1024]{1,0:T(8,128)(2,1)S(1)}, bf16[128,1024]{1,0:T(8,128)(2,1)S(1)}, u32[]{:S(2)}, u32[]{:S(2)}) collective-permute-start(bf16[128,1024]{1,0:T(8,128)(2,1)S(1)} %get-tuple-element.9), channel_id=1, source_target_pairs={{6,10},{7,11},{8,12},{9,13},{10,6},{11,7},{12,8},{13,9},{22,26},{2... | collective-permute-start | bytes 786440 | tf_op jit(solution)/shard_map/ppermute | solution.py:359
  13.0 31.1 %collective-permute-start.2 = (bf16[128,1024]{1,0:T(8,128)(2,1)S(1)}, bf16[128,1024]{1,0:T(8,128)(2,1)S(1)}, u32[]{:S(2)}, u32[]{:S(2)}) collective-permute-start(bf16[128,1024]{1,0:T(8,128)(2,1)S(1)} %get-tuple-element.7), channel_id=1, source_target_pairs={{10,14},{11,15},{12,0},{13,1},{14,10},{15,11},{0,12},{1,13},{26,30... | collective-permute-start | bytes 786440 | tf_op jit(solution)/shard_map/ppermute | solution.py:359
  23.3 10.7 %all-to-all-start = ((f32[16,1,128]{2,1,0:T(1,128)}), f32[16,1,128]{2,1,0:T(1,128)S(1)}, u32[]{:S(2)}, u32[]{:S(2)}) async-start(f32[16,1,128]{2,1,0:T(1,128)} %bitcast.1), calls=%async_computation | async-start | bytes 16384 | tf_op jit(solution)/shard_map/all_to_all | solution.py:403

commit v12 on v10

--- a/solution.py
+++ b/solution.py
@@ -359,7 +359,8 @@
     half = nodes // 2
     first_half = half_of(sections, 0)
     source, first_half = lax.optimization_barrier((sections, first_half))
-    others = [swapped(first_half, 0), swapped(half_of(source, 1), 1)]
+    others = [swapped(first_half, 0)]
+    others += [swapped(half_of(source, lower), lower) for lower in range(1, SECTIONS - 1)]
 
     vmem = pl.BlockSpec(memory_space=pltpu.VMEM)
     params = pltpu.CompilerParams(vmem_limit_bytes=16 * 2**20)
@@ -383,9 +384,6 @@
             name=f"chain{step}",
         )(coarse_offsets, sections, others[step - 1], valid_mask, *extra)
         gathered.append(lax.all_to_all(sent, "tile", 0, 0, tiled=True))
-        if step + 1 < SECTIONS - 1:
-            later, sent = lax.optimization_barrier((half_of(source, step + 1), sent))
-            others.append(swapped(later, step + 1))
     return pl.pallas_call(
         functools.partial(home_kernel, rows, nodes),
         out_shape=(

time: 49.5 us -> 49.5 us (level)
  blocking collectives: 19.1 us -> 8.98 us
  waiting for transfers between devices: 6.33 us -> 12.6 us
  starting transfers between devices: 15.8 us -> 19.1 us
  Pallas kernels: 5.99 us -> 6.58 us
    all_to_all x2 -> x1, blocking collectives: 19.1 us -> 8.98 us  [shards(): gathered.append(lax.all_to_all(sent, 'tile', 0, 0, tiled=True))]
    all_to_all x1 -> x2, waiting for transfers between devices: 6.32 us -> 12.6 us  [shards(): gathered.append(lax.all_to_all(sent, 'tile', 0, 0, tiled=True))]
    all_to_all x1 -> x2, starting transfers between devices: 4.15 us -> 7.38 us  [shards(): gathered.append(lax.all_to_all(sent, 'tile', 0, 0, tiled=True))]
    pallas_call x3, Pallas kernels: 3.69 us -> 4.28 us  [shards(): pl.pallas_call(functools.partial(chain_kernel, step, rows, nodes), out_sh...]
  transfers between devices with their start and end apart: 4 -> 5, of which waited for: 1 -> 2; matrix products, arithmetic and copies ran while one was open for 0% -> 0% of each run, Pallas kernels for 3% -> 5%
where the time goes in v12:
time: 49.5 us; the launch traced here: 49.2 us
  starting transfers between devices  19.1 us (39%)
  waiting for transfers between devices  12.6 us (25%)
  blocking collectives  8.98 us (18%)
  Pallas kernels  6.58 us (13%)
  local copies, waits for them, and re-layouts  1.17 us (2%)
  between operations  0.79 us (2%)
    all_to_all x2, waiting for transfers between devices, shards(): gathered.append(lax.all_to_all(sent, 'tile', 0, 0, tiled=True))  12.6 us
    ppermute x3, starting transfers between devices, shards(): moved = lambda value, pairs: lax.ppermute(value, 'tile', pairs)  11.7 us
    all_to_all x1, blocking collectives, shards(): gathered.append(lax.all_to_all(sent, 'tile', 0, 0, tiled=True))  8.98 us
    all_to_all x2, starting transfers between devices, shards(): gathered.append(lax.all_to_all(sent, 'tile', 0, 0, tiled=True))  7.38 us
    pallas_call x3, Pallas kernels, shards(): pl.pallas_call(functools.partial(chain_kernel, step, rows, nodes), out_sh...  4.28 us
    pallas_call x1, Pallas kernels, shards(): pl.pallas_call(functools.partial(home_kernel, rows, nodes), out_shape=(ja...  2.3 us
    dynamic_slice x2, local copies, waits for them, and re-layouts, half_of(): return lax.dynamic_slice_in_dim(source, start, half * PATCH, 1)  1.06 us
  transfers between devices with their start and end apart: 5, of which 2 were waited for; matrix products, arithmetic and copies ran while one was open for 0% of the time, Pallas kernels for 5%

profile of v12, /device:TPU:0, one launch (start us, length us, event | category | flops | bytes accessed | tf_op | source)
XLA Modules:
  0.0 49.2 jit_solution(5900186167144985464)
XLA Ops:
  0.6 0.0 copy-start
  0.7 1.0 %constant_dynamic-slice_fusion.2 = bf16[128,1024]{1,0:T(8,128)(2,1)S(1)} fusion(bf16[128,2048]{1,0:T(8,128)(2,1)} %own_ref.7, s32[]{:T(128)S(6)} %select_n.26), kind=kLoop, calls=%fused_computation.2 | loop fusion | bytes 524292 | tf_op jit(solution)/shard_map/dynamic_slice | solution.py:353
  1.7 0.7 %collective-permute-start = (bf16[128,1024]{1,0:T(8,128)(2,1)S(1)}, bf16[128,1024]{1,0:T(8,128)(2,1)S(1)}, u32[]{:S(2)}, u32[]{:S(2)}) collective-permute-start(bf16[128,1024]{1,0:T(8,128)(2,1)S(1)} %constant_dynamic-slice_fusion.2), channel_id=1, source_target_pairs={{2,6},{3,7},{4,8},{5,9},{6,2},{7,3},{8,4},{9,5},{18,22},{19,23},{2... | collective-permute-start | bytes 786440 | tf_op jit(solution)/shard_map/ppermute | solution.py:349
  2.4 0.0 copy-done
  2.5 0.0 copy-start.2
  2.5 0.7 %collective-permute-start.1 = (bf16[128,1024]{1,0:T(8,128)(2,1)S(1)}, bf16[128,1024]{1,0:T(8,128)(2,1)S(1)}, u32[]{:S(2)}, u32[]{:S(2)}) collective-permute-start(bf16[128,1024]{1,0:T(8,128)(2,1)S(1)} %get-tuple-element.7), channel_id=1, source_target_pairs={{6,10},{7,11},{8,12},{9,13},{10,6},{11,7},{12,8},{13,9},{22,26},{2... | collective-permute-start | bytes 786440 | tf_op jit(solution)/shard_map/ppermute | solution.py:349
  3.2 0.0 copy-start.1
  3.2 10.3 %collective-permute-start.2 = (bf16[128,1024]{1,0:T(8,128)(2,1)S(1)}, bf16[128,1024]{1,0:T(8,128)(2,1)S(1)}, u32[]{:S(2)}, u32[]{:S(2)}) collective-permute-start(bf16[128,1024]{1,0:T(8,128)(2,1)S(1)} %get-tuple-element.6), channel_id=1, source_target_pairs={{10,14},{11,15},{12,0},{13,1},{14,10},{15,11},{0,12},{1,13},{26,30... | collective-permute-start | bytes 786440 | tf_op jit(solution)/shard_map/ppermute | solution.py:349
  13.5 0.0 copy-done.2
  13.5 0.1 copy.8.offsets_ref
  13.6 0.0 collective-permute-done.other_ref
  13.6 0.0 copy-done.1
  13.6 1.7 %chain1.1 = f32[16,128]{1,0:T(8,128)} custom-call(s32[4,2]{1,0:T(4,128)S(1)} %copy.8.offsets_ref, bf16[128,2048]{1,0:T(8,128)(2,1)S(1)} %copy-done, bf16[128,1024]{1,0:T(8,128)(2,1)S(1)} %collective-permute-done.other_ref, s32[1,16]{1,0:T(1,128)S(1)} %copy-done.1), custom_call_target="tpu_custom_call" | custom-call | tf_op jit(solution)/shard_map/chain1/pallas_call | solution.py:370
  15.3 3.5 %all-to-all-start = ((f32[16,1,128]{2,1,0:T(1,128)}), f32[16,1,128]{2,1,0:T(1,128)S(1)}, u32[]{:S(2)}, u32[]{:S(2)}) async-start(f32[16,1,128]{2,1,0:T(1,128)} %bitcast.1), calls=%async_computation | async-start | bytes 16384 | tf_op jit(solution)/shard_map/all_to_all | solution.py:386
  18.8 0.0 collective-permute-done.1.other_ref
  18.8 6.3 %all-to-all-done = f32[16,1,128]{2,1,0:T(1,128)S(1)} async-done(((f32[16,1,128]{2,1,0:T(1,128)}), f32[16,1,128]{2,1,0:T(1,128)S(1)}, u32[]{:S(2)}, u32[]{:S(2)}) %all-to-all-start) | async-done | bytes 8224 | tf_op jit(solution)/shard_map/all_to_all | solution.py:386
  25.1 0.6 %chain2.1 = f32[16,128]{1,0:T(8,128)} custom-call(s32[4,2]{1,0:T(4,128)S(1)} %copy.8.offsets_ref, bf16[128,2048]{1,0:T(8,128)(2,1)S(1)} %copy-done, bf16[128,1024]{1,0:T(8,128)(2,1)S(1)} %collective-permute-done.1.other_ref, s32[1,16]{1,0:T(1,128)S(1)} %copy-done.1, f32[16,128]{1,0:T(8,128)S(1)} %bitcast.12), custom_call_target="tpu_custom_call" | custom-call | tf_op jit(solution)/shard_map/chain2/pallas_call | solution.py:370
  25.7 3.9 %all-to-all-start.1 = ((f32[16,1,128]{2,1,0:T(1,128)}), f32[16,1,128]{2,1,0:T(1,128)S(1)}, u32[]{:S(2)}, u32[]{:S(2)}) async-start(f32[16,1,128]{2,1,0:T(1,128)} %bitcast.4), calls=%async_computation.1 | async-start | bytes 16384 | tf_op jit(solution)/shard_map/all_to_all | solution.py:386
  29.6 0.0 collective-permute-done.2.other_ref
  29.6 6.3 %all-to-all-done.1 = f32[16,1,128]{2,1,0:T(1,128)S(1)} async-done(((f32[16,1,128]{2,1,0:T(1,128)}), f32[16,1,128]{2,1,0:T(1,128)S(1)}, u32[]{:S(2)}, u32[]{:S(2)}) %all-to-all-start.1) | async-done | bytes 8224 | tf_op jit(solution)/shard_map/all_to_all | solution.py:386
  36.0 2.0 %chain3.1 = f32[16,128]{1,0:T(8,128)S(1)} custom-call(s32[4,2]{1,0:T(4,128)S(1)} %copy.8.offsets_ref, bf16[128,2048]{1,0:T(8,128)(2,1)S(1)} %copy-done, bf16[128,1024]{1,0:T(8,128)(2,1)S(1)} %collective-permute-done.2.other_ref, s32[1,16]{1,0:T(1,128)S(1)} %copy-done.1, f32[16,128]{1,0:T(8,128)S(1)} %bitcast.14), custom_call_target="tpu_custom_call" | custom-call | tf_op jit(solution)/shard_map/chain3/pallas_call | solution.py:370
  37.9 9.0 %all_to_all.33 = f32[16,1,128]{2,1,0:T(1,128)S(1)} all-to-all(f32[16,1,128]{2,1,0:T(1,128)S(1)} %bitcast.17), channel_id=1, replica_groups=mesh['parts'=2,'tile'=16] {'tile'}, dimensions={0} | all-to-all | bytes 16384 | tf_op jit(solution)/shard_map/all_to_all | solution.py:386
  46.9 2.3 %home.1 = (bf16[128,2048]{1,0:T(8,128)(2,1)}, f32[2,1,16]{2,1,0:T(1,128)}) custom-call(bf16[128,2048]{1,0:T(8,128)(2,1)S(1)} %copy-done, f32[16,128]{1,0:T(8,128)S(1)} %bitcast.13, f32[16,128]{1,0:T(8,128)S(1)} %bitcast.15, f32[16,128]{1,0:T(8,128)S(1)} %bitcast.16), custom_call_target="tpu_custom_call" | custom-call | tf_op jit(solution)/shard_map/home/pallas_call | solution.py:387
  (1 shorter events, 0.0 us)
Async XLA Ops:
  0.6 1.8 %copy-start = (bf16[128,2048]{1,0:T(8,128)(2,1)S(1)}, bf16[128,2048]{1,0:T(8,128)(2,1)}, u32[]{:S(2)}) copy-start(bf16[128,2048]{1,0:T(8,128)(2,1)} %own_ref.7) | copy-start | bytes 1572868
  1.7 11.9 %collective-permute-start = (bf16[128,1024]{1,0:T(8,128)(2,1)S(1)}, bf16[128,1024]{1,0:T(8,128)(2,1)S(1)}, u32[]{:S(2)}, u32[]{:S(2)}) collective-permute-start(bf16[128,1024]{1,0:T(8,128)(2,1)S(1)} %constant_dynamic-slice_fusion.2), channel_id=1, source_target_pairs={{2,6},{3,7},{4,8},{5,9},{6,2},{7,3},{8,4},{9,5},{18,22},{19,23},{2... | collective-permute-start | bytes 786440 | tf_op jit(solution)/shard_map/ppermute | solution.py:349
  2.5 11.0 %copy-start.2 = (s32[4,2]{0,1:T(2,128)S(1)}, s32[4,2]{0,1:T(2,128)}, u32[]{:S(2)}) copy-start(s32[4,2]{0,1:T(2,128)} %param.5) | copy-start | bytes 100
  2.5 16.3 %collective-permute-start.1 = (bf16[128,1024]{1,0:T(8,128)(2,1)S(1)}, bf16[128,1024]{1,0:T(8,128)(2,1)S(1)}, u32[]{:S(2)}, u32[]{:S(2)}) collective-permute-start(bf16[128,1024]{1,0:T(8,128)(2,1)S(1)} %get-tuple-element.7), channel_id=1, source_target_pairs={{6,10},{7,11},{8,12},{9,13},{10,6},{11,7},{12,8},{13,9},{22,26},{2... | collective-permute-start | bytes 786440 | tf_op jit(solution)/shard_map/ppermute | solution.py:349
  3.2 10.4 %copy-start.1 = (s32[1,16]{1,0:T(1,128)S(1)}, s32[1,16]{1,0:T(1,128)}, u32[]{:S(2)}) copy-start(s32[1,16]{1,0:T(1,128)} %mask_ref.5) | copy-start | bytes 196
  3.2 26.5 %collective-permute-start.2 = (bf16[128,1024]{1,0:T(8,128)(2,1)S(1)}, bf16[128,1024]{1,0:T(8,128)(2,1)S(1)}, u32[]{:S(2)}, u32[]{:S(2)}) collective-permute-start(bf16[128,1024]{1,0:T(8,128)(2,1)S(1)} %get-tuple-element.6), channel_id=1, source_target_pairs={{10,14},{11,15},{12,0},{13,1},{14,10},{15,11},{0,12},{1,13},{26,30... | collective-permute-start | bytes 786440 | tf_op jit(solution)/shard_map/ppermute | solution.py:349
  15.3 9.8 %all-to-all-start = ((f32[16,1,128]{2,1,0:T(1,128)}), f32[16,1,128]{2,1,0:T(1,128)S(1)}, u32[]{:S(2)}, u32[]{:S(2)}) async-start(f32[16,1,128]{2,1,0:T(1,128)} %bitcast.1), calls=%async_computation | async-start | bytes 16384 | tf_op jit(solution)/shard_map/all_to_all | solution.py:386
  25.7 10.2 %all-to-all-start.1 = ((f32[16,1,128]{2,1,0:T(1,128)}), f32[16,1,128]{2,1,0:T(1,128)S(1)}, u32[]{:S(2)}, u32[]{:S(2)}) async-start(f32[16,1,128]{2,1,0:T(1,128)} %bitcast.4), calls=%async_computation.1 | async-start | bytes 16384 | tf_op jit(solution)/shard_map/all_to_all | solution.py:386

commit v13 on v12

--- a/solution.py
+++ b/solution.py
@@ -383,6 +383,8 @@
             compiler_params=params,
             name=f"chain{step}",
         )(coarse_offsets, sections, others[step - 1], valid_mask, *extra)
+        if 1 < step < SECTIONS - 1:
+            sent, others[step] = lax.optimization_barrier((sent, others[step]))
         gathered.append(lax.all_to_all(sent, "tile", 0, 0, tiled=True))
     return pl.pallas_call(
         functools.partial(home_kernel, rows, nodes),

time: 49.5 us -> 48.8 us (0.986)
  blocking collectives: 8.98 us -> 19.1 us
  waiting for transfers between devices: 12.6 us -> 6.31 us
  starting transfers between devices: 19.1 us -> 15.1 us
  Pallas kernels: 6.58 us -> 5.98 us
    all_to_all x1 -> x2, blocking collectives: 8.98 us -> 19.1 us  [shards(): gathered.append(lax.all_to_all(sent, 'tile', 0, 0, tiled=True))]
    all_to_all x2 -> x1, waiting for transfers between devices: 12.6 us -> 6.3 us  [shards(): gathered.append(lax.all_to_all(sent, 'tile', 0, 0, tiled=True))]
    all_to_all x2 -> x1, starting transfers between devices: 7.38 us -> 3.47 us  [shards(): gathered.append(lax.all_to_all(sent, 'tile', 0, 0, tiled=True))]
    pallas_call x3, Pallas kernels: 4.28 us -> 3.68 us  [shards(): pl.pallas_call(functools.partial(chain_kernel, step, rows, nodes), out_sh...]
  transfers between devices with their start and end apart: 5 -> 4, of which waited for: 2 -> 1; matrix products, arithmetic and copies ran while one was open for 0% -> 0% of each run, Pallas kernels for 5% -> 4%
where the time goes in v13:
time: 48.8 us; the launch traced here: 48.5 us
  blocking collectives  19.1 us (39%)
  starting transfers between devices  15.1 us (31%)
  waiting for transfers between devices  6.31 us (13%)
  Pallas kernels  5.98 us (12%)
  local copies, waits for them, and re-layouts  1.17 us (2%)
  between operations  0.78 us (2%)
    all_to_all x2, blocking collectives, shards(): gathered.append(lax.all_to_all(sent, 'tile', 0, 0, tiled=True))  19.1 us
    ppermute x3, starting transfers between devices, shards(): moved = lambda value, pairs: lax.ppermute(value, 'tile', pairs)  11.7 us
    all_to_all x1, waiting for transfers between devices, shards(): gathered.append(lax.all_to_all(sent, 'tile', 0, 0, tiled=True))  6.3 us
    pallas_call x3, Pallas kernels, shards(): pl.pallas_call(functools.partial(chain_kernel, step, rows, nodes), out_sh...  3.68 us
    all_to_all x1, starting transfers between devices, shards(): gathered.append(lax.all_to_all(sent, 'tile', 0, 0, tiled=True))  3.47 us
    pallas_call x1, Pallas kernels, shards(): pl.pallas_call(functools.partial(home_kernel, rows, nodes), out_shape=(ja...  2.3 us
    dynamic_slice x2, local copies, waits for them, and re-layouts, half_of(): return lax.dynamic_slice_in_dim(source, start, half * PATCH, 1)  1.06 us
  transfers between devices with their start and end apart: 4, of which 1 were waited for; matrix products, arithmetic and copies ran while one was open for 0% of the time, Pallas kernels for 4%

profile of v13, /device:TPU:0, one launch (start us, length us, event | category | flops | bytes accessed | tf_op | source)
XLA Modules:
  0.0 48.5 jit_solution(3935411280580784622)
XLA Ops:
  0.6 0.0 copy-start
  0.7 1.0 %constant_dynamic-slice_fusion.2 = bf16[128,1024]{1,0:T(8,128)(2,1)S(1)} fusion(bf16[128,2048]{1,0:T(8,128)(2,1)} %own_ref.7, s32[]{:T(128)S(6)} %select_n.26), kind=kLoop, calls=%fused_computation.2 | loop fusion | bytes 524292 | tf_op jit(solution)/shard_map/dynamic_slice | solution.py:353
  1.7 0.7 %collective-permute-start = (bf16[128,1024]{1,0:T(8,128)(2,1)S(1)}, bf16[128,1024]{1,0:T(8,128)(2,1)S(1)}, u32[]{:S(2)}, u32[]{:S(2)}) collective-permute-start(bf16[128,1024]{1,0:T(8,128)(2,1)S(1)} %constant_dynamic-slice_fusion.2), channel_id=1, source_target_pairs={{2,6},{3,7},{4,8},{5,9},{6,2},{7,3},{8,4},{9,5},{18,22},{19,23},{2... | collective-permute-start | bytes 786440 | tf_op jit(solution)/shard_map/ppermute | solution.py:349
  2.4 0.0 copy-done
  2.5 0.0 copy-start.2
  2.5 0.7 %collective-permute-start.1 = (bf16[128,1024]{1,0:T(8,128)(2,1)S(1)}, bf16[128,1024]{1,0:T(8,128)(2,1)S(1)}, u32[]{:S(2)}, u32[]{:S(2)}) collective-permute-start(bf16[128,1024]{1,0:T(8,128)(2,1)S(1)} %get-tuple-element.11), channel_id=1, source_target_pairs={{6,10},{7,11},{8,12},{9,13},{10,6},{11,7},{12,8},{13,9},{22,26},{2... | collective-permute-start | bytes 786440 | tf_op jit(solution)/shard_map/ppermute | solution.py:349
  3.2 0.0 copy-start.1
  3.2 10.3 %collective-permute-start.2 = (bf16[128,1024]{1,0:T(8,128)(2,1)S(1)}, bf16[128,1024]{1,0:T(8,128)(2,1)S(1)}, u32[]{:S(2)}, u32[]{:S(2)}) collective-permute-start(bf16[128,1024]{1,0:T(8,128)(2,1)S(1)} %get-tuple-element.10), channel_id=1, source_target_pairs={{10,14},{11,15},{12,0},{13,1},{14,10},{15,11},{0,12},{1,13},{26,30... | collective-permute-start | bytes 786440 | tf_op jit(solution)/shard_map/ppermute | solution.py:349
  13.5 0.0 copy-done.2
  13.5 0.1 copy.8.offsets_ref
  13.6 0.0 collective-permute-done.other_ref
  13.6 0.0 copy-done.1
  13.6 1.7 %chain1.1 = f32[16,128]{1,0:T(8,128)} custom-call(s32[4,2]{1,0:T(4,128)S(1)} %copy.8.offsets_ref, bf16[128,2048]{1,0:T(8,128)(2,1)S(1)} %copy-done, bf16[128,1024]{1,0:T(8,128)(2,1)S(1)} %collective-permute-done.other_ref, s32[1,16]{1,0:T(1,128)S(1)} %copy-done.1), custom_call_target="tpu_custom_call" | custom-call | tf_op jit(solution)/shard_map/chain1/pallas_call | solution.py:370
  15.3 3.5 %all-to-all-start = ((f32[16,1,128]{2,1,0:T(1,128)}), f32[16,1,128]{2,1,0:T(1,128)S(1)}, u32[]{:S(2)}, u32[]{:S(2)}) async-start(f32[16,1,128]{2,1,0:T(1,128)} %bitcast.1), calls=%async_computation | async-start | bytes 16384 | tf_op jit(solution)/shard_map/all_to_all | solution.py:388
  18.8 0.0 collective-permute-done.1.other_ref
  18.8 6.3 %all-to-all-done = f32[16,1,128]{2,1,0:T(1,128)S(1)} async-done(((f32[16,1,128]{2,1,0:T(1,128)}), f32[16,1,128]{2,1,0:T(1,128)S(1)}, u32[]{:S(2)}, u32[]{:S(2)}) %all-to-all-start) | async-done | bytes 8224 | tf_op jit(solution)/shard_map/all_to_all | solution.py:388
  25.1 0.0 collective-permute-done.2.other_ref
  25.1 10.1 %all_to_all.33 = f32[16,1,128]{2,1,0:T(1,128)S(1)} all-to-all(f32[16,1,128]{2,1,0:T(1,128)S(1)} %bitcast.16), channel_id=1, replica_groups=mesh['parts'=2,'tile'=16] {'tile'}, dimensions={0} | all-to-all | bytes 16384 | tf_op jit(solution)/shard_map/all_to_all | solution.py:388
  35.2 2.0 %chain3.1 = f32[16,128]{1,0:T(8,128)S(1)} custom-call(s32[4,2]{1,0:T(4,128)S(1)} %copy.8.offsets_ref, bf16[128,2048]{1,0:T(8,128)(2,1)S(1)} %copy-done, bf16[128,1024]{1,0:T(8,128)(2,1)S(1)} %collective-permute-done.2.other_ref, s32[1,16]{1,0:T(1,128)S(1)} %copy-done.1, f32[16,128]{1,0:T(8,128)S(1)} %bitcast.14), custom_call_target="tpu_custom_call" | custom-call | tf_op jit(solution)/shard_map/chain3/pallas_call | solution.py:370
  37.2 9.0 %all_to_all.34 = f32[16,1,128]{2,1,0:T(1,128)S(1)} all-to-all(f32[16,1,128]{2,1,0:T(1,128)S(1)} %bitcast.18), channel_id=1, replica_groups=mesh['parts'=2,'tile'=16] {'tile'}, dimensions={0} | all-to-all | bytes 16384 | tf_op jit(solution)/shard_map/all_to_all | solution.py:388
  46.2 2.3 %home.1 = (bf16[128,2048]{1,0:T(8,128)(2,1)}, f32[2,1,16]{2,1,0:T(1,128)}) custom-call(bf16[128,2048]{1,0:T(8,128)(2,1)S(1)} %copy-done, f32[16,128]{1,0:T(8,128)S(1)} %bitcast.13, f32[16,128]{1,0:T(8,128)S(1)} %bitcast.15, f32[16,128]{1,0:T(8,128)S(1)} %bitcast.17), custom_call_target="tpu_custom_call" | custom-call | tf_op jit(solution)/shard_map/home/pallas_call | solution.py:389
  (2 shorter events, 0.0 us)
Async XLA Ops:
  0.6 1.8 %copy-start = (bf16[128,2048]{1,0:T(8,128)(2,1)S(1)}, bf16[128,2048]{1,0:T(8,128)(2,1)}, u32[]{:S(2)}) copy-start(bf16[128,2048]{1,0:T(8,128)(2,1)} %own_ref.7) | copy-start | bytes 1572868
  1.7 11.9 %collective-permute-start = (bf16[128,1024]{1,0:T(8,128)(2,1)S(1)}, bf16[128,1024]{1,0:T(8,128)(2,1)S(1)}, u32[]{:S(2)}, u32[]{:S(2)}) collective-permute-start(bf16[128,1024]{1,0:T(8,128)(2,1)S(1)} %constant_dynamic-slice_fusion.2), channel_id=1, source_target_pairs={{2,6},{3,7},{4,8},{5,9},{6,2},{7,3},{8,4},{9,5},{18,22},{19,23},{2... | collective-permute-start | bytes 786440 | tf_op jit(solution)/shard_map/ppermute | solution.py:349
  2.5 11.0 %copy-start.2 = (s32[4,2]{0,1:T(2,128)S(1)}, s32[4,2]{0,1:T(2,128)}, u32[]{:S(2)}) copy-start(s32[4,2]{0,1:T(2,128)} %param.5) | copy-start | bytes 100
  2.5 16.3 %collective-permute-start.1 = (bf16[128,1024]{1,0:T(8,128)(2,1)S(1)}, bf16[128,1024]{1,0:T(8,128)(2,1)S(1)}, u32[]{:S(2)}, u32[]{:S(2)}) collective-permute-start(bf16[128,1024]{1,0:T(8,128)(2,1)S(1)} %get-tuple-element.11), channel_id=1, source_target_pairs={{6,10},{7,11},{8,12},{9,13},{10,6},{11,7},{12,8},{13,9},{22,26},{2... | collective-permute-start | bytes 786440 | tf_op jit(solution)/shard_map/ppermute | solution.py:349
  3.2 10.4 %copy-start.1 = (s32[1,16]{1,0:T(1,128)S(1)}, s32[1,16]{1,0:T(1,128)}, u32[]{:S(2)}) copy-start(s32[1,16]{1,0:T(1,128)} %mask_ref.5) | copy-start | bytes 196
  3.2 21.9 %collective-permute-start.2 = (bf16[128,1024]{1,0:T(8,128)(2,1)S(1)}, bf16[128,1024]{1,0:T(8,128)(2,1)S(1)}, u32[]{:S(2)}, u32[]{:S(2)}) collective-permute-start(bf16[128,1024]{1,0:T(8,128)(2,1)S(1)} %get-tuple-element.10), channel_id=1, source_target_pairs={{10,14},{11,15},{12,0},{13,1},{14,10},{15,11},{0,12},{1,13},{26,30... | collective-permute-start | bytes 786440 | tf_op jit(solution)/shard_map/ppermute | solution.py:349
  15.3 9.8 %all-to-all-start = ((f32[16,1,128]{2,1,0:T(1,128)}), f32[16,1,128]{2,1,0:T(1,128)S(1)}, u32[]{:S(2)}, u32[]{:S(2)}) async-start(f32[16,1,128]{2,1,0:T(1,128)} %bitcast.1), calls=%async_computation | async-start | bytes 16384 | tf_op jit(solution)/shard_map/all_to_all | solution.py:388

commit v14 on v13

--- a/solution.py
+++ b/solution.py
@@ -253,7 +253,7 @@
         area = float(PATCH * PATCH)
 
         if step > 1:
-            row_shift = own_row(relax(section_grid(refs[0][...], step - 1, rows), rows, nodes), row_index)
+            row_shift = own_row(relax(refs[0][...], rows, nodes), row_index)
             base_ref[...], swing_ref[...] = kernels_of(row_shift, first, cols, nodes)
 
         def stage(index, slot):
@@ -366,7 +366,7 @@
     params = pltpu.CompilerParams(vmem_limit_bytes=16 * 2**20)
     gathered = []
     for step in range(1, SECTIONS):
-        extra = gathered[-1:]
+        extra = [section_grid(gathered[-1], step - 1, rows)] if gathered else []
         sent = pl.pallas_call(
             functools.partial(chain_kernel, step, rows, nodes),
             out_shape=jax.ShapeDtypeStruct((count, LANES), f32),

time: 48.8 us -> 48.1 us (0.986)
  blocking collectives: 19.1 us -> 28.8 us
  waiting for transfers between devices: 6.31 us -> 0.01 us
  starting transfers between devices: 15.1 us -> 11.7 us
  Pallas kernels: 5.98 us -> 5.41 us
    all_to_all x2 -> x3, blocking collectives: 19.1 us -> 28.8 us  [shards(): gathered.append(lax.all_to_all(sent, 'tile', 0, 0, tiled=True))]
    all_to_all x1 -> x0, waiting for transfers between devices: 6.3 us -> none  [shards(): gathered.append(lax.all_to_all(sent, 'tile', 0, 0, tiled=True))]
    all_to_all x1 -> x0, starting transfers between devices: 3.47 us -> none  [shards(): gathered.append(lax.all_to_all(sent, 'tile', 0, 0, tiled=True))]
    pallas_call x3, Pallas kernels: 3.68 us -> 3.11 us  [shards(): pl.pallas_call(functools.partial(chain_kernel, step, rows, nodes), out_sh...]
  transfers between devices with their start and end apart: 4 -> 3, of which waited for: 1 -> 0; matrix products, arithmetic and copies ran while one was open for 0% -> 0% of each run, Pallas kernels for 4% -> 2%
where the time goes in v14:
time: 48.1 us; the launch traced here: 47.8 us
  blocking collectives  28.8 us (60%)
  starting transfers between devices  11.7 us (24%)
  Pallas kernels  5.41 us (11%)
  local copies, waits for them, and re-layouts  1.19 us (2%)
  between operations  0.79 us (2%)
    all_to_all x3, blocking collectives, shards(): gathered.append(lax.all_to_all(sent, 'tile', 0, 0, tiled=True))  28.8 us
    ppermute x3, starting transfers between devices, shards(): moved = lambda value, pairs: lax.ppermute(value, 'tile', pairs)  11.7 us
    pallas_call x3, Pallas kernels, shards(): pl.pallas_call(functools.partial(chain_kernel, step, rows, nodes), out_sh...  3.11 us
    pallas_call x1, Pallas kernels, shards(): pl.pallas_call(functools.partial(home_kernel, rows, nodes), out_shape=(ja...  2.3 us
    dynamic_slice x2, local copies, waits for them, and re-layouts, half_of(): return lax.dynamic_slice_in_dim(source, start, half * PATCH, 1)  1.06 us
  transfers between devices with their start and end apart: 3, of which 0 were waited for; matrix products, arithmetic and copies ran while one was open for 0% of the time, Pallas kernels for 2%

profile of v14, /device:TPU:0, one launch (start us, length us, event | category | flops | bytes accessed | tf_op | source)
XLA Modules:
  0.0 47.8 jit_solution(11675386403096703515)
XLA Ops:
  0.6 0.0 copy-start
  0.7 1.0 %constant_dynamic-slice_fusion.2 = bf16[128,1024]{1,0:T(8,128)(2,1)S(1)} fusion(bf16[128,2048]{1,0:T(8,128)(2,1)} %own_ref.7, s32[]{:T(128)S(6)} %select_n.26), kind=kLoop, calls=%fused_computation.6 | loop fusion | bytes 524292 | tf_op jit(solution)/shard_map/dynamic_slice | solution.py:353
  1.7 0.7 %collective-permute-start = (bf16[128,1024]{1,0:T(8,128)(2,1)S(1)}, bf16[128,1024]{1,0:T(8,128)(2,1)S(1)}, u32[]{:S(2)}, u32[]{:S(2)}) collective-permute-start(bf16[128,1024]{1,0:T(8,128)(2,1)S(1)} %constant_dynamic-slice_fusion.2), channel_id=1, source_target_pairs={{2,6},{3,7},{4,8},{5,9},{6,2},{7,3},{8,4},{9,5},{18,22},{19,23},{2... | collective-permute-start | bytes 786440 | tf_op jit(solution)/shard_map/ppermute | solution.py:349
  2.4 0.0 copy-done
  2.5 0.0 copy-start.2
  2.5 0.7 %collective-permute-start.1 = (bf16[128,1024]{1,0:T(8,128)(2,1)S(1)}, bf16[128,1024]{1,0:T(8,128)(2,1)S(1)}, u32[]{:S(2)}, u32[]{:S(2)}) collective-permute-start(bf16[128,1024]{1,0:T(8,128)(2,1)S(1)} %get-tuple-element.11), channel_id=1, source_target_pairs={{6,10},{7,11},{8,12},{9,13},{10,6},{11,7},{12,8},{13,9},{22,26},{2... | collective-permute-start | bytes 786440 | tf_op jit(solution)/shard_map/ppermute | solution.py:349
  3.2 0.0 copy-start.1
  3.2 10.3 %collective-permute-start.2 = (bf16[128,1024]{1,0:T(8,128)(2,1)S(1)}, bf16[128,1024]{1,0:T(8,128)(2,1)S(1)}, u32[]{:S(2)}, u32[]{:S(2)}) collective-permute-start(bf16[128,1024]{1,0:T(8,128)(2,1)S(1)} %get-tuple-element.10), channel_id=1, source_target_pairs={{10,14},{11,15},{12,0},{13,1},{14,10},{15,11},{0,12},{1,13},{26,30... | collective-permute-start | bytes 786440 | tf_op jit(solution)/shard_map/ppermute | solution.py:349
  13.5 0.0 copy-done.2
  13.5 0.1 copy.8.offsets_ref
  13.6 0.0 collective-permute-done.other_ref
  13.6 0.0 copy-done.1
  13.6 1.1 %chain1.1 = f32[16,128]{1,0:T(8,128)S(1)} custom-call(s32[4,2]{1,0:T(4,128)S(1)} %copy.8.offsets_ref, bf16[128,2048]{1,0:T(8,128)(2,1)S(1)} %copy-done, bf16[128,1024]{1,0:T(8,128)(2,1)S(1)} %collective-permute-done.other_ref, s32[1,16]{1,0:T(1,128)S(1)} %copy-done.1), custom_call_target="tpu_custom_call" | custom-call | tf_op jit(solution)/shard_map/chain1/pallas_call | solution.py:370
  14.7 9.7 %all_to_all.33 = f32[16,1,128]{2,1,0:T(1,128)S(1)} all-to-all(f32[16,1,128]{2,1,0:T(1,128)S(1)} %bitcast.25), channel_id=1, replica_groups=mesh['parts'=2,'tile'=16] {'tile'}, dimensions={0} | all-to-all | bytes 16384 | tf_op jit(solution)/shard_map/all_to_all | solution.py:388
  24.4 0.0 collective-permute-done.1.other_ref
  24.4 0.0 collective-permute-done.2.other_ref
  24.4 10.1 %all_to_all.34 = f32[16,1,128]{2,1,0:T(1,128)S(1)} all-to-all(f32[16,1,128]{2,1,0:T(1,128)S(1)} %bitcast.22), channel_id=1, replica_groups=mesh['parts'=2,'tile'=16] {'tile'}, dimensions={0} | all-to-all | bytes 16384 | tf_op jit(solution)/shard_map/all_to_all | solution.py:388
  34.6 2.0 %chain3.1 = f32[16,128]{1,0:T(8,128)S(1)} custom-call(s32[4,2]{1,0:T(4,128)S(1)} %copy.8.offsets_ref, bf16[128,2048]{1,0:T(8,128)(2,1)S(1)} %copy-done, bf16[128,1024]{1,0:T(8,128)(2,1)S(1)} %collective-permute-done.2.other_ref, s32[1,16]{1,0:T(1,128)S(1)} %copy-done.1, f32[8,128]{1,0:T(8,128)S(1)} %concatenate.7.refs_0_), custom_call_target="tpu_custom_call" | custom-call | tf_op jit(solution)/shard_map/chain3/pallas_call | solution.py:370
  36.6 9.0 %all_to_all.35 = f32[16,1,128]{2,1,0:T(1,128)S(1)} all-to-all(f32[16,1,128]{2,1,0:T(1,128)S(1)} %bitcast.24), channel_id=1, replica_groups=mesh['parts'=2,'tile'=16] {'tile'}, dimensions={0} | all-to-all | bytes 16384 | tf_op jit(solution)/shard_map/all_to_all | solution.py:388
  45.5 2.3 %home.1 = (bf16[128,2048]{1,0:T(8,128)(2,1)}, f32[2,1,16]{2,1,0:T(1,128)}) custom-call(bf16[128,2048]{1,0:T(8,128)(2,1)S(1)} %copy-done, f32[16,128]{1,0:T(8,128)S(1)} %bitcast.19, f32[16,128]{1,0:T(8,128)S(1)} %bitcast.21, f32[16,128]{1,0:T(8,128)S(1)} %bitcast.23), custom_call_target="tpu_custom_call" | custom-call | tf_op jit(solution)/shard_map/home/pallas_call | solution.py:389
  (6 shorter events, 0.1 us)
Async XLA Ops:
  0.6 1.8 %copy-start = (bf16[128,2048]{1,0:T(8,128)(2,1)S(1)}, bf16[128,2048]{1,0:T(8,128)(2,1)}, u32[]{:S(2)}) copy-start(bf16[128,2048]{1,0:T(8,128)(2,1)} %own_ref.7) | copy-start | bytes 1572868
  1.7 11.9 %collective-permute-start = (bf16[128,1024]{1,0:T(8,128)(2,1)S(1)}, bf16[128,1024]{1,0:T(8,128)(2,1)S(1)}, u32[]{:S(2)}, u32[]{:S(2)}) collective-permute-start(bf16[128,1024]{1,0:T(8,128)(2,1)S(1)} %constant_dynamic-slice_fusion.2), channel_id=1, source_target_pairs={{2,6},{3,7},{4,8},{5,9},{6,2},{7,3},{8,4},{9,5},{18,22},{19,23},{2... | collective-permute-start | bytes 786440 | tf_op jit(solution)/shard_map/ppermute | solution.py:349
  2.5 11.0 %copy-start.2 = (s32[4,2]{0,1:T(2,128)S(1)}, s32[4,2]{0,1:T(2,128)}, u32[]{:S(2)}) copy-start(s32[4,2]{0,1:T(2,128)} %param.5) | copy-start | bytes 100
  2.5 21.9 %collective-permute-start.1 = (bf16[128,1024]{1,0:T(8,128)(2,1)S(1)}, bf16[128,1024]{1,0:T(8,128)(2,1)S(1)}, u32[]{:S(2)}, u32[]{:S(2)}) collective-permute-start(bf16[128,1024]{1,0:T(8,128)(2,1)S(1)} %get-tuple-element.11), channel_id=1, source_target_pairs={{6,10},{7,11},{8,12},{9,13},{10,6},{11,7},{12,8},{13,9},{22,26},{2... | collective-permute-start | bytes 786440 | tf_op jit(solution)/shard_map/ppermute | solution.py:349
  3.2 10.4 %copy-start.1 = (s32[1,16]{1,0:T(1,128)S(1)}, s32[1,16]{1,0:T(1,128)}, u32[]{:S(2)}) copy-start(s32[1,16]{1,0:T(1,128)} %mask_ref.5) | copy-start | bytes 196
  3.2 21.3 %collective-permute-start.2 = (bf16[128,1024]{1,0:T(8,128)(2,1)S(1)}, bf16[128,1024]{1,0:T(8,128)(2,1)S(1)}, u32[]{:S(2)}, u32[]{:S(2)}) collective-permute-start(bf16[128,1024]{1,0:T(8,128)(2,1)S(1)} %get-tuple-element.10), channel_id=1, source_target_pairs={{10,14},{11,15},{12,0},{13,1},{14,10},{15,11},{0,12},{1,13},{26,30... | collective-permute-start | bytes 786440 | tf_op jit(solution)/shard_map/ppermute | solution.py:349

commit v15 on v14

--- a/solution.py
+++ b/solution.py
@@ -325,7 +325,7 @@
     group, row_index = rotated // rows, rotated % rows
     grid = None
     for step in range(1, SECTIONS):
-        part = section_grid(refs[step - 1][...], step, rows)
+        part = refs[step - 1][...]
         grid = part if grid is None else jnp.where(group == step, part, grid)
     row_shift = own_row(relax(grid, rows, nodes), row_index)
     row_shift = jnp.where(group == 0, 0.0, row_shift)
@@ -366,7 +366,7 @@
     params = pltpu.CompilerParams(vmem_limit_bytes=16 * 2**20)
     gathered = []
     for step in range(1, SECTIONS):
-        extra = [section_grid(gathered[-1], step - 1, rows)] if gathered else []
+        extra = gathered[-1:]
         sent = pl.pallas_call(
             functools.partial(chain_kernel, step, rows, nodes),
             out_shape=jax.ShapeDtypeStruct((count, LANES), f32),
@@ -385,7 +385,7 @@
         )(coarse_offsets, sections, others[step - 1], valid_mask, *extra)
         if 1 < step < SECTIONS - 1:
             sent, others[step] = lax.optimization_barrier((sent, others[step]))
-        gathered.append(lax.all_to_all(sent, "tile", 0, 0, tiled=True))
+        gathered.append(section_grid(lax.all_to_all(sent, "tile", 0, 0, tiled=True), step, rows))
     return pl.pallas_call(
         functools.partial(home_kernel, rows, nodes),
         out_shape=(

time: 48.1 us -> 48.2 us (level)
  no operation moved by 1% of the time
where the time goes in v15:
time: 48.2 us; the launch traced here: 47.9 us
  blocking collectives  28.8 us (60%)
  starting transfers between devices  11.7 us (24%)
  Pallas kernels  5.42 us (11%)
  local copies, waits for them, and re-layouts  1.2 us (2%)
  between operations  0.8 us (2%)
    all_to_all x3, blocking collectives, shards(): lax.all_to_all(sent, 'tile', 0, 0, tiled=True)  28.8 us
    ppermute x3, starting transfers between devices, shards(): moved = lambda value, pairs: lax.ppermute(value, 'tile', pairs)  11.7 us
    pallas_call x3, Pallas kernels, shards(): pl.pallas_call(functools.partial(chain_kernel, step, rows, nodes), out_sh...  3.11 us
    pallas_call x1, Pallas kernels, shards(): pl.pallas_call(functools.partial(home_kernel, rows, nodes), out_shape=(ja...  2.31 us
    dynamic_slice x2, local copies, waits for them, and re-layouts, half_of(): return lax.dynamic_slice_in_dim(source, start, half * PATCH, 1)  1.06 us
  transfers between devices with their start and end apart: 3, of which 0 were waited for; matrix products, arithmetic and copies ran while one was open for 0% of the time, Pallas kernels for 2%

profile of v15, /device:TPU:0, one launch (start us, length us, event | category | flops | bytes accessed | tf_op | source)
XLA Modules:
  0.0 47.9 jit_solution(13080892490356538476)
XLA Ops:
  0.6 0.0 copy-start
  0.7 1.0 %constant_dynamic-slice_fusion.2 = bf16[128,1024]{1,0:T(8,128)(2,1)S(1)} fusion(bf16[128,2048]{1,0:T(8,128)(2,1)} %own_ref.7, s32[]{:T(128)S(6)} %select_n.26), kind=kLoop, calls=%fused_computation.11 | loop fusion | bytes 524292 | tf_op jit(solution)/shard_map/dynamic_slice | solution.py:353
  1.7 0.7 %collective-permute-start = (bf16[128,1024]{1,0:T(8,128)(2,1)S(1)}, bf16[128,1024]{1,0:T(8,128)(2,1)S(1)}, u32[]{:S(2)}, u32[]{:S(2)}) collective-permute-start(bf16[128,1024]{1,0:T(8,128)(2,1)S(1)} %constant_dynamic-slice_fusion.2), channel_id=1, source_target_pairs={{2,6},{3,7},{4,8},{5,9},{6,2},{7,3},{8,4},{9,5},{18,22},{19,23},{2... | collective-permute-start | bytes 786440 | tf_op jit(solution)/shard_map/ppermute | solution.py:349
  2.4 0.0 copy-done
  2.5 0.0 copy-start.2
  2.5 0.7 %collective-permute-start.1 = (bf16[128,1024]{1,0:T(8,128)(2,1)S(1)}, bf16[128,1024]{1,0:T(8,128)(2,1)S(1)}, u32[]{:S(2)}, u32[]{:S(2)}) collective-permute-start(bf16[128,1024]{1,0:T(8,128)(2,1)S(1)} %get-tuple-element.11), channel_id=1, source_target_pairs={{6,10},{7,11},{8,12},{9,13},{10,6},{11,7},{12,8},{13,9},{22,26},{2... | collective-permute-start | bytes 786440 | tf_op jit(solution)/shard_map/ppermute | solution.py:349
  3.2 0.0 copy-start.1
  3.2 10.3 %collective-permute-start.2 = (bf16[128,1024]{1,0:T(8,128)(2,1)S(1)}, bf16[128,1024]{1,0:T(8,128)(2,1)S(1)}, u32[]{:S(2)}, u32[]{:S(2)}) collective-permute-start(bf16[128,1024]{1,0:T(8,128)(2,1)S(1)} %get-tuple-element.10), channel_id=1, source_target_pairs={{10,14},{11,15},{12,0},{13,1},{14,10},{15,11},{0,12},{1,13},{26,30... | collective-permute-start | bytes 786440 | tf_op jit(solution)/shard_map/ppermute | solution.py:349
  13.5 0.0 copy-done.2
  13.5 0.1 copy.8.offsets_ref
  13.6 0.0 collective-permute-done.other_ref
  13.6 0.0 copy-done.1
  13.6 1.1 %chain1.1 = f32[16,128]{1,0:T(8,128)S(1)} custom-call(s32[4,2]{1,0:T(4,128)S(1)} %copy.8.offsets_ref, bf16[128,2048]{1,0:T(8,128)(2,1)S(1)} %copy-done, bf16[128,1024]{1,0:T(8,128)(2,1)S(1)} %collective-permute-done.other_ref, s32[1,16]{1,0:T(1,128)S(1)} %copy-done.1), custom_call_target="tpu_custom_call" | custom-call | tf_op jit(solution)/shard_map/chain1/pallas_call | solution.py:370
  14.7 9.7 %all_to_all.27 = f32[16,1,128]{2,1,0:T(1,128)S(1)} all-to-all(f32[16,1,128]{2,1,0:T(1,128)S(1)} %bitcast.26), channel_id=1, replica_groups=mesh['parts'=2,'tile'=16] {'tile'}, dimensions={0} | all-to-all | bytes 16384 | tf_op jit(solution)/shard_map/all_to_all | solution.py:388
  24.4 0.0 collective-permute-done.1.other_ref
  24.4 0.0 collective-permute-done.2.other_ref
  24.4 10.1 %all_to_all.28 = f32[16,1,128]{2,1,0:T(1,128)S(1)} all-to-all(f32[16,1,128]{2,1,0:T(1,128)S(1)} %bitcast.24), channel_id=1, replica_groups=mesh['parts'=2,'tile'=16] {'tile'}, dimensions={0} | all-to-all | bytes 16384 | tf_op jit(solution)/shard_map/all_to_all | solution.py:388
  34.6 2.0 %chain3.1 = f32[16,128]{1,0:T(8,128)S(1)} custom-call(s32[4,2]{1,0:T(4,128)S(1)} %copy.8.offsets_ref, bf16[128,2048]{1,0:T(8,128)(2,1)S(1)} %copy-done, bf16[128,1024]{1,0:T(8,128)(2,1)S(1)} %collective-permute-done.2.other_ref, s32[1,16]{1,0:T(1,128)S(1)} %copy-done.1, f32[8,128]{1,0:T(8,128)S(1)} %concatenate.13.refs_0_.refs_1_), custom_call_target="tpu_custom_call" | custom-call | tf_op jit(solution)/shard_map/chain3/pallas_call | solution.py:370
  36.6 9.0 %all_to_all.29 = f32[16,1,128]{2,1,0:T(1,128)S(1)} all-to-all(f32[16,1,128]{2,1,0:T(1,128)S(1)} %bitcast.25), channel_id=1, replica_groups=mesh['parts'=2,'tile'=16] {'tile'}, dimensions={0} | all-to-all | bytes 16384 | tf_op jit(solution)/shard_map/all_to_all | solution.py:388
  45.6 2.3 %home.1 = (bf16[128,2048]{1,0:T(8,128)(2,1)}, f32[2,1,16]{2,1,0:T(1,128)}) custom-call(bf16[128,2048]{1,0:T(8,128)(2,1)S(1)} %copy-done, f32[8,128]{1,0:T(8,128)S(1)} %concatenate.12.refs_0_, f32[8,128]{1,0:T(8,128)S(1)} %concatenate.13.refs_0_.refs_1_, f32[8,128]{1,0:T(8,128)S(1)} %concatenate.15.refs_2_), custom_call_target="tpu_custom_call" | custom-call | tf_op jit(solution)/shard_map/home/pallas_call | solution.py:389
  (10 shorter events, 0.1 us)
Async XLA Ops:
  0.6 1.8 %copy-start = (bf16[128,2048]{1,0:T(8,128)(2,1)S(1)}, bf16[128,2048]{1,0:T(8,128)(2,1)}, u32[]{:S(2)}) copy-start(bf16[128,2048]{1,0:T(8,128)(2,1)} %own_ref.7) | copy-start | bytes 1572868
  1.7 11.9 %collective-permute-start = (bf16[128,1024]{1,0:T(8,128)(2,1)S(1)}, bf16[128,1024]{1,0:T(8,128)(2,1)S(1)}, u32[]{:S(2)}, u32[]{:S(2)}) collective-permute-start(bf16[128,1024]{1,0:T(8,128)(2,1)S(1)} %constant_dynamic-slice_fusion.2), channel_id=1, source_target_pairs={{2,6},{3,7},{4,8},{5,9},{6,2},{7,3},{8,4},{9,5},{18,22},{19,23},{2... | collective-permute-start | bytes 786440 | tf_op jit(solution)/shard_map/ppermute | solution.py:349
  2.5 11.0 %copy-start.2 = (s32[4,2]{0,1:T(2,128)S(1)}, s32[4,2]{0,1:T(2,128)}, u32[]{:S(2)}) copy-start(s32[4,2]{0,1:T(2,128)} %param.5) | copy-start | bytes 100
  2.5 21.9 %collective-permute-start.1 = (bf16[128,1024]{1,0:T(8,128)(2,1)S(1)}, bf16[128,1024]{1,0:T(8,128)(2,1)S(1)}, u32[]{:S(2)}, u32[]{:S(2)}) collective-permute-start(bf16[128,1024]{1,0:T(8,128)(2,1)S(1)} %get-tuple-element.11), channel_id=1, source_target_pairs={{6,10},{7,11},{8,12},{9,13},{10,6},{11,7},{12,8},{13,9},{22,26},{2... | collective-permute-start | bytes 786440 | tf_op jit(solution)/shard_map/ppermute | solution.py:349
  3.2 10.4 %copy-start.1 = (s32[1,16]{1,0:T(1,128)S(1)}, s32[1,16]{1,0:T(1,128)}, u32[]{:S(2)}) copy-start(s32[1,16]{1,0:T(1,128)} %mask_ref.5) | copy-start | bytes 196
  3.2 21.3 %collective-permute-start.2 = (bf16[128,1024]{1,0:T(8,128)(2,1)S(1)}, bf16[128,1024]{1,0:T(8,128)(2,1)S(1)}, u32[]{:S(2)}, u32[]{:S(2)}) collective-permute-start(bf16[128,1024]{1,0:T(8,128)(2,1)S(1)} %get-tuple-element.10), channel_id=1, source_target_pairs={{10,14},{11,15},{12,0},{13,1},{14,10},{15,11},{0,12},{1,13},{26,30... | collective-permute-start | bytes 786440 | tf_op jit(solution)/shard_map/ppermute | solution.py:349
